TPU v7x, 256 devices: a whole 4x4x8 slice. The times are simulated.
256 devices in a mesh: gz: 64 (over z, x, y_hi), br: 4 (over y_lo, core).
Axes of the slice: x: 4, y: 4 (y_hi: 2, y_lo: 2; y = y_hi * 2 + y_lo), z: 8, core: 2. Of those that a mesh axis runs over, the one named last changes fastest.
Arguments:
- features: bfloat16 [32, 256, 16, 128], P('br', 'gz'), may hold values from -6 to 6
- tap_weights: bfloat16 [4, 3, 3, 3, 128, 256], P('br'), may hold values from -0.109375 to 0.109375
- branch_bias: float32 [4, 256], P('br'), may hold values from -3 to 3
- proj_weights: bfloat16 [4, 256, 256], P('br'), may hold values from -0.1875 to 0.1875
- out_bias: float32 [256], replicated, may hold values from -3 to 3
- cotangent: bfloat16 [32, 256, 16, 256], P('br', 'gz'), may hold values from -0.75 to 0.75
Outputs:
- head_out: bfloat16 [32, 256, 16, 256], P('br', 'gz')
- feature_grad: bfloat16 [32, 256, 16, 128], P('br', 'gz')
- tap_grads: float32 [4, 3, 3, 3, 128, 256], P('br')
- proj_grads: float32 [4, 256, 256], P('br')
All inputs are finite; a program needn't handle non-finite values.
Results may differ from a plain program's by a relative error of at most 0.006.
Values may be sent and summed in bfloat16 or wider, within the bound.
No kernel may reach another device: no remote copies, remote signals or barrier semaphores. Data moves between devices by JAX's collectives and lax.ppermute only.
A program may use at most 128 MiB of HBM per device.

v0:
```python
import jax
import jax.numpy as jnp
from jax import lax
from jax.sharding import PartitionSpec as P


def passed_along(x, axis, by):
    peers = lax.axis_size(axis)
    pairs = [(i, i + by) for i in range(peers) if 0 <= i + by < peers]
    return lax.ppermute(x, axis, pairs)


def silu_slope(values):
    logistic = jax.nn.sigmoid(values)
    return logistic * (1.0 + values * (1.0 - logistic))


def tap_mask(branch):
    depth_pos = jnp.arange(3)[:, None, None]
    row_pos = jnp.arange(3)[None, :, None]
    col_pos = jnp.arange(3)[None, None, :]
    centre = (depth_pos == 1) & (row_pos == 1) & (col_pos == 1)
    return jnp.where((branch > 0) | centre, 1.0, 0.0).astype(jnp.float32)


def in_plane(values):
    breadth = values.shape[0]
    height = values.shape[2]
    padded = jnp.pad(values, ((1, 1), (0, 0), (1, 1), (0, 0)))
    return jnp.concatenate(
        [
            padded[across : across + breadth, :, upward : upward + height, :]
            for across in range(3)
            for upward in range(3)
        ],
        axis=-1,
    )


def select_branch(options, branch):
    return lax.dynamic_index_in_dim(jnp.stack(options), branch, 0, keepdims=False)


def shards(features, tap_weights, branch_bias, proj_weights, out_bias, cotangent):
    channels = features.shape[3]
    hidden_width = tap_weights.shape[5]
    quarter = features.shape[0]
    groups = lax.axis_size("br")
    branch = lax.axis_index("br")
    mask_here = tap_mask(branch)
    masked = tap_weights[0] * mask_here.astype(jnp.bfloat16)[:, :, :, None, None]
    centre_taps = lax.all_gather(features, "br", axis=0, tiled=True)
    shifted = {}
    for stride in (1, -1, 2, -2, 4, -4):
        shifted[stride] = passed_along(centre_taps, "gz", stride)
    below_taps = select_branch([centre_taps, shifted[1], shifted[2], shifted[4]], branch)
    above_taps = select_branch([centre_taps, shifted[-1], shifted[-2], shifted[-4]], branch)
    columns = [in_plane(below_taps), in_plane(centre_taps), in_plane(above_taps)]
    preact = branch_bias[0]
    for tap_index in range(3):
        preact = preact + jnp.dot(
            columns[tap_index],
            masked[tap_index].reshape(9 * channels, hidden_width),
            preferred_element_type=jnp.float32,
        )
    hidden = jax.nn.silu(preact).astype(jnp.bfloat16)
    summed = (
        lax.psum_scatter(
            jnp.dot(hidden, proj_weights[0], preferred_element_type=jnp.float32),
            "br",
            scatter_dimension=0,
            tiled=True,
        )
        + out_bias
    )
    head_out = jax.nn.silu(summed).astype(jnp.bfloat16)
    d_out = (cotangent.astype(jnp.float32) * silu_slope(summed)).astype(jnp.bfloat16)
    shard_rows = lax.all_gather(d_out, "br", axis=0, tiled=True)
    product_rows = lax.dot_general(
        shard_rows, proj_weights[0], (((3,), (1,)), ((), ())), preferred_element_type=jnp.float32
    )
    d_hidden = product_rows
    proj_sum = lax.dot_general(
        hidden, shard_rows, (((0, 1, 2), (0, 1, 2)), ((), ())), preferred_element_type=jnp.float32
    )
    d_hidden, proj_local = (d_hidden, proj_sum)
    d_pre = (d_hidden * silu_slope(preact)).astype(jnp.bfloat16)
    local_taps = jnp.stack(
        [
            lax.dot_general(
                columns[tap_index],
                d_pre,
                (((0, 1, 2), (0, 1, 2)), ((), ())),
                preferred_element_type=jnp.float32,
            )
            for tap_index in range(3)
        ]
    )
    local_taps = (
        local_taps.reshape(3, 3, 3, channels, hidden_width) * mask_here[:, :, :, None, None]
    )
    tap_total, proj_total = lax.psum((local_taps, proj_local), "gz")
    flipped = masked[:, ::-1, ::-1].transpose(0, 1, 2, 4, 3).reshape(3, 9 * hidden_width, channels)
    d_columns = in_plane(d_pre)
    per_tap = jnp.stack(
        [
            jnp.dot(d_columns, flipped[tap_index], preferred_element_type=jnp.float32)
            for tap_index in range(3)
        ]
    )
    per_tap = per_tap.reshape((3, groups, quarter) + per_tap.shape[2:])
    returned = lax.all_to_all(per_tap, "br", split_axis=1, concat_axis=1, tiled=True)
    gradient = jnp.sum(returned[1], axis=0)
    for source in range(1, groups):
        stride = 2 ** (source - 1)
        for tap_index, direction in ((0, -1), (2, 1)):
            gradient = gradient + passed_along(
                returned[tap_index, source], "gz", direction * stride
            )
    return (head_out, gradient.astype(jnp.bfloat16), tap_total[None], proj_total[None])


def solution(mesh):
    in_specs = (
        P("br", "gz", None, None),
        P("br", None, None, None, None, None),
        P("br", None),
        P("br", None, None),
        P(),
        P("br", "gz", None, None),
    )
    out_specs = (
        P("br", "gz", None, None),
        P("br", "gz", None, None),
        P("br", None, None, None, None, None),
        P("br", None, None),
    )
    return jax.shard_map(shards, mesh=mesh, in_specs=in_specs, out_specs=out_specs, check_vma=False)
```

profile of v0, /device:TPU:64, one launch (start us, length us, event | category | flops | bytes accessed | tf_op | source)
XLA Modules:
  0.0 880.1 jit_solution(2921355540596622031)
XLA Ops:
  7.2 7.5 all_gather.6
  14.7 6.5 collective-permute-start.3
  21.2 2.7 collective-permute-start.4
  24.0 2.4 collective-permute-start.5
  26.4 2.6 collective-permute-start
  29.0 2.8 collective-permute-start.1
  40.0 1.8 bitcast_multiply_fusion
  41.9 5.4 collective-permute-start.2
  49.7 7.1 collective-permute-done.4
  56.8 10.7 %collective-permute-done.5 = bf16[32,4,16,128]{3,2,1,0:T(8,128)(2,1)} collective-permute-done((bf16[32,4,16,128]{3,2,1,0:T(8,128)(2,1)S(1)}, bf16[32,4,16,128]{3,2,1,0:T(8,128)(2,1)}, u32[]{:S(2)}, u32[]{:S(2)}) %collective-permute-start.5) | collective-permute-done | bytes 524320 | tf_op jit(solution)/shard_map/ppermute | solution.py:10
  74.3 1.6 add_add_fusion
  77.2 2.0 fusion.42
  79.3 48.2 %reduce-scatter.2.cloned.1.call-done = f32[8,4,16,256]{3,2,1,0:T(8,128)} async-done(((f32[32,4,16,256]{3,2,1,0:T(8,128)}), f32[8,4,16,256]{3,2,1,0:T(8,128)}) %reduce-scatter.2.cloned.1.call-update) | async-done | bytes 524304 | tf_op jit(solution)/shard_map/reduce_scatter | solution.py:68
  127.5 2.1 multiply_convert_fusion.2
  131.8 22.5 %all-gather.2.cloned.1.call-done = bf16[32,4,16,256]{3,2,1,0:T(8,128)(2,1)} async-done(((bf16[8,4,16,256]{3,2,1,0:T(8,128)(2,1)}), bf16[32,4,16,256]{3,2,1,0:T(8,128)(2,1)}) %all-gather.2.cloned.1.call-update) | async-done | bytes 1048592 | tf_op jit(solution)/shard_map/all_gather | solution.py:78
  154.3 2.9 multiply_convert_fusion
  157.3 3.9 fusion.51
  167.1 2.7 convolution_bitcast_fusion.2
  170.7 3.0 convolution_bitcast_fusion.1
  173.7 2.2 fusion
  178.2 5.2 convolution_bitcast_fusion
  184.2 53.8 %all_to_all.5 = f32[3,4,8,4,16,128]{5,4,3,2,0,1:T(8,128)S(1)} all-to-all(f32[3,4,8,4,16,128]{5,4,3,2,0,1:T(8,128)S(1)} %copy.24), channel_id=1, replica_groups=mesh['gz'=64,'br'=4] {'br'}, dimensions={1} | all-to-all | bytes 6291456 | tf_op jit(solution)/shard_map/all_to_all | solution.py:112
  238.1 5.4 collective-permute-start.10
  243.5 1.9 collective-permute-start.11
  245.5 8.6 collective-permute-start.6
  254.1 1.9 collective-permute-start.7
  256.0 3.0 collective-permute-start.8
  259.0 3.5 collective-permute-start.9
  263.8 4.6 collective-permute-done.7
  268.4 4.0 collective-permute-done.8
  273.2 595.4 %all-reduce.7.cloned.1.call-done = (f32[1,3,3,3,128,256]{5,4,3,2,1,0:T(8,128)}, f32[1,256,256]{2,1,0:T(8,128)}) async-done(((f32[1,3,3,3,128,256]{5,4,3,2,1,0:T(8,128)}, f32[1,256,256]{2,1,0:T(8,128)}), (f32[1,3,3,3,128,256]{5,4,3,2,1,0:T(8,128)}, f32[1,256,256]{2,1,0:T(8,128)})) %all-reduce.7.cloned.1.call-update) | async-done | bytes 3801104 | tf_op jit(solution)/shard_map/psum | solution.py:102
  868.6 4.2 copy.96
  (110 shorter events, 33.6 us)
Async XLA Ops:
  7.2 70.1 %copy-start = (bf16[1,256,256]{2,1,0:T(8,128)(2,1)S(1)}, bf16[1,256,256]{2,1,0:T(8,128)(2,1)}, u32[]{:S(2)}) copy-start(bf16[1,256,256]{2,1,0:T(8,128)(2,1)} %param.9) | copy-start | bytes 393220
  7.2 120.3 %reduce-scatter.2.cloned.1.call-start = ((), (), s32[]{:S(2)}) async-start(), calls=%async_computation.2 | async-start | bytes 2621440 | tf_op jit(solution)/shard_map/reduce_scatter | solution.py:68
  14.7 27.2 %collective-permute-start.3 = (bf16[32,4,16,128]{3,2,1,0:T(8,128)(2,1)S(1)}, bf16[32,4,16,128]{3,2,1,0:T(8,128)(2,1)S(1)}, u32[]{:S(2)}, u32[]{:S(2)}) collective-permute-start(bf16[32,4,16,128]{3,2,1,0:T(8,128)(2,1)S(1)} %all_gather.6), channel_id=1, source_target_pairs={{4,0},{8,4},{12,8},{16,12},{20,16},{24,20},{28,24},{32,28},{36,32}... | collective-permute-start | bytes 1572872 | tf_op jit(solution)/shard_map/ppermute | solution.py:10
  21.2 35.6 %collective-permute-start.4 = (bf16[32,4,16,128]{3,2,1,0:T(8,128)(2,1)S(1)}, bf16[32,4,16,128]{3,2,1,0:T(8,128)(2,1)S(1)}, u32[]{:S(2)}, u32[]{:S(2)}) collective-permute-start(bf16[32,4,16,128]{3,2,1,0:T(8,128)(2,1)S(1)} %all_gather.6), channel_id=1, source_target_pairs={{8,0},{12,4},{16,8},{20,12},{24,16},{28,20},{32,24},{36,28},{40,32... | collective-permute-start | bytes 1572872 | tf_op jit(solution)/shard_map/ppermute | solution.py:10
  24.0 43.5 %collective-permute-start.5 = (bf16[32,4,16,128]{3,2,1,0:T(8,128)(2,1)S(1)}, bf16[32,4,16,128]{3,2,1,0:T(8,128)(2,1)}, u32[]{:S(2)}, u32[]{:S(2)}) collective-permute-start(bf16[32,4,16,128]{3,2,1,0:T(8,128)(2,1)S(1)} %all_gather.6), channel_id=1, source_target_pairs={{16,0},{20,4},{24,8},{28,12},{32,16},{36,20},{40,24},{44,28},{48,3... | collective-permute-start | bytes 1572872 | tf_op jit(solution)/shard_map/ppermute | solution.py:10
  26.4 41.1 %collective-permute-start = (bf16[32,4,16,128]{3,2,1,0:T(8,128)(2,1)S(1)}, bf16[32,4,16,128]{3,2,1,0:T(8,128)(2,1)}, u32[]{:S(2)}, u32[]{:S(2)}) collective-permute-start(bf16[32,4,16,128]{3,2,1,0:T(8,128)(2,1)S(1)} %all_gather.6), channel_id=1, source_target_pairs={{0,4},{4,8},{8,12},{12,16},{16,20},{20,24},{24,28},{28,32},{32,36}... | collective-permute-start | bytes 1572872 | tf_op jit(solution)/shard_map/ppermute | solution.py:10
  29.0 38.5 %collective-permute-start.1 = (bf16[32,4,16,128]{3,2,1,0:T(8,128)(2,1)S(1)}, bf16[32,4,16,128]{3,2,1,0:T(8,128)(2,1)}, u32[]{:S(2)}, u32[]{:S(2)}) collective-permute-start(bf16[32,4,16,128]{3,2,1,0:T(8,128)(2,1)S(1)} %all_gather.6), channel_id=1, source_target_pairs={{0,8},{4,12},{8,16},{12,20},{16,24},{20,28},{24,32},{28,36},{32,40... | collective-permute-start | bytes 1572872 | tf_op jit(solution)/shard_map/ppermute | solution.py:10
  39.9 7.4 copy-start.9
  41.9 25.6 %collective-permute-start.2 = (bf16[32,4,16,128]{3,2,1,0:T(8,128)(2,1)S(1)}, bf16[32,4,16,128]{3,2,1,0:T(8,128)(2,1)S(1)}, u32[]{:S(2)}, u32[]{:S(2)}) collective-permute-start(bf16[32,4,16,128]{3,2,1,0:T(8,128)(2,1)S(1)} %all_gather.6), channel_id=1, source_target_pairs={{0,16},{4,20},{8,24},{12,28},{16,32},{20,36},{24,40},{28,44},{32,4... | collective-permute-start | bytes 1572872 | tf_op jit(solution)/shard_map/ppermute | solution.py:10
  47.6 2.1 copy-start.10
  70.4 4.0 copy-start.2
  72.1 2.2 copy-start.11
  72.1 2.2 copy-start.12
  77.2 50.3 %copy-start.7 = (bf16[8,4,16,256]{3,2,1,0:T(8,128)(2,1)S(1)}, bf16[8,4,16,256]{3,2,1,0:T(8,128)(2,1)}, u32[]{:S(2)}) copy-start(bf16[8,4,16,256]{3,2,1,0:T(8,128)(2,1)} %param.11) | copy-start | bytes 786436
  77.2 50.3 %copy-start.13 = (f32[256]{0:T(256)S(1)}, f32[256]{0:T(256)}, u32[]{:S(2)}) copy-start(f32[256]{0:T(256)} %param.10) | copy-start | bytes 3076
  79.3 75.0 %all-gather.2.cloned.1.call-start = ((), (), s32[]{:S(2)}) async-start(), calls=%async_computation.3 | async-start | bytes 1310720 | tf_op jit(solution)/shard_map/all_gather | solution.py:78
  129.6 739.0 %all-reduce.7.cloned.1.call-start = ((), (), s32[]{:S(2)}) async-start(), calls=%async_computation.4 | async-start | bytes 7602176 | tf_op jit(solution)/shard_map/psum | solution.py:102
  154.3 6.9 slice-start.2
  157.2 4.0 slice-start.3
  157.2 5.4 slice-start
  167.0 3.6 copy-start.8
  167.1 3.6 copy-start.5
  173.7 2.2 copy-start.4
  173.7 3.0 copy-start.14
  238.1 20.9 %collective-permute-start.10 = (f32[8,4,16,128]{3,2,1,0:T(8,128)S(1)}, f32[8,4,16,128]{3,2,1,0:T(8,128)S(1)}, u32[]{:S(2)}, u32[]{:S(2)}) collective-permute-start(f32[8,4,16,128]{3,2,1,0:T(8,128)S(1)} %get-tuple-element.11), channel_id=1, source_target_pairs={{16,0},{20,4},{24,8},{28,12},{32,16},{36,20},{40,24},{44,28},{48,3... | collective-permute-start | bytes 786440 | tf_op jit(solution)/shard_map/ppermute | solution.py:10
  243.5 19.0 %collective-permute-start.11 = (f32[8,4,16,128]{3,2,1,0:T(8,128)S(1)}, f32[8,4,16,128]{3,2,1,0:T(8,128)S(1)}, u32[]{:S(2)}, u32[]{:S(2)}) collective-permute-start(f32[8,4,16,128]{3,2,1,0:T(8,128)S(1)} %get-tuple-element.10), channel_id=1, source_target_pairs={{0,16},{4,20},{8,24},{12,28},{16,32},{20,36},{24,40},{28,44},{32,4... | collective-permute-start | bytes 786440 | tf_op jit(solution)/shard_map/ppermute | solution.py:10
  245.5 18.4 %collective-permute-start.6 = (f32[8,4,16,128]{3,2,1,0:T(8,128)S(1)}, f32[8,4,16,128]{3,2,1,0:T(8,128)S(1)}, u32[]{:S(2)}, u32[]{:S(2)}) collective-permute-start(f32[8,4,16,128]{3,2,1,0:T(8,128)S(1)} %get-tuple-element.6), channel_id=1, source_target_pairs={{4,0},{8,4},{12,8},{16,12},{20,16},{24,20},{28,24},{32,28},{36,32}... | collective-permute-start | bytes 786440 | tf_op jit(solution)/shard_map/ppermute | solution.py:10
  254.1 14.3 %collective-permute-start.7 = (f32[8,4,16,128]{3,2,1,0:T(8,128)S(1)}, f32[8,4,16,128]{3,2,1,0:T(8,128)S(1)}, u32[]{:S(2)}, u32[]{:S(2)}) collective-permute-start(f32[8,4,16,128]{3,2,1,0:T(8,128)S(1)} %get-tuple-element.9), channel_id=1, source_target_pairs={{0,4},{4,8},{8,12},{12,16},{16,20},{20,24},{24,28},{28,32},{32,36}... | collective-permute-start | bytes 786440 | tf_op jit(solution)/shard_map/ppermute | solution.py:10
  256.0 16.4 %collective-permute-start.8 = (f32[8,4,16,128]{3,2,1,0:T(8,128)S(1)}, f32[8,4,16,128]{3,2,1,0:T(8,128)S(1)}, u32[]{:S(2)}, u32[]{:S(2)}) collective-permute-start(f32[8,4,16,128]{3,2,1,0:T(8,128)S(1)} %get-tuple-element.8), channel_id=1, source_target_pairs={{8,0},{12,4},{16,8},{20,12},{24,16},{28,20},{32,24},{36,28},{40,32... | collective-permute-start | bytes 786440 | tf_op jit(solution)/shard_map/ppermute | solution.py:10
  259.0 13.4 %collective-permute-start.9 = (f32[8,4,16,128]{3,2,1,0:T(8,128)S(1)}, f32[8,4,16,128]{3,2,1,0:T(8,128)S(1)}, u32[]{:S(2)}, u32[]{:S(2)}) collective-permute-start(f32[8,4,16,128]{3,2,1,0:T(8,128)S(1)} %get-tuple-element.7), channel_id=1, source_target_pairs={{0,8},{4,12},{8,16},{12,20},{16,24},{20,28},{24,32},{28,36},{32,40... | collective-permute-start | bytes 786440 | tf_op jit(solution)/shard_map/ppermute | solution.py:10
  262.4 611.1 %copy-start.1 = (bf16[1,256,256]{2,1,0:T(8,128)(2,1)S(1)}, bf16[1,256,256]{2,1,0:T(8,128)(2,1)}, u32[]{:S(2)}) copy-start(bf16[1,256,256]{2,1,0:T(8,128)(2,1)} %param.9) | copy-start | bytes 393220
  868.6 4.2 copy-start.6
  (2 other events, 2.8 us)
Sparse Core Ops, SparseCore 0:
  79.4 48.0 reduce-scatter.1
  130.0 24.2 all-gather.1
  178.3 690.2 all-reduce.6
where the time goes:
time: 897 us; the launch traced here: 880 us
  waiting for transfers between devices  694 us (77%)
  blocking collectives  61.2 us (7%)
  starting transfers between devices  47 us (5%)
  matrix products  28.8 us (3%)
  local copies, waits for them, and re-layouts  26.6 us (3%)
  between operations  14.4 us (2%)
    psum x1, waiting for transfers between devices, shards(): tap_total, proj_total = lax.psum((local_taps, proj_local), 'gz')  595 us
    all_to_all x1, blocking collectives, shards(): lax.all_to_all(per_tap, 'br', split_axis=1, concat_axis=1, tiled=True)  53.8 us
    reduce_scatter x1, waiting for transfers between devices, shards(): lax.psum_scatter(jnp.dot(hidden, proj_weights[0], preferred_element_type=...  48.2 us
    ppermute x12, starting transfers between devices, passed_along(): return lax.ppermute(x, axis, pairs)  46.7 us
    ppermute x12, waiting for transfers between devices, passed_along(): return lax.ppermute(x, axis, pairs)  27.7 us
    unnamed x71, local copies, waits for them, and re-layouts  22.8 us
    all_gather x1, waiting for transfers between devices, shards(): shard_rows = lax.all_gather(d_out, 'br', axis=0, tiled=True)  22.5 us
  transfers between devices with their start and end apart: 15, of which 8 were waited for; matrix products, arithmetic and copies ran while one was open for 2% of the time, Pallas kernels for 0%

commit v1 on v0

v1 whole, which is shorter than its diff:
```python
import functools

import jax
import jax.numpy as jnp
from jax import lax
from jax.experimental import pallas as pl
from jax.experimental.pallas import tpu as pltpu
from jax.sharding import Mesh
from jax.sharding import PartitionSpec as P

C = 128
F = 256
COL = 64
ROWS = 2048
QUART = 512
TAPS = 27 * C
GRAD_ROWS = TAPS + F
bf16 = jnp.bfloat16
f32 = jnp.float32
GZ = ("z", "x", "yh")
BR = ("yl", "c")
SWAP = [(0, 1), (1, 0)]
VMEM = pl.BlockSpec(memory_space=pltpu.VMEM)
SMEM = pl.BlockSpec(memory_space=pltpu.SMEM)


def silu_slope(values):
    logistic = jax.nn.sigmoid(values)
    return logistic * (1.0 + values * (1.0 - logistic))


def height_of(rows, lanes):
    return lax.broadcasted_iota(jnp.int32, (rows, lanes), 0) & 15


def from_below(values):
    rolled = pltpu.roll(values, 1, 0)
    return jnp.where(height_of(*values.shape) == 0, 0.0, rolled)


def from_above(values):
    rolled = pltpu.roll(values, values.shape[0] - 1, 0)
    return jnp.where(height_of(*values.shape) == 15, 0.0, rolled)


def matmul(lhs, rhs):
    return jnp.dot(lhs, rhs, preferred_element_type=f32)


def matmul_rt(lhs, rhs):
    return lax.dot_general(lhs, rhs, (((1,), (1,)), ((), ())), preferred_element_type=f32)


def forward_kernel(core_ref, below, centre, above, weights, bias, proj, preact, hidden, keep, send, padded):
    for t, slab in enumerate((below, centre, above)):
        padded[t, 0:COL] = jnp.zeros((COL, C), bf16)
        padded[t, COL + ROWS : 2 * COL + ROWS] = jnp.zeros((COL, C), bf16)
        padded[t, COL : COL + ROWS] = slab[...]
    core = core_ref[0]
    for q in range(4):
        start = q * QUART
        window = jnp.concatenate(
            [padded[t, start + i * COL : start + i * COL + QUART] for t in range(3) for i in range(3)], axis=1
        )
        parts = matmul(window, weights[...])
        value = bias[...] + parts[:, F : 2 * F]
        value = value + from_below(parts[:, :F]) + from_above(parts[:, 2 * F :])
        preact[start : start + QUART] = value
        active = (value * jax.nn.sigmoid(value)).astype(bf16)
        hidden[start : start + QUART] = active
        projected = matmul(active, proj[...])

        @pl.when(core == q % 2)
        def _():
            keep[q // 2] = projected

        @pl.when(core != q % 2)
        def _():
            send[q // 2] = projected.astype(bf16)


def prepare_kernel(below, centre, above, preact, hidden, slope, hidden_t, features_t):
    for q in range(4):
        cells = slice(q * QUART, (q + 1) * QUART)
        slope[cells] = silu_slope(preact[cells])
        hidden_t[:, cells] = hidden[cells].astype(f32).T.astype(bf16)
        for t, slab in enumerate((below, centre, above)):
            value = slab[cells].astype(f32)
            for j, moved in enumerate((from_below(value), value, from_above(value))):
                block = (t * 3 + j) * C
                features_t[block : block + C, cells] = moved.T.astype(bf16)


def feature_kernel(core_ref, own, other, slope, proj, weights, d_pre, low, mid, high):
    d_pre[0:COL] = jnp.zeros((COL, F), bf16)
    d_pre[COL + ROWS : 2 * COL + ROWS] = jnp.zeros((COL, F), bf16)
    for q in range(4):
        start = q * QUART
        mine = core_ref[0] == q % 2
        rows = jnp.where(mine, own[q // 2], other[q // 2])
        d_hidden = matmul_rt(rows, proj[...])
        d_pre[COL + start : COL + start + QUART] = (d_hidden * slope[start : start + QUART]).astype(bf16)
    for q in range(4):
        start = q * QUART
        window = jnp.concatenate(
            [d_pre[start + (2 - i) * COL : start + (2 - i) * COL + QUART] for i in range(3)], axis=1
        )
        parts = matmul_rt(window, weights[...])
        total = parts[:, 3 * C : 6 * C] + from_above(parts[:, : 3 * C]) + from_below(parts[:, 6 * C :])
        cells = slice(start, start + QUART)
        low[cells] = total[:, :C].astype(bf16)
        mid[cells] = total[:, C : 2 * C]
        high[cells] = total[:, 2 * C :].astype(bf16)


def gradient_kernel(core_ref, keep_ref, d_pre, features_t, hidden_t, own, other, grads, window, d_out):
    for i in range(3):
        window[:, i * F : (i + 1) * F] = d_pre[(2 - i) * COL : (2 - i) * COL + ROWS]
    off_centre = keep_ref[0]
    for t in range(3):
        block = matmul(features_t[t * 3 * C : (t + 1) * 3 * C], window[...])
        for i in range(3):
            for j in range(3):
                tap = (t * 9 + i * 3 + j) * C
                piece = block[j * C : (j + 1) * C, i * F : (i + 1) * F]
                if (t, i, j) != (1, 1, 1):
                    piece = piece * off_centre
                grads[tap : tap + C] = piece.astype(bf16)
    for q in range(4):
        mine = core_ref[0] == q % 2
        d_out[q * QUART : (q + 1) * QUART] = jnp.where(mine, own[q // 2], other[q // 2])
    grads[TAPS:] = matmul(hidden_t[...], d_out[...]).astype(bf16)


def call(kernel, outs, specs, scratch, flops, *args):
    return pl.pallas_call(
        kernel,
        out_shape=[jax.ShapeDtypeStruct(*o) for o in outs],
        in_specs=specs,
        out_specs=[VMEM] * len(outs),
        scratch_shapes=scratch,
        compiler_params=pltpu.CompilerParams(vmem_limit_bytes=44 * 1024 * 1024),
        cost_estimate=pl.CostEstimate(flops=flops, bytes_accessed=8_000_000, transcendentals=0),
    )(*args)


def depth_pairs(mesh_gz, sign):
    strides = (0, 1, 2, 4)
    pairs = []
    for g in range(mesh_gz):
        for b in range(1, 4):
            target = g + sign * strides[b]
            if 0 <= target < mesh_gz:
                pairs.append((g * 4 + b, target * 4 + b))
    return pairs


def gathered(values, axis, peers):
    return lax.all_to_all(jnp.broadcast_to(values[None], (peers,) + values.shape), axis, 0, 0, tiled=True)


def shards(slabs, features, tap_weights, branch_bias, proj_weights, out_bias, cotangent):
    branch = lax.axis_index(BR)
    core = lax.axis_index("c")
    core_arg = core.astype(jnp.int32)[None]
    up = depth_pairs(slabs, 1)
    down = depth_pairs(slabs, -1)
    everywhere = GZ + BR
    proj = proj_weights[0]

    centre = lax.all_gather(features.reshape(QUART, C), BR, axis=0, tiled=True)
    below = lax.ppermute(centre, everywhere, up)
    above = lax.ppermute(centre, everywhere, down)

    tap = jnp.arange(27).reshape(3, 3, 3)
    off_centre = jnp.where(branch > 0, 1.0, 0.0).astype(f32)
    mask = jnp.where(tap == 13, 1.0, off_centre).astype(bf16)
    masked = tap_weights[0] * mask[:, :, :, None, None]
    weights_fwd = masked.transpose(0, 1, 3, 2, 4).reshape(9 * C, 3 * F)
    weights_bwd = masked.transpose(2, 0, 3, 1, 4).reshape(9 * C, 3 * F)
    cot_mine = cotangent.reshape(QUART, F)
    cot_pair = lax.ppermute(cot_mine, "yl", SWAP)

    preact, hidden, keep, send = call(
        forward_kernel,
        [((ROWS, F), f32), ((ROWS, F), bf16), ((2, QUART, F), f32), ((2, QUART, F), bf16)],
        [SMEM] + [VMEM] * 6,
        [pltpu.VMEM((3, ROWS + 2 * COL, C), bf16)],
        2 * ROWS * 27 * C * F,
        core_arg, below, centre, above, weights_fwd, branch_bias, proj,
    )
    chip_sum = keep + lax.ppermute(send, "c", SWAP).astype(f32)
    slope, hidden_t, features_t = call(
        prepare_kernel,
        [((ROWS, F), f32), ((F, ROWS), bf16), ((9 * C, ROWS), bf16)],
        [VMEM] * 5,
        [],
        2 * ROWS * 9 * C * F,
        below, centre, above, preact, hidden,
    )
    summed = chip_sum + lax.ppermute(chip_sum.astype(bf16), "yl", SWAP).astype(f32) + out_bias
    row = lax.axis_index("yl")
    first = row == 0
    cot = jnp.stack([jnp.where(first, cot_mine, cot_pair), jnp.where(first, cot_pair, cot_mine)])
    own = (cot.astype(f32) * silu_slope(summed)).astype(bf16)
    head_out = jax.nn.silu(jnp.where(first, summed[0], summed[1])).astype(bf16)
    other = lax.ppermute(own, "c", SWAP)

    d_pre, low, mid, high = call(
        feature_kernel,
        [((ROWS + 2 * COL, F), bf16), ((ROWS, C), bf16), ((ROWS, C), f32), ((ROWS, C), bf16)],
        [SMEM] + [VMEM] * 5,
        [],
        2 * ROWS * 27 * C * F,
        core_arg, own, other, slope, proj, weights_bwd,
    )
    from_low = lax.ppermute(low, everywhere, down)
    from_high = lax.ppermute(high, everywhere, up)
    (grads,) = call(
        gradient_kernel,
        [((GRAD_ROWS, F), bf16)],
        [SMEM, SMEM] + [VMEM] * 5,
        [pltpu.VMEM((ROWS, 3 * F), bf16), pltpu.VMEM((ROWS, F), bf16)],
        2 * ROWS * 27 * C * F,
        core_arg, off_centre[None], d_pre, features_t, hidden_t, own, other,
    )

    plane = lax.axis_size("x") * lax.axis_size("yh")
    tall = lax.axis_size("z")
    part = lax.all_to_all(grads.reshape(plane, GRAD_ROWS // plane, F), ("x", "yh"), 0, 0, tiled=True)
    part = jnp.sum(part.astype(f32), axis=0).astype(bf16)
    part = lax.all_to_all(part.reshape(tall, GRAD_ROWS // plane // tall, F), "z", 0, 0, tiled=True)
    part = jnp.sum(part.astype(f32), axis=0).astype(bf16)
    part = gathered(part, "z", tall).reshape(GRAD_ROWS // plane, F)
    total = gathered(part, ("x", "yh"), plane).reshape(GRAD_ROWS, F).astype(f32)

    branch_grad = (mid + from_low.astype(f32) + from_high.astype(f32)).reshape(2, 2, QUART, C)
    sent = lax.dynamic_index_in_dim(branch_grad, 1 - core, 1, keepdims=False).astype(bf16)
    kept = lax.dynamic_index_in_dim(branch_grad, core, 1, keepdims=False)
    chip_grad = kept + lax.ppermute(sent, "c", SWAP).astype(f32)
    sent = lax.dynamic_index_in_dim(chip_grad, 1 - row, 0, keepdims=False).astype(bf16)
    kept = lax.dynamic_index_in_dim(chip_grad, row, 0, keepdims=False)
    feature_grad = (kept + lax.ppermute(sent, "yl", SWAP).astype(f32)).astype(bf16)

    return (
        head_out.reshape(cotangent.shape),
        feature_grad.reshape(features.shape),
        total[:TAPS].reshape(1, 3, 3, 3, C, F),
        total[TAPS:].reshape(1, F, F),
    )


def solution(mesh):
    slabs = mesh.shape["gz"]
    split = (8, 4, 2) if slabs == 64 else (slabs, 1, 1)
    fine = Mesh(mesh.devices.reshape(split + (2, 2)), GZ + BR)
    in_specs = (
        P(BR, GZ, None, None),
        P(BR, None, None, None, None, None),
        P(BR, None),
        P(BR, None, None),
        P(),
        P(BR, GZ, None, None),
    )
    out_specs = (
        P(BR, GZ, None, None),
        P(BR, GZ, None, None),
        P(BR, None, None, None, None, None),
        P(BR, None, None),
    )
    return jax.shard_map(
        functools.partial(shards, slabs), mesh=fine, in_specs=in_specs, out_specs=out_specs, check_vma=False
    )
```

time: 897 us -> 202 us (0.23)
  the two profiles are of different devices: /device:TPU:64 before, /device:TPU:1 now
where the time goes in v1:
time: 202 us
  waiting for transfers between devices  66 us (33%)
  starting transfers between devices  43.1 us (21%)
  blocking collectives  39.5 us (20%)
  Pallas kernels  19.5 us (10%)
  local copies, waits for them, and re-layouts  17 us (8%)
  other arithmetic  15.6 us (8%)
    all_to_all x1, blocking collectives, shards(): lax.all_to_all(grads.reshape(plane, GRAD_ROWS // plane, F), ('x', 'yh'),...  29.7 us
    pallas_call x4, Pallas kernels, call(): pl.pallas_call(kernel, out_shape=[jax.ShapeDtypeStruct(*o) for o in outs]...  19.5 us
    ppermute x1, waiting for transfers between devices, shards(): lax.ppermute(sent, 'yl', SWAP).astype(f32)  18.8 us
    ppermute x1, waiting for transfers between devices, shards(): cot_pair = lax.ppermute(cot_mine, 'yl', SWAP)  17.9 us
    all_to_all x2, waiting for transfers between devices, gathered(): lax.all_to_all(jnp.broadcast_to(values[None], (peers,) + values.shape), a...  15.7 us
    all_to_all x2, starting transfers between devices, gathered(): lax.all_to_all(jnp.broadcast_to(values[None], (peers,) + values.shape), a...  12.3 us
    ppermute x1, starting transfers between devices, shards(): lax.ppermute(chip_sum.astype(bf16), 'yl', SWAP).astype(f32)  10.8 us
    all_gather x1, blocking collectives, shards(): centre = lax.all_gather(features.reshape(QUART, C), BR, axis=0, tiled=True)  9.8 us
  transfers between devices with their start and end apart: 13, of which 8 were waited for; matrix products, arithmetic and copies ran while one was open for 7% of the time, Pallas kernels for 2%

profile of v1, /device:TPU:1, one launch (start us, length us, event | category | flops | bytes accessed | tf_op | source)
XLA Modules:
  0.0 201.6 jit_solution(13540900278546278294)
XLA Ops:
  0.6 9.8 %all_gather.3.centre = bf16[2048,128]{1,0:T(8,128)(2,1)S(1)} all-gather(bf16[512,128]{1,0:T(8,128)(2,1)} %bitcast.59), channel_id=1, replica_groups=mesh['z'=8,'x'=4,'yh'=2,'yl'=2,'c'=2] {'yl','c'}, dimensions={0}, use_global_device_ids=true | all-gather | bytes 655360 | tf_op jit(solution)/shard_map/all_gather | solution.py:171
  10.4 3.6 %collective-permute-start = (bf16[2048,128]{1,0:T(8,128)(2,1)S(1)}, bf16[2048,128]{1,0:T(8,128)(2,1)S(1)}, u32[]{:S(2)}, u32[]{:S(2)}) collective-permute-start(bf16[2048,128]{1,0:T(8,128)(2,1)S(1)} %all_gather.3.centre), channel_id=1, source_target_pairs={{1,5},{2,10},{3,19},{5,9},{6,14},{7,23},{9,13},{10,18},{11,27},{13... | collective-permute-start | bytes 1572872 | tf_op jit(solution)/shard_map/ppermute | solution.py:172
  15.3 3.0 %fusion = (bf16[3,3,128,3,256]{4,2,0,3,1:T(8,128)(2,1)}, bf16[3,3,128,3,256]{4,2,3,1,0:T(8,128)(2,1)S(1)}) fusion(bf16[1,3,3,3,128,256]{5,4,3,2,1,0:T(8,128)(2,1)} %param.7, bf16[3,3,3]{2,1,0:T(4,128)(2,1)S(1)} %select_convert_fusion), kind=kLoop, calls=%fused_computation.2 | loop fusion | flops 884736 | bytes 5308470 | tf_op jit(solution)/shard_map/transpose | solution.py:180
  18.3 1.5 copy.12
  20.3 5.3 %collective-permute-done.below = bf16[2048,128]{1,0:T(8,128)(2,1)S(1)} collective-permute-done((bf16[2048,128]{1,0:T(8,128)(2,1)S(1)}, bf16[2048,128]{1,0:T(8,128)(2,1)S(1)}, u32[]{:S(2)}, u32[]{:S(2)}) %collective-permute-start) | collective-permute-done | bytes 524320 | tf_op jit(solution)/shard_map/ppermute | solution.py:172
  27.5 6.8 %shard_map.93 = (f32[2048,256]{1,0:T(8,128)S(1)}, bf16[2048,256]{1,0:T(8,128)(2,1)S(1)}, f32[2,512,256]{2,1,0:T(8,128)S(1)}, bf16[2,512,256]{2,1,0:T(8,128)(2,1)S(1)}) custom-call(s32[1]{0:T(128)} %bitcast.core_ref, bf16[2048,128]{1,0:T(8,128)(2,1)S(1)} %collective-permute-done.below, bf16[2048,128]{1,0:T(8,128)(2,1)S(1)} %all_gather.3.centre, ...), custom_call_target="tpu_custom_call" | custom-call | flops 3623878656 | bytes 8000000 | tf_op jit(solution)/shard_map/pallas_call | solution.py:136
  35.7 2.0 %collective-permute-done.2 = bf16[2,512,256]{2,1,0:T(8,128)(2,1)} collective-permute-done((bf16[2,512,256]{2,1,0:T(8,128)(2,1)S(1)}, bf16[2,512,256]{2,1,0:T(8,128)(2,1)}, u32[]{:S(2)}, u32[]{:S(2)}) %collective-permute-start.2) | collective-permute-done | bytes 524320 | tf_op jit(solution)/shard_map/ppermute | solution.py:192
  37.7 1.9 fusion.2
  39.6 10.8 %collective-permute-start.3 = (bf16[2,512,256]{2,1,0:T(8,128)(2,1)}, bf16[2,512,256]{2,1,0:T(8,128)(2,1)}, u32[]{:S(2)}, u32[]{:S(2)}) collective-permute-start(bf16[2,512,256]{2,1,0:T(8,128)(2,1)} %fusion.2), channel_id=1, source_target_pairs={{0,2},{2,0},{1,3},{3,1},{4,6},{6,4},{5,7},{7,5},{8,10},{10,8},{9,1... | collective-permute-start | bytes 1572872 | tf_op jit(solution)/shard_map/ppermute | solution.py:201
  50.5 17.9 %collective-permute-done.4 = bf16[512,256]{1,0:T(8,128)(2,1)} collective-permute-done((bf16[512,256]{1,0:T(8,128)(2,1)S(1)}, bf16[512,256]{1,0:T(8,128)(2,1)}, u32[]{:S(2)}, u32[]{:S(2)}) %collective-permute-start.4) | collective-permute-done | bytes 262176 | tf_op jit(solution)/shard_map/ppermute | solution.py:182
  69.4 2.8 %multiply_convert_fusion = (bf16[2,512,256]{2,1,0:T(8,128)(2,1)S(1)}, f32[2,512,256]{2,1,0:T(8,128)}) fusion(bf16[1,512,256]{2,1,0:T(8,128)(2,1)S(1)} %get-tuple-element.31, bf16[1,512,256]{2,1,0:T(8,128)(2,1)S(1)} %get-tuple-element.30, f32[256]{0:T(256)S(1)} %copy-done.13, bf16[2,512,256]{2,1,0:T(8,128)(2,1)} %collective-permute-done.3, ...), kind=kLoop, calls=%fused_computation.5 | loop fusion | flops 4194304 | bytes 4195328 | tf_op jit(solution)/shard_map/convert_element_type | solution.py:205
  73.2 1.5 copy.13
  76.4 3.9 %shard_map.94 = (f32[2048,256]{1,0:T(8,128)S(1)}, bf16[256,2048]{1,0:T(8,128)(2,1)S(1)}, bf16[1152,2048]{1,0:T(8,128)(2,1)}) custom-call(bf16[2048,128]{1,0:T(8,128)(2,1)S(1)} %collective-permute-done.below, bf16[2048,128]{1,0:T(8,128)(2,1)S(1)} %all_gather.3.centre, bf16[2048,128]{1,0:T(8,128)(2,1)S(1)} %copy-done.4, f32[2048,256]{1,0:T(8,128)S(1)} %copy-done.1, ...), custom_call_target="tpu_custom_call" | custom-call | flops 1207959552 | bytes 8000000 | tf_op jit(solution)/shard_map/pallas_call | solution.py:136
  80.3 1.3 copy-done.6
  81.6 1.6 copy-done.7
  83.2 4.6 %shard_map.95 = (bf16[2176,256]{1,0:T(8,128)(2,1)S(1)}, bf16[2048,128]{1,0:T(8,128)(2,1)S(1)}, f32[2048,128]{1,0:T(8,128)S(1)}, bf16[2048,128]{1,0:T(8,128)(2,1)S(1)}) custom-call(s32[1]{0:T(128)} %bitcast.core_ref, bf16[2,512,256]{2,1,0:T(8,128)(2,1)S(1)} %get-tuple-element.26.own, bf16[2,512,256]{2,1,0:T(8,128)(2,1)S(1)} %collective-permute-done.5.other, ...), custom_call_target="tpu_custom_call" | custom-call | flops 3623878656 | bytes 8000000 | tf_op jit(solution)/shard_map/pallas_call | solution.py:136
  87.8 4.2 %shard_map.96 = bf16[3712,256]{1,0:T(8,128)(2,1)S(1)} custom-call(s32[1]{0:T(128)} %bitcast.core_ref, f32[1]{0:T(128)} %bitcast.16.keep_ref, bf16[2176,256]{1,0:T(8,128)(2,1)S(1)} %get-tuple-element.23.d_pre, bf16[1152,2048]{1,0:T(8,128)(2,1)S(1)} %copy-done.5, bf16[256,2048]{1,0:T(8,128)(2,1)S(1)} %get-tuple-element.25.hidden_t, ...), custom_call_target="tpu_custom_call" | custom-call | flops 3623878656 | bytes 8000000 | tf_op jit(solution)/shard_map/pallas_call | solution.py:136
  92.0 29.7 %all_to_all.20 = bf16[8,464,256]{2,1,0:T(8,128)(2,1)} all-to-all(bf16[8,464,256]{2,1,0:T(8,128)(2,1)S(1)} %bitcast.47), channel_id=1, replica_groups=mesh['z'=8,'x'=4,'yh'=2,'yl'=2,'c'=2] {'x','yh'}, dimensions={0} | all-to-all | bytes 3801088 | tf_op jit(solution)/shard_map/all_to_all | solution.py:230
  121.7 1.9 reduce_sum.24
  124.3 8.9 %all-to-all-start.1 = ((bf16[8,58,256]{2,1,0:T(8,128)(2,1)}), bf16[8,58,256]{2,1,0:T(8,128)(2,1)S(1)}, u32[]{:S(2)}, u32[]{:S(2)}) async-start(bf16[8,58,256]{2,1,0:T(8,128)(2,1)} %reshape.93), calls=%async_computation.1 | async-start | bytes 524288 | tf_op jit(solution)/shard_map/all_to_all | solution.py:232
  133.2 3.6 %collective-permute-start.7 = (bf16[2048,128]{1,0:T(8,128)(2,1)S(1)}, bf16[2048,128]{1,0:T(8,128)(2,1)}, u32[]{:S(2)}, u32[]{:S(2)}) collective-permute-start(bf16[2048,128]{1,0:T(8,128)(2,1)S(1)} %get-tuple-element.22), channel_id=1, source_target_pairs={{1,5},{2,10},{3,19},{5,9},{6,14},{7,23},{9,13},{10,18},{11,27},{13... | collective-permute-start | bytes 1572872 | tf_op jit(solution)/shard_map/ppermute | solution.py:218
  138.0 4.8 %all-to-all-done.1 = bf16[8,58,256]{2,1,0:T(8,128)(2,1)S(1)} async-done(((bf16[8,58,256]{2,1,0:T(8,128)(2,1)}), bf16[8,58,256]{2,1,0:T(8,128)(2,1)S(1)}, u32[]{:S(2)}, u32[]{:S(2)}) %all-to-all-start.1) | async-done | bytes 237600 | tf_op jit(solution)/shard_map/all_to_all | solution.py:232
  143.6 8.0 %all-to-all-start.2 = ((bf16[8,58,256]{2,1,0:T(8,128)(2,1)}), bf16[8,58,256]{2,1,0:T(8,128)(2,1)S(1)}, u32[]{:S(2)}, u32[]{:S(2)}) async-start(bf16[8,58,256]{2,1,0:T(8,128)(2,1)} %broadcast_in_dim.33), calls=%async_computation.2 | async-start | bytes 524288 | tf_op jit(solution)/shard_map/all_to_all | solution.py:159
  151.6 11.1 %all-to-all-done.2 = bf16[8,58,256]{2,1,0:T(8,128)(2,1)S(1)} async-done(((bf16[8,58,256]{2,1,0:T(8,128)(2,1)}), bf16[8,58,256]{2,1,0:T(8,128)(2,1)S(1)}, u32[]{:S(2)}, u32[]{:S(2)}) %all-to-all-start.2) | async-done | bytes 237600 | tf_op jit(solution)/shard_map/all_to_all | solution.py:159
  162.8 1.4 broadcast_in_dim.35
  164.1 4.3 %all-to-all-start.3 = ((bf16[8,464,256]{2,1,0:T(8,128)(2,1)}), bf16[8,464,256]{2,1,0:T(8,128)(2,1)}, u32[]{:S(2)}, u32[]{:S(2)}) async-start(bf16[8,464,256]{2,1,0:T(8,128)(2,1)} %broadcast_in_dim.35), calls=%async_computation.3 | async-start | bytes 3801088 | tf_op jit(solution)/shard_map/all_to_all | solution.py:159
  168.5 1.4 convert_add_fusion
  170.2 1.4 collective-permute-done.8
  172.9 18.8 %collective-permute-done.9 = bf16[512,128]{1,0:T(8,128)(2,1)S(1)} collective-permute-done((bf16[512,128]{1,0:T(8,128)(2,1)S(1)}, bf16[512,128]{1,0:T(8,128)(2,1)S(1)}, u32[]{:S(2)}, u32[]{:S(2)}) %collective-permute-start.9) | collective-permute-done | bytes 131104 | tf_op jit(solution)/shard_map/ppermute | solution.py:243
  192.5 4.6 %all-to-all-done.3 = bf16[8,464,256]{2,1,0:T(8,128)(2,1)} async-done(((bf16[8,464,256]{2,1,0:T(8,128)(2,1)}), bf16[8,464,256]{2,1,0:T(8,128)(2,1)}, u32[]{:S(2)}, u32[]{:S(2)}) %all-to-all-start.3) | async-done | bytes 1900576 | tf_op jit(solution)/shard_map/all_to_all | solution.py:159
  197.0 1.8 bitcast_convert_fusion
  198.9 2.0 %slice.18 = f32[3456,256]{1,0:T(8,128)} slice(f32[3712,256]{1,0:T(8,128)S(1)} %bitcast_convert_fusion), slice={[0:3456], [0:256]} | slice | bytes 7077888 | tf_op jit(solution)/shard_map/slice | solution.py:248
  (53 shorter events, 14.3 us)
Async XLA Ops:
  10.4 15.3 %collective-permute-start = (bf16[2048,128]{1,0:T(8,128)(2,1)S(1)}, bf16[2048,128]{1,0:T(8,128)(2,1)S(1)}, u32[]{:S(2)}, u32[]{:S(2)}) collective-permute-start(bf16[2048,128]{1,0:T(8,128)(2,1)S(1)} %all_gather.3.centre), channel_id=1, source_target_pairs={{1,5},{2,10},{3,19},{5,9},{6,14},{7,23},{9,13},{10,18},{11,27},{13... | collective-permute-start | bytes 1572872 | tf_op jit(solution)/shard_map/ppermute | solution.py:172
  14.0 11.7 %collective-permute-start.1 = (bf16[2048,128]{1,0:T(8,128)(2,1)S(1)}, bf16[2048,128]{1,0:T(8,128)(2,1)S(1)}, u32[]{:S(2)}, u32[]{:S(2)}) collective-permute-start(bf16[2048,128]{1,0:T(8,128)(2,1)S(1)} %all_gather.3.centre), channel_id=1, source_target_pairs={{5,1},{9,5},{10,2},{13,9},{14,6},{17,13},{18,10},{19,3},{21,17},{2... | collective-permute-start | bytes 1572872 | tf_op jit(solution)/shard_map/ppermute | solution.py:173
  19.9 6.6 %copy-start.8 = (bf16[1,256,256]{2,1,0:T(8,128)(2,1)S(1)}, bf16[1,256,256]{2,1,0:T(8,128)(2,1)}, u32[]{:S(2)}) copy-start(bf16[1,256,256]{2,1,0:T(8,128)(2,1)} %param.9) | copy-start | bytes 393220
  19.9 6.6 %copy-start.9 = (f32[1,256]{1,0:T(1,128)S(1)}, f32[1,256]{1,0:T(1,128)}, u32[]{:S(2)}) copy-start(f32[1,256]{1,0:T(1,128)} %bias.1) | copy-start | bytes 3076
  25.7 0.8 copy-start.2
  26.5 1.0 copy-start.3
  34.3 1.3 copy-start
  35.6 14.8 %copy-start.12 = (bf16[8,4,16,256]{3,2,1,0:T(8,128)(2,1)S(1)}, bf16[8,4,16,256]{3,2,1,0:T(8,128)(2,1)}, u32[]{:S(2)}) copy-start(bf16[8,4,16,256]{3,2,1,0:T(8,128)(2,1)} %param.11) | copy-start | bytes 786436
  35.6 33.8 %copy-start.13 = (f32[256]{0:T(256)S(1)}, f32[256]{0:T(256)}, u32[]{:S(2)}) copy-start(f32[256]{0:T(256)} %param.10) | copy-start | bytes 3076
  35.6 2.0 %collective-permute-start.2 = (bf16[2,512,256]{2,1,0:T(8,128)(2,1)S(1)}, bf16[2,512,256]{2,1,0:T(8,128)(2,1)}, u32[]{:S(2)}, u32[]{:S(2)}) collective-permute-start(bf16[2,512,256]{2,1,0:T(8,128)(2,1)S(1)} %get-tuple-element.16), channel_id=1, source_target_pairs={{0,1},{1,0},{2,3},{3,2},{4,5},{5,4},{6,7},{7,6},{8,9},{9,8},{10,11... | collective-permute-start | bytes 1572872 | tf_op jit(solution)/shard_map/ppermute | solution.py:192
  39.6 29.8 %collective-permute-start.3 = (bf16[2,512,256]{2,1,0:T(8,128)(2,1)}, bf16[2,512,256]{2,1,0:T(8,128)(2,1)}, u32[]{:S(2)}, u32[]{:S(2)}) collective-permute-start(bf16[2,512,256]{2,1,0:T(8,128)(2,1)} %fusion.2), channel_id=1, source_target_pairs={{0,2},{2,0},{1,3},{3,1},{4,6},{6,4},{5,7},{7,5},{8,10},{10,8},{9,1... | collective-permute-start | bytes 1572872 | tf_op jit(solution)/shard_map/ppermute | solution.py:201
  50.5 17.9 %collective-permute-start.4 = (bf16[512,256]{1,0:T(8,128)(2,1)S(1)}, bf16[512,256]{1,0:T(8,128)(2,1)}, u32[]{:S(2)}, u32[]{:S(2)}) collective-permute-start(bf16[512,256]{1,0:T(8,128)(2,1)S(1)} %bitcast.58), channel_id=1, source_target_pairs={{0,2},{2,0},{1,3},{3,1},{4,6},{6,4},{5,7},{7,5},{8,10},{10,8},{9,1... | collective-permute-start | bytes 786440 | tf_op jit(solution)/shard_map/ppermute | solution.py:182
  69.4 3.7 %copy-start.10 = (bf16[3,3,128,3,256]{4,2,0,3,1:T(8,128)(2,1)S(1)}, bf16[3,3,128,3,256]{4,2,0,3,1:T(8,128)(2,1)}, u32[]{:S(2)}) copy-start(bf16[3,3,128,3,256]{4,2,0,3,1:T(8,128)(2,1)} %get-tuple-element.28) | copy-start | bytes 5308420
  72.3 9.3 %collective-permute-start.5 = (bf16[2,512,256]{2,1,0:T(8,128)(2,1)S(1)}, bf16[2,512,256]{2,1,0:T(8,128)(2,1)S(1)}, u32[]{:S(2)}, u32[]{:S(2)}) collective-permute-start(bf16[2,512,256]{2,1,0:T(8,128)(2,1)S(1)} %get-tuple-element.26.own), channel_id=1, source_target_pairs={{0,1},{1,0},{2,3},{3,2},{4,5},{5,4},{6,7},{7,6},{8,9},{9,8},{10,11... | collective-permute-start | bytes 1572872 | tf_op jit(solution)/shard_map/ppermute | solution.py:207
  74.7 1.6 copy-start.1
  74.7 1.7 copy-start.4
  80.3 1.3 copy-start.6
  81.6 1.6 copy-start.7
  83.2 4.6 %copy-start.5 = (bf16[1152,2048]{1,0:T(8,128)(2,1)S(1)}, bf16[1152,2048]{1,0:T(8,128)(2,1)}, u32[]{:S(2)}) copy-start(bf16[1152,2048]{1,0:T(8,128)(2,1)} %get-tuple-element.24.features_t) | copy-start | bytes 14155780
  124.3 18.5 %all-to-all-start.1 = ((bf16[8,58,256]{2,1,0:T(8,128)(2,1)}), bf16[8,58,256]{2,1,0:T(8,128)(2,1)S(1)}, u32[]{:S(2)}, u32[]{:S(2)}) async-start(bf16[8,58,256]{2,1,0:T(8,128)(2,1)} %reshape.93), calls=%async_computation.1 | async-start | bytes 524288 | tf_op jit(solution)/shard_map/all_to_all | solution.py:232
  133.2 35.3 %collective-permute-start.7 = (bf16[2048,128]{1,0:T(8,128)(2,1)S(1)}, bf16[2048,128]{1,0:T(8,128)(2,1)}, u32[]{:S(2)}, u32[]{:S(2)}) collective-permute-start(bf16[2048,128]{1,0:T(8,128)(2,1)S(1)} %get-tuple-element.22), channel_id=1, source_target_pairs={{1,5},{2,10},{3,19},{5,9},{6,14},{7,23},{9,13},{10,18},{11,27},{13... | collective-permute-start | bytes 1572872 | tf_op jit(solution)/shard_map/ppermute | solution.py:218
  136.8 31.7 %collective-permute-start.6 = (bf16[2048,128]{1,0:T(8,128)(2,1)S(1)}, bf16[2048,128]{1,0:T(8,128)(2,1)}, u32[]{:S(2)}, u32[]{:S(2)}) collective-permute-start(bf16[2048,128]{1,0:T(8,128)(2,1)S(1)} %get-tuple-element.21), channel_id=1, source_target_pairs={{5,1},{9,5},{10,2},{13,9},{14,6},{17,13},{18,10},{19,3},{21,17},{2... | collective-permute-start | bytes 1572872 | tf_op jit(solution)/shard_map/ppermute | solution.py:217
  143.6 19.1 %all-to-all-start.2 = ((bf16[8,58,256]{2,1,0:T(8,128)(2,1)}), bf16[8,58,256]{2,1,0:T(8,128)(2,1)S(1)}, u32[]{:S(2)}, u32[]{:S(2)}) async-start(bf16[8,58,256]{2,1,0:T(8,128)(2,1)} %broadcast_in_dim.33), calls=%async_computation.2 | async-start | bytes 524288 | tf_op jit(solution)/shard_map/all_to_all | solution.py:159
  164.1 32.9 %all-to-all-start.3 = ((bf16[8,464,256]{2,1,0:T(8,128)(2,1)}), bf16[8,464,256]{2,1,0:T(8,128)(2,1)}, u32[]{:S(2)}, u32[]{:S(2)}) async-start(bf16[8,464,256]{2,1,0:T(8,128)(2,1)} %broadcast_in_dim.35), calls=%async_computation.3 | async-start | bytes 3801088 | tf_op jit(solution)/shard_map/all_to_all | solution.py:159
  168.5 1.6 copy-start.11
  170.0 1.6 collective-permute-start.8
  171.7 20.1 %collective-permute-start.9 = (bf16[512,128]{1,0:T(8,128)(2,1)S(1)}, bf16[512,128]{1,0:T(8,128)(2,1)S(1)}, u32[]{:S(2)}, u32[]{:S(2)}) collective-permute-start(bf16[512,128]{1,0:T(8,128)(2,1)S(1)} %fusion.5), channel_id=1, source_target_pairs={{0,2},{2,0},{1,3},{3,1},{4,6},{6,4},{5,7},{7,5},{8,10},{10,8},{9,1... | collective-permute-start | bytes 393224 | tf_op jit(solution)/shard_map/ppermute | solution.py:243

commit v2 on v1

v2 whole, which is shorter than its diff:
```python
import functools

import jax
import jax.numpy as jnp
from jax import lax
from jax.experimental import pallas as pl
from jax.experimental.pallas import tpu as pltpu
from jax.sharding import Mesh
from jax.sharding import PartitionSpec as P

C = 128
F = 256
COL = 64
ROWS = 2048
QUART = 512
TAPS = 27 * C
GRAD_ROWS = TAPS + F
bf16 = jnp.bfloat16
f32 = jnp.float32
GZ = ("z", "x", "yh")
BR = ("yl", "c")
SWAP = [(0, 1), (1, 0)]
VMEM = pl.BlockSpec(memory_space=pltpu.VMEM)
SMEM = pl.BlockSpec(memory_space=pltpu.SMEM)


def silu_slope(values):
    logistic = jax.nn.sigmoid(values)
    return logistic * (1.0 + values * (1.0 - logistic))


def height_of(rows, lanes):
    return lax.broadcasted_iota(jnp.int32, (rows, lanes), 0) & 15


def from_below(values):
    rolled = pltpu.roll(values, 1, 0)
    return jnp.where(height_of(*values.shape) == 0, 0.0, rolled)


def from_above(values):
    rolled = pltpu.roll(values, values.shape[0] - 1, 0)
    return jnp.where(height_of(*values.shape) == 15, 0.0, rolled)


def matmul(lhs, rhs):
    return jnp.dot(lhs, rhs, preferred_element_type=f32)


def matmul_rt(lhs, rhs):
    return lax.dot_general(lhs, rhs, (((1,), (1,)), ((), ())), preferred_element_type=f32)


def pad_columns(padded, slab):
    padded[0:COL] = jnp.zeros((COL, C), bf16)
    padded[COL + ROWS : 2 * COL + ROWS] = jnp.zeros((COL, C), bf16)
    padded[COL : COL + ROWS] = slab[...]


def over_height(parts):
    return parts[:, F : 2 * F] + from_below(parts[:, :F]) + from_above(parts[:, 2 * F :])


def centre_kernel(centre, weights, bias, base, padded):
    pad_columns(padded, centre)
    for q in range(4):
        start = q * QUART
        window = jnp.concatenate([padded[start + i * COL : start + i * COL + QUART] for i in range(3)], axis=1)
        base[start : start + QUART] = bias[...] + over_height(matmul(window, weights[3 * C : 6 * C]))


def forward_kernel(core_ref, below, above, weights, base, proj, preact, hidden, keep, send, low, high, outer):
    pad_columns(low, below)
    pad_columns(high, above)
    outer[: 3 * C] = weights[: 3 * C]
    outer[3 * C :] = weights[6 * C :]
    core = core_ref[0]
    for q in range(4):
        start = q * QUART
        window = jnp.concatenate(
            [slab[start + i * COL : start + i * COL + QUART] for slab in (low, high) for i in range(3)], axis=1
        )
        value = base[start : start + QUART] + over_height(matmul(window, outer[...]))
        preact[start : start + QUART] = value
        active = (value * jax.nn.sigmoid(value)).astype(bf16)
        hidden[start : start + QUART] = active
        projected = matmul(active, proj[...])

        @pl.when(core == q % 2)
        def _():
            keep[q // 2] = projected

        @pl.when(core != q % 2)
        def _():
            send[q // 2] = projected.astype(bf16)


def prepare_kernel(below, centre, above, preact, hidden, slope, hidden_t, features_t):
    for q in range(4):
        cells = slice(q * QUART, (q + 1) * QUART)
        slope[cells] = silu_slope(preact[cells])
        hidden_t[:, cells] = hidden[cells].astype(f32).T.astype(bf16)
        for t, slab in enumerate((below, centre, above)):
            value = slab[cells].astype(f32)
            for j, moved in enumerate((from_below(value), value, from_above(value))):
                block = (t * 3 + j) * C
                features_t[block : block + C, cells] = moved.T.astype(bf16)


def output_kernel(row_ref, chip_sum, recv, bias, cot_mine, cot_pair, own, head_out):
    row = row_ref[0]
    mine = chip_sum[row] + recv[row].astype(f32) + bias[...]
    head_out[...] = (mine * jax.nn.sigmoid(mine)).astype(bf16)
    own[row] = (cot_mine[...].astype(f32) * silu_slope(mine)).astype(bf16)
    pair = chip_sum[1 - row] + recv[1 - row].astype(f32) + bias[...]
    own[1 - row] = (cot_pair[...].astype(f32) * silu_slope(pair)).astype(bf16)


def gradient_kernel(
    core_ref, keep_ref, own, other, slope, proj, features_t, hidden_t, grads, d_pre, window, d_out
):
    d_pre[0:COL] = jnp.zeros((COL, F), bf16)
    d_pre[COL + ROWS : 2 * COL + ROWS] = jnp.zeros((COL, F), bf16)
    for q in range(4):
        start = q * QUART
        rows = jnp.where(core_ref[0] == q % 2, own[q // 2], other[q // 2])
        d_out[start : start + QUART] = rows
        d_hidden = matmul_rt(rows, proj[...])
        d_pre[COL + start : COL + start + QUART] = (d_hidden * slope[start : start + QUART]).astype(bf16)
    for i in range(3):
        window[:, i * F : (i + 1) * F] = d_pre[(2 - i) * COL : (2 - i) * COL + ROWS]
    off_centre = keep_ref[0]
    for t in range(3):
        block = matmul(features_t[t * 3 * C : (t + 1) * 3 * C], window[...])
        for i in range(3):
            for j in range(3):
                tap = (t * 9 + i * 3 + j) * C
                piece = block[j * C : (j + 1) * C, i * F : (i + 1) * F]
                if (t, i, j) != (1, 1, 1):
                    piece = piece * off_centre
                grads[tap : tap + C] = piece.astype(bf16)
    grads[TAPS:] = matmul(hidden_t[...], d_out[...]).astype(bf16)


def feature_kernel(d_pre, weights, low, mid, high):
    for q in range(4):
        start = q * QUART
        window = jnp.concatenate(
            [d_pre[start + (2 - i) * COL : start + (2 - i) * COL + QUART] for i in range(3)], axis=1
        )
        parts = matmul_rt(window, weights[...])
        total = parts[:, 3 * C : 6 * C] + from_above(parts[:, : 3 * C]) + from_below(parts[:, 6 * C :])
        cells = slice(start, start + QUART)
        low[cells] = total[:, :C].astype(bf16)
        mid[cells] = total[:, C : 2 * C]
        high[cells] = total[:, 2 * C :].astype(bf16)


def first_sum_kernel(parts, total):
    rows = parts.shape[1]
    acc = parts[0].astype(f32)
    for k in range(1, parts.shape[0]):
        acc = acc + parts[k].astype(f32)
    total[0:rows] = acc.astype(bf16)
    if total.shape[0] > rows:
        total[rows:] = jnp.zeros((total.shape[0] - rows, F), bf16)


def second_sum_kernel(parts, copies):
    acc = parts[0].astype(f32)
    for k in range(1, parts.shape[0]):
        acc = acc + parts[k].astype(f32)
    total = acc.astype(bf16)
    for k in range(copies.shape[0]):
        copies[k] = total


def call(kernel, outs, specs, scratch, flops, *args):
    return pl.pallas_call(
        kernel,
        out_shape=[jax.ShapeDtypeStruct(*o) for o in outs],
        in_specs=specs,
        out_specs=[VMEM] * len(outs),
        scratch_shapes=scratch,
        compiler_params=pltpu.CompilerParams(vmem_limit_bytes=16 * 1024 * 1024),
        cost_estimate=pl.CostEstimate(flops=flops, bytes_accessed=8_000_000, transcendentals=0),
    )(*args)


def depth_pairs(mesh_gz, sign):
    strides = (0, 1, 2, 4)
    pairs = []
    for g in range(mesh_gz):
        for b in range(1, 4):
            target = g + sign * strides[b]
            if 0 <= target < mesh_gz:
                pairs.append((g * 4 + b, target * 4 + b))
    return pairs


def shards(slabs, features, tap_weights, branch_bias, proj_weights, out_bias, cotangent):
    branch = lax.axis_index(BR)
    core = lax.axis_index("c")
    row = lax.axis_index("yl")
    core_arg = core.astype(jnp.int32)[None]
    row_arg = row.astype(jnp.int32)[None]
    up = depth_pairs(slabs, 1)
    down = depth_pairs(slabs, -1)
    everywhere = GZ + BR
    proj = proj_weights[0]

    centre = lax.all_gather(features.reshape(QUART, C), BR, axis=0, tiled=True)
    tap = jnp.arange(27).reshape(3, 3, 3)
    off_centre = jnp.where(branch > 0, 1.0, 0.0).astype(f32)
    mask = jnp.where(tap == 13, 1.0, off_centre).astype(bf16)
    cot_mine = cotangent.reshape(QUART, F)
    centre, cot_mine = lax.optimization_barrier((centre, cot_mine))
    below = lax.ppermute(centre, everywhere, up)
    above = lax.ppermute(centre, everywhere, down)
    cot_pair = lax.ppermute(cot_mine, "yl", SWAP)
    masked = tap_weights[0] * mask[:, :, :, None, None]
    weights_fwd = masked.transpose(0, 1, 3, 2, 4).reshape(9 * C, 3 * F)
    weights_bwd = masked.transpose(2, 0, 3, 1, 4).reshape(9 * C, 3 * F)
    (base,) = call(
        centre_kernel,
        [((ROWS, F), f32)],
        [VMEM] * 3,
        [pltpu.VMEM((ROWS + 2 * COL, C), bf16)],
        2 * ROWS * 9 * C * F,
        centre, weights_fwd, branch_bias,
    )
    below, above, cot_pair, base, weights_bwd = lax.optimization_barrier((below, above, cot_pair, base, weights_bwd))

    preact, hidden, keep, send = call(
        forward_kernel,
        [((ROWS, F), f32), ((ROWS, F), bf16), ((2, QUART, F), f32), ((2, QUART, F), bf16)],
        [SMEM] + [VMEM] * 5,
        [pltpu.VMEM((ROWS + 2 * COL, C), bf16)] * 2 + [pltpu.VMEM((6 * C, 3 * F), bf16)],
        2 * ROWS * 18 * C * F,
        core_arg, below, above, weights_fwd, base, proj,
    )
    chip_sum = keep + lax.ppermute(send, "c", SWAP).astype(f32)
    chip_send, preact, hidden = lax.optimization_barrier((chip_sum.astype(bf16), preact, hidden))
    recv = lax.ppermute(chip_send, "yl", SWAP)
    slope, hidden_t, features_t = call(
        prepare_kernel,
        [((ROWS, F), f32), ((F, ROWS), bf16), ((9 * C, ROWS), bf16)],
        [VMEM] * 5,
        [],
        2 * ROWS * 9 * C * F,
        below, centre, above, preact, hidden,
    )
    recv, slope, hidden_t, features_t = lax.optimization_barrier((recv, slope, hidden_t, features_t))
    own, head_out = call(
        output_kernel,
        [((2, QUART, F), bf16), ((QUART, F), bf16)],
        [SMEM] + [VMEM] * 5,
        [],
        1_000_000,
        row_arg, chip_sum, recv, out_bias[None], cot_mine, cot_pair,
    )
    other = lax.ppermute(own, "c", SWAP)

    grads, d_pre = call(
        gradient_kernel,
        [((GRAD_ROWS, F), bf16), ((ROWS + 2 * COL, F), bf16)],
        [SMEM, SMEM] + [VMEM] * 6,
        [pltpu.VMEM((ROWS, 3 * F), bf16), pltpu.VMEM((ROWS, F), bf16)],
        2 * ROWS * 27 * C * F,
        core_arg, off_centre[None], own, other, slope, proj, features_t, hidden_t,
    )
    plane = lax.axis_size("x") * lax.axis_size("yh")
    tall = lax.axis_size("z")
    share = GRAD_ROWS // plane
    piece = -(-share // (16 * tall)) * 16
    part = lax.all_to_all(grads.reshape(plane, share, F), ("x", "yh"), 0, 0, tiled=True)
    low, mid, high = call(
        feature_kernel,
        [((ROWS, C), bf16), ((ROWS, C), f32), ((ROWS, C), bf16)],
        [VMEM] * 2,
        [],
        2 * ROWS * 27 * C * F,
        d_pre, weights_bwd,
    )
    part, low, mid, high = lax.optimization_barrier((part, low, mid, high))
    from_low = lax.ppermute(low, everywhere, down)
    from_high = lax.ppermute(high, everywhere, up)
    (part,) = call(first_sum_kernel, [((tall * piece, F), bf16)], [VMEM], [], 1_000_000, part)
    part = lax.all_to_all(part.reshape(tall, piece, F), "z", 0, 0, tiled=True)
    (part,) = call(second_sum_kernel, [((tall, piece, F), bf16)], [VMEM], [], 100_000, part)
    part, from_low, from_high = lax.optimization_barrier((part, from_low, from_high))
    part = lax.all_to_all(part, "z", 0, 0, tiled=True).reshape(tall * piece, F)

    branch_grad = (mid + from_low.astype(f32) + from_high.astype(f32)).reshape(2, 2, QUART, C)
    sent = lax.dynamic_index_in_dim(branch_grad, 1 - core, 1, keepdims=False).astype(bf16)
    kept = lax.dynamic_index_in_dim(branch_grad, core, 1, keepdims=False)
    chip_grad = kept + lax.ppermute(sent, "c", SWAP).astype(f32)
    sent = lax.dynamic_index_in_dim(chip_grad, 1 - row, 0, keepdims=False).astype(bf16)
    kept = lax.dynamic_index_in_dim(chip_grad, row, 0, keepdims=False)
    feature_grad = (kept + lax.ppermute(sent, "yl", SWAP).astype(f32)).astype(bf16)
    part, feature_grad = lax.optimization_barrier((part, feature_grad))

    copies = jnp.broadcast_to(part[None, :share], (plane, share, F))
    total = lax.all_to_all(copies, ("x", "yh"), 0, 0, tiled=True).reshape(GRAD_ROWS, F)
    tap_total = total[:TAPS].astype(f32)
    proj_total = total[TAPS:].astype(f32)

    return (
        head_out.reshape(cotangent.shape),
        feature_grad.reshape(features.shape),
        tap_total.reshape(1, 3, 3, 3, C, F),
        proj_total.reshape(1, F, F),
    )


def solution(mesh):
    slabs = mesh.shape["gz"]
    split = (8, 4, 2) if slabs == 64 else (slabs, 1, 1)
    fine = Mesh(mesh.devices.reshape(split + (2, 2)), GZ + BR)
    in_specs = (
        P(BR, GZ, None, None),
        P(BR, None, None, None, None, None),
        P(BR, None),
        P(BR, None, None),
        P(),
        P(BR, GZ, None, None),
    )
    out_specs = (
        P(BR, GZ, None, None),
        P(BR, GZ, None, None),
        P(BR, None, None, None, None, None),
        P(BR, None, None),
    )
    return jax.shard_map(
        functools.partial(shards, slabs), mesh=fine, in_specs=in_specs, out_specs=out_specs, check_vma=False
    )
```

time: 202 us -> 182 us (0.901)
  the two profiles are of different devices: /device:TPU:1 before, /device:TPU:8 now
where the time goes in v2:
time: 182 us; the launch traced here: 181 us
  waiting for transfers between devices  73.6 us (40%)
  blocking collectives  40.7 us (22%)
  starting transfers between devices  27.5 us (15%)
  Pallas kernels  20.1 us (11%)
  local copies, waits for them, and re-layouts  11.3 us (6%)
  other arithmetic  6.94 us (4%)
    all_to_all x1, blocking collectives, shards(): lax.all_to_all(copies, ('x', 'yh'), 0, 0, tiled=True).reshape(GRAD_ROWS, F)  32.6 us
    all_to_all x1, waiting for transfers between devices, shards(): lax.all_to_all(grads.reshape(plane, share, F), ('x', 'yh'), 0, 0, tiled=T...  21.5 us
    pallas_call x8, Pallas kernels, call(): pl.pallas_call(kernel, out_shape=[jax.ShapeDtypeStruct(*o) for o in outs]...  20.1 us
    all_to_all x1, waiting for transfers between devices, shards(): part = lax.all_to_all(part.reshape(tall, piece, F), 'z', 0, 0, tiled=True)  12.2 us
    ppermute x1, waiting for transfers between devices, shards(): recv = lax.ppermute(chip_send, 'yl', SWAP)  11.6 us
    all_to_all x1, starting transfers between devices, shards(): part = lax.all_to_all(part.reshape(tall, piece, F), 'z', 0, 0, tiled=True)  8.31 us
    all_gather x1, blocking collectives, shards(): centre = lax.all_gather(features.reshape(QUART, C), BR, axis=0, tiled=True)  8.08 us
    unnamed x20, local copies, waits for them, and re-layouts  7.92 us
  transfers between devices with their start and end apart: 13, of which 9 were waited for; matrix products, arithmetic and copies ran while one was open for 4% of the time, Pallas kernels for 6%

profile of v2, /device:TPU:8, one launch (start us, length us, event | category | flops | bytes accessed | tf_op | source)
XLA Modules:
  0.0 181.0 jit_solution(1900987153786406679)
XLA Ops:
  0.6 8.1 %all_gather.3.centre = bf16[2048,128]{1,0:T(8,128)(2,1)S(1)} all-gather(bf16[512,128]{1,0:T(8,128)(2,1)} %bitcast.64), channel_id=1, replica_groups=mesh['z'=8,'x'=4,'yh'=2,'yl'=2,'c'=2] {'yl','c'}, dimensions={0}, use_global_device_ids=true | all-gather | bytes 655360 | tf_op jit(solution)/shard_map/all_gather | solution.py:212
  8.7 2.3 %collective-permute-start = (bf16[2048,128]{1,0:T(8,128)(2,1)S(1)}, bf16[2048,128]{1,0:T(8,128)(2,1)S(1)}, u32[]{:S(2)}, u32[]{:S(2)}) collective-permute-start(bf16[2048,128]{1,0:T(8,128)(2,1)S(1)} %all_gather.3.centre), channel_id=1, source_target_pairs={{1,5},{2,10},{3,19},{5,9},{6,14},{7,23},{9,13},{10,18},{11,27},{13... | collective-permute-start | bytes 1572872 | tf_op jit(solution)/shard_map/ppermute | solution.py:218
  11.0 1.3 collective-permute-start.1
  12.5 1.8 fusion
  14.3 1.5 copy.12
  16.2 1.5 copy.13
  17.8 1.7 copy.15
  19.5 1.8 shard_map.93.base
  21.3 6.2 %collective-permute-done.2.cot_pair = bf16[512,256]{1,0:T(8,128)(2,1)S(1)} collective-permute-done((bf16[512,256]{1,0:T(8,128)(2,1)}, bf16[512,256]{1,0:T(8,128)(2,1)S(1)}, u32[]{:S(2)}, u32[]{:S(2)}) %collective-permute-start.2) | collective-permute-done | bytes 262176 | tf_op jit(solution)/shard_map/ppermute | solution.py:220
  27.5 6.6 %collective-permute-done.1.above = bf16[2048,128]{1,0:T(8,128)(2,1)S(1)} collective-permute-done((bf16[2048,128]{1,0:T(8,128)(2,1)S(1)}, bf16[2048,128]{1,0:T(8,128)(2,1)S(1)}, u32[]{:S(2)}, u32[]{:S(2)}) %collective-permute-start.1) | collective-permute-done | bytes 524320 | tf_op jit(solution)/shard_map/ppermute | solution.py:219
  34.1 4.6 %shard_map.94 = (f32[2048,256]{1,0:T(8,128)S(1)}, bf16[2048,256]{1,0:T(8,128)(2,1)S(1)}, f32[2,512,256]{2,1,0:T(8,128)S(1)}, bf16[2,512,256]{2,1,0:T(8,128)(2,1)S(1)}) custom-call(s32[1]{0:T(128)} %bitcast.1.core_ref, bf16[2048,128]{1,0:T(8,128)(2,1)S(1)} %collective-permute-done.below, bf16[2048,128]{1,0:T(8,128)(2,1)S(1)} %collective-permute-done.1.above, ...), custom_call_target="tpu_custom_call" | custom-call | flops 2415919104 | bytes 8000000 | tf_op jit(solution)/shard_map/pallas_call | solution.py:179
  38.9 1.9 %collective-permute-done.3 = bf16[2,512,256]{2,1,0:T(8,128)(2,1)S(1)} collective-permute-done((bf16[2,512,256]{2,1,0:T(8,128)(2,1)S(1)}, bf16[2,512,256]{2,1,0:T(8,128)(2,1)S(1)}, u32[]{:S(2)}, u32[]{:S(2)}) %collective-permute-start.3) | collective-permute-done | bytes 524320 | tf_op jit(solution)/shard_map/ppermute | solution.py:242
  41.2 2.3 %shard_map.95 = (f32[2048,256]{1,0:T(8,128)S(1)}, bf16[256,2048]{1,0:T(8,128)(2,1)S(1)}, bf16[1152,2048]{1,0:T(8,128)(2,1)S(1)}) custom-call(bf16[2048,128]{1,0:T(8,128)(2,1)S(1)} %collective-permute-done.below, bf16[2048,128]{1,0:T(8,128)(2,1)S(1)} %all_gather.3.centre, bf16[2048,128]{1,0:T(8,128)(2,1)S(1)} %collective-permute-done.1.above, ...), custom_call_target="tpu_custom_call" | custom-call | flops 1207959552 | bytes 8000000 | tf_op jit(solution)/shard_map/pallas_call | solution.py:179
  43.5 11.6 %collective-permute-done.4.recv = bf16[2,512,256]{2,1,0:T(8,128)(2,1)S(1)} collective-permute-done((bf16[2,512,256]{2,1,0:T(8,128)(2,1)S(1)}, bf16[2,512,256]{2,1,0:T(8,128)(2,1)S(1)}, u32[]{:S(2)}, u32[]{:S(2)}) %collective-permute-start.4) | collective-permute-done | bytes 524320 | tf_op jit(solution)/shard_map/ppermute | solution.py:244
  56.1 1.9 %collective-permute-done.5.other = bf16[2,512,256]{2,1,0:T(8,128)(2,1)S(1)} collective-permute-done((bf16[2,512,256]{2,1,0:T(8,128)(2,1)S(1)}, bf16[2,512,256]{2,1,0:T(8,128)(2,1)S(1)}, u32[]{:S(2)}, u32[]{:S(2)}) %collective-permute-start.5) | collective-permute-done | bytes 524320 | tf_op jit(solution)/shard_map/ppermute | solution.py:262
  58.0 4.5 %shard_map.97 = (bf16[3712,256]{1,0:T(8,128)(2,1)S(1)}, bf16[2176,256]{1,0:T(8,128)(2,1)S(1)}) custom-call(s32[1]{0:T(128)} %bitcast.1.core_ref, f32[1]{0:T(128)} %bitcast.10.keep_ref, bf16[2,512,256]{2,1,0:T(8,128)(2,1)S(1)} %get-tuple-element.59.own, bf16[2,512,256]{2,1,0:T(8,128)(2,1)S(1)} %collective-permute-done.5.other, ...), custom_call_target="tpu_custom_call" | custom-call | flops 3623878656 | bytes 8000000 | tf_op jit(solution)/shard_map/pallas_call | solution.py:179
  62.5 1.2 copy-done
  64.8 3.6 %all-to-all-start = ((bf16[8,464,256]{2,1,0:T(8,128)(2,1)}), bf16[8,464,256]{2,1,0:T(8,128)(2,1)S(1)}, u32[]{:S(2)}, u32[]{:S(2)}) async-start(bf16[8,464,256]{2,1,0:T(8,128)(2,1)} %bitcast.47), calls=%async_computation | async-start | bytes 3801088 | tf_op jit(solution)/shard_map/all_to_all | solution.py:276
  68.4 1.5 copy-done.1
  69.8 1.2 copy-done.8
  71.1 4.3 %shard_map.98 = (bf16[2048,128]{1,0:T(8,128)(2,1)S(1)}, f32[2048,128]{1,0:T(8,128)S(1)}, bf16[2048,128]{1,0:T(8,128)(2,1)S(1)}) custom-call(bf16[2176,256]{1,0:T(8,128)(2,1)S(1)} %copy-done.8, bf16[1152,768]{1,0:T(8,128)(2,1)S(1)} %bitcast.48), custom_call_target="tpu_custom_call" | custom-call | flops 3623878656 | bytes 8000000 | tf_op jit(solution)/shard_map/pallas_call | solution.py:179
  76.2 21.5 %all-to-all-done.parts = bf16[8,464,256]{2,1,0:T(8,128)(2,1)S(1)} async-done(((bf16[8,464,256]{2,1,0:T(8,128)(2,1)}), bf16[8,464,256]{2,1,0:T(8,128)(2,1)S(1)}, u32[]{:S(2)}, u32[]{:S(2)}) %all-to-all-start) | async-done | bytes 1900576 | tf_op jit(solution)/shard_map/all_to_all | solution.py:276
  97.7 1.3 collective-permute-start.6
  98.9 5.4 %collective-permute-start.7 = (bf16[2048,128]{1,0:T(8,128)(2,1)S(1)}, bf16[2048,128]{1,0:T(8,128)(2,1)}, u32[]{:S(2)}, u32[]{:S(2)}) collective-permute-start(bf16[2048,128]{1,0:T(8,128)(2,1)S(1)} %get-tuple-element.71), channel_id=1, source_target_pairs={{1,5},{2,10},{3,19},{5,9},{6,14},{7,23},{9,13},{10,18},{11,27},{13... | collective-permute-start | bytes 1572872 | tf_op jit(solution)/shard_map/ppermute | solution.py:287
  105.3 8.3 %all-to-all-start.1 = ((bf16[8,64,256]{2,1,0:T(8,128)(2,1)}), bf16[8,64,256]{2,1,0:T(8,128)(2,1)S(1)}, u32[]{:S(2)}, u32[]{:S(2)}) async-start(bf16[8,64,256]{2,1,0:T(8,128)(2,1)} %bitcast.12), calls=%async_computation.1 | async-start | bytes 524288 | tf_op jit(solution)/shard_map/all_to_all | solution.py:289
  113.6 12.2 %all-to-all-done.1.parts = bf16[8,64,256]{2,1,0:T(8,128)(2,1)S(1)} async-done(((bf16[8,64,256]{2,1,0:T(8,128)(2,1)}), bf16[8,64,256]{2,1,0:T(8,128)(2,1)S(1)}, u32[]{:S(2)}, u32[]{:S(2)}) %all-to-all-start.1) | async-done | bytes 262176 | tf_op jit(solution)/shard_map/all_to_all | solution.py:289
  126.5 1.3 convert_add_fusion
  128.0 4.7 %all-to-all-start.2 = ((bf16[8,64,256]{2,1,0:T(8,128)(2,1)}), bf16[8,64,256]{2,1,0:T(8,128)(2,1)S(1)}, u32[]{:S(2)}, u32[]{:S(2)}) async-start(bf16[8,64,256]{2,1,0:T(8,128)(2,1)} %shard_map.100), calls=%async_computation.2 | async-start | bytes 524288 | tf_op jit(solution)/shard_map/all_to_all | solution.py:292
  132.9 5.6 %collective-permute-done.9 = bf16[512,128]{1,0:T(8,128)(2,1)S(1)} collective-permute-done((bf16[512,128]{1,0:T(8,128)(2,1)S(1)}, bf16[512,128]{1,0:T(8,128)(2,1)S(1)}, u32[]{:S(2)}, u32[]{:S(2)}) %collective-permute-start.9) | collective-permute-done | bytes 131104 | tf_op jit(solution)/shard_map/ppermute | solution.py:300
  139.2 6.1 %all-to-all-done.2 = bf16[8,64,256]{2,1,0:T(8,128)(2,1)S(1)} async-done(((bf16[8,64,256]{2,1,0:T(8,128)(2,1)}), bf16[8,64,256]{2,1,0:T(8,128)(2,1)S(1)}, u32[]{:S(2)}, u32[]{:S(2)}) %all-to-all-start.2) | async-done | bytes 262176 | tf_op jit(solution)/shard_map/all_to_all | solution.py:292
  145.4 32.6 %all_to_all.20 = bf16[8,464,256]{2,1,0:T(8,128)(2,1)S(1)} all-to-all(bf16[8,464,256]{2,1,0:T(8,128)(2,1)S(1)} %broadcast_in_dim.33), channel_id=1, replica_groups=mesh['z'=8,'x'=4,'yh'=2,'yl'=2,'c'=2] {'x','yh'}, dimensions={0} | all-to-all | bytes 3801088 | tf_op jit(solution)/shard_map/all_to_all | solution.py:304
  178.8 2.2 %convert.2 = f32[1,3,3,3,128,256]{5,4,3,2,1,0:T(8,128)} convert(bf16[1,3,3,3,128,256]{5,4,3,2,1,0:T(8,128)(2,1)S(1)} %bitcast.60) | non-fusion elementwise | flops 884736 | bytes 5308416 | tf_op jit(solution)/shard_map/reshape | solution.py:311
  (39 shorter events, 7.5 us)
Async XLA Ops:
  8.7 18.8 %collective-permute-start = (bf16[2048,128]{1,0:T(8,128)(2,1)S(1)}, bf16[2048,128]{1,0:T(8,128)(2,1)S(1)}, u32[]{:S(2)}, u32[]{:S(2)}) collective-permute-start(bf16[2048,128]{1,0:T(8,128)(2,1)S(1)} %all_gather.3.centre), channel_id=1, source_target_pairs={{1,5},{2,10},{3,19},{5,9},{6,14},{7,23},{9,13},{10,18},{11,27},{13... | collective-permute-start | bytes 1572872 | tf_op jit(solution)/shard_map/ppermute | solution.py:218
  11.0 23.1 %collective-permute-start.1 = (bf16[2048,128]{1,0:T(8,128)(2,1)S(1)}, bf16[2048,128]{1,0:T(8,128)(2,1)S(1)}, u32[]{:S(2)}, u32[]{:S(2)}) collective-permute-start(bf16[2048,128]{1,0:T(8,128)(2,1)S(1)} %all_gather.3.centre), channel_id=1, source_target_pairs={{5,1},{9,5},{10,2},{13,9},{14,6},{17,13},{18,10},{19,3},{21,17},{2... | collective-permute-start | bytes 1572872 | tf_op jit(solution)/shard_map/ppermute | solution.py:219
  12.3 15.2 %collective-permute-start.2 = (bf16[512,256]{1,0:T(8,128)(2,1)}, bf16[512,256]{1,0:T(8,128)(2,1)S(1)}, u32[]{:S(2)}, u32[]{:S(2)}) collective-permute-start(bf16[512,256]{1,0:T(8,128)(2,1)} %bitcast.51), channel_id=1, source_target_pairs={{0,2},{2,0},{1,3},{3,1},{4,6},{6,4},{5,7},{7,5},{8,10},{10,8},{9,1... | collective-permute-start | bytes 786440 | tf_op jit(solution)/shard_map/ppermute | solution.py:220
  17.8 1.7 copy-start.6
  19.5 14.6 %copy-start.5 = (bf16[1,256,256]{2,1,0:T(8,128)(2,1)S(1)}, bf16[1,256,256]{2,1,0:T(8,128)(2,1)}, u32[]{:S(2)}) copy-start(bf16[1,256,256]{2,1,0:T(8,128)(2,1)} %param.9) | copy-start | bytes 393220
  38.8 2.0 %collective-permute-start.3 = (bf16[2,512,256]{2,1,0:T(8,128)(2,1)S(1)}, bf16[2,512,256]{2,1,0:T(8,128)(2,1)S(1)}, u32[]{:S(2)}, u32[]{:S(2)}) collective-permute-start(bf16[2,512,256]{2,1,0:T(8,128)(2,1)S(1)} %get-tuple-element.47), channel_id=1, source_target_pairs={{0,1},{1,0},{2,3},{3,2},{4,5},{5,4},{6,7},{7,6},{8,9},{9,8},{10,11... | collective-permute-start | bytes 1572872 | tf_op jit(solution)/shard_map/ppermute | solution.py:242
  40.9 14.3 %copy-start.2 = (bf16[8,4,16,256]{3,2,1,0:T(8,128)(2,1)S(1)}, bf16[8,4,16,256]{3,2,1,0:T(8,128)(2,1)}, u32[]{:S(2)}) copy-start(bf16[8,4,16,256]{3,2,1,0:T(8,128)(2,1)} %param.11) | copy-start | bytes 786436
  40.9 14.2 %copy-start.3 = (f32[256]{0:T(256)S(1)}, f32[256]{0:T(256)}, u32[]{:S(2)}) copy-start(f32[256]{0:T(256)} %param.10) | copy-start | bytes 3076
  40.9 14.2 %collective-permute-start.4 = (bf16[2,512,256]{2,1,0:T(8,128)(2,1)S(1)}, bf16[2,512,256]{2,1,0:T(8,128)(2,1)S(1)}, u32[]{:S(2)}, u32[]{:S(2)}) collective-permute-start(bf16[2,512,256]{2,1,0:T(8,128)(2,1)S(1)} %get-tuple-element.50), channel_id=1, source_target_pairs={{0,2},{2,0},{1,3},{3,1},{4,6},{6,4},{5,7},{7,5},{8,10},{10,8},{9,1... | collective-permute-start | bytes 1572872 | tf_op jit(solution)/shard_map/ppermute | solution.py:244
  56.1 1.9 %collective-permute-start.5 = (bf16[2,512,256]{2,1,0:T(8,128)(2,1)S(1)}, bf16[2,512,256]{2,1,0:T(8,128)(2,1)S(1)}, u32[]{:S(2)}, u32[]{:S(2)}) collective-permute-start(bf16[2,512,256]{2,1,0:T(8,128)(2,1)S(1)} %get-tuple-element.59.own), channel_id=1, source_target_pairs={{0,1},{1,0},{2,3},{3,2},{4,5},{5,4},{6,7},{7,6},{8,9},{9,8},{10,11... | collective-permute-start | bytes 1572872 | tf_op jit(solution)/shard_map/ppermute | solution.py:262
  62.5 1.3 copy-start
  63.8 1.0 copy-start.7
  64.8 32.9 %all-to-all-start = ((bf16[8,464,256]{2,1,0:T(8,128)(2,1)}), bf16[8,464,256]{2,1,0:T(8,128)(2,1)S(1)}, u32[]{:S(2)}, u32[]{:S(2)}) async-start(bf16[8,464,256]{2,1,0:T(8,128)(2,1)} %bitcast.47), calls=%async_computation | async-start | bytes 3801088 | tf_op jit(solution)/shard_map/all_to_all | solution.py:276
  68.4 1.5 copy-start.1
  69.8 1.2 copy-start.8
  75.4 0.8 copy-start.4
  97.7 28.9 %collective-permute-start.6 = (bf16[2048,128]{1,0:T(8,128)(2,1)}, bf16[2048,128]{1,0:T(8,128)(2,1)}, u32[]{:S(2)}, u32[]{:S(2)}) collective-permute-start(bf16[2048,128]{1,0:T(8,128)(2,1)} %copy-done.4), channel_id=1, source_target_pairs={{5,1},{9,5},{10,2},{13,9},{14,6},{17,13},{18,10},{19,3},{21,17},{2... | collective-permute-start | bytes 1572872 | tf_op jit(solution)/shard_map/ppermute | solution.py:286
  98.9 27.6 %collective-permute-start.7 = (bf16[2048,128]{1,0:T(8,128)(2,1)S(1)}, bf16[2048,128]{1,0:T(8,128)(2,1)}, u32[]{:S(2)}, u32[]{:S(2)}) collective-permute-start(bf16[2048,128]{1,0:T(8,128)(2,1)S(1)} %get-tuple-element.71), channel_id=1, source_target_pairs={{1,5},{2,10},{3,19},{5,9},{6,14},{7,23},{9,13},{10,18},{11,27},{13... | collective-permute-start | bytes 1572872 | tf_op jit(solution)/shard_map/ppermute | solution.py:287
  105.3 20.5 %all-to-all-start.1 = ((bf16[8,64,256]{2,1,0:T(8,128)(2,1)}), bf16[8,64,256]{2,1,0:T(8,128)(2,1)S(1)}, u32[]{:S(2)}, u32[]{:S(2)}) async-start(bf16[8,64,256]{2,1,0:T(8,128)(2,1)} %bitcast.12), calls=%async_computation.1 | async-start | bytes 524288 | tf_op jit(solution)/shard_map/all_to_all | solution.py:289
  127.9 4.8 %collective-permute-start.8 = (bf16[2,512,128]{2,1,0:T(8,128)(2,1)S(1)}, bf16[2,512,128]{2,1,0:T(8,128)(2,1)S(1)}, u32[]{:S(2)}, u32[]{:S(2)}) collective-permute-start(bf16[2,512,128]{2,1,0:T(8,128)(2,1)S(1)} %fusion.2), channel_id=1, source_target_pairs={{0,1},{1,0},{2,3},{3,2},{4,5},{5,4},{6,7},{7,6},{8,9},{9,8},{10,11... | collective-permute-start | bytes 786440 | tf_op jit(solution)/shard_map/ppermute | solution.py:297
  128.0 17.2 %all-to-all-start.2 = ((bf16[8,64,256]{2,1,0:T(8,128)(2,1)}), bf16[8,64,256]{2,1,0:T(8,128)(2,1)S(1)}, u32[]{:S(2)}, u32[]{:S(2)}) async-start(bf16[8,64,256]{2,1,0:T(8,128)(2,1)} %shard_map.100), calls=%async_computation.2 | async-start | bytes 524288 | tf_op jit(solution)/shard_map/all_to_all | solution.py:292
  132.8 5.7 %collective-permute-start.9 = (bf16[512,128]{1,0:T(8,128)(2,1)S(1)}, bf16[512,128]{1,0:T(8,128)(2,1)S(1)}, u32[]{:S(2)}, u32[]{:S(2)}) collective-permute-start(bf16[512,128]{1,0:T(8,128)(2,1)S(1)} %fusion.4), channel_id=1, source_target_pairs={{0,2},{2,0},{1,3},{3,1},{4,6},{6,4},{5,7},{7,5},{8,10},{10,8},{9,1... | collective-permute-start | bytes 393224 | tf_op jit(solution)/shard_map/ppermute | solution.py:300

commit v3 on v2

v3 whole, which is shorter than its diff:
```python
import functools

import jax
import jax.numpy as jnp
from jax import lax
from jax.experimental import pallas as pl
from jax.experimental.pallas import tpu as pltpu
from jax.sharding import Mesh
from jax.sharding import PartitionSpec as P

C = 128
F = 256
COL = 64
ROWS = 2048
HALF = 1024
QUART = 512
TAPS = 27 * C
GRAD_ROWS = TAPS + F
bf16 = jnp.bfloat16
f32 = jnp.float32
GZ = ("zh", "zl", "x", "yh")
NEAR = ("zl", "x", "yh")
BR = ("yl", "c")
SWAP = [(0, 1), (1, 0)]
VMEM = pl.BlockSpec(memory_space=pltpu.VMEM)
HBM = pl.BlockSpec(memory_space=pltpu.HBM)
SMEM = pl.BlockSpec(memory_space=pltpu.SMEM)


def silu_slope(values):
    logistic = jax.nn.sigmoid(values)
    return logistic * (1.0 + values * (1.0 - logistic))


def height_of(rows, lanes):
    return lax.broadcasted_iota(jnp.int32, (rows, lanes), 0) & 15


def from_below(values):
    rolled = pltpu.roll(values, 1, 0)
    return jnp.where(height_of(*values.shape) == 0, 0.0, rolled)


def from_above(values):
    rolled = pltpu.roll(values, values.shape[0] - 1, 0)
    return jnp.where(height_of(*values.shape) == 15, 0.0, rolled)


def matmul(lhs, rhs):
    return jnp.dot(lhs, rhs, preferred_element_type=f32)


def matmul_rt(lhs, rhs):
    return lax.dot_general(lhs, rhs, (((1,), (1,)), ((), ())), preferred_element_type=f32)


def pad_columns(padded, slab):
    padded[0:COL] = jnp.zeros((COL, C), bf16)
    padded[COL + ROWS : 2 * COL + ROWS] = jnp.zeros((COL, C), bf16)
    padded[COL : COL + ROWS] = slab[...]


def pad_half(padded, slab, half):
    if half == 0:
        padded[0:COL] = jnp.zeros((COL, C), bf16)
        padded[COL:] = slab[0 : HALF + COL]
    else:
        padded[0 : HALF + COL] = slab[HALF - COL :]
        padded[HALF + COL :] = jnp.zeros((COL, C), bf16)


def over_height(parts):
    return parts[:, F : 2 * F] + from_below(parts[:, :F]) + from_above(parts[:, 2 * F :])


def centre_kernel(centre, weights, bias, base, padded):
    pad_columns(padded, centre)
    for q in range(4):
        start = q * QUART
        window = jnp.concatenate([padded[start + i * COL : start + i * COL + QUART] for i in range(3)], axis=1)
        base[start : start + QUART] = bias[...] + over_height(matmul(window, weights[...]))


def forward_kernel(half, core_ref, below, above, weights, base, proj, preact, hidden, keep, send, low, high):
    pad_half(low, below, half)
    pad_half(high, above, half)
    core = core_ref[0]
    for side in range(2):
        start = side * QUART
        cells = slice(start, start + QUART)
        window = jnp.concatenate(
            [slab[start + i * COL : start + i * COL + QUART] for slab in (low, high) for i in range(3)], axis=1
        )
        value = base[half * HALF + start : half * HALF + start + QUART] + over_height(matmul(window, weights[...]))
        preact[cells] = value
        active = (value * jax.nn.sigmoid(value)).astype(bf16)
        hidden[cells] = active
        projected = matmul(active, proj[...])

        @pl.when(core == side)
        def _():
            keep[...] = projected

        @pl.when(core != side)
        def _():
            send[...] = projected.astype(bf16)


def prepare_kernel(
    below, centre, above, preact_a, preact_b, hidden_a, hidden_b, slope, hidden_t, features_t
):
    for q in range(4):
        cells = slice(q * QUART, (q + 1) * QUART)
        local = slice(q % 2 * QUART, (q % 2 + 1) * QUART)
        preact, hidden = ((preact_a, hidden_a), (preact_b, hidden_b))[q // 2]
        slope[cells] = silu_slope(preact[local])
        hidden_t[:, cells] = hidden[local].astype(f32).T.astype(bf16)
        for t, slab in enumerate((below, centre, above)):
            value = slab[cells].astype(f32)
            for j, moved in enumerate((from_below(value), value, from_above(value))):
                block = (t * 3 + j) * C
                features_t[block : block + C, cells] = moved.T.astype(bf16)


def output_kernel(half, row_ref, chip_sum, recv, bias, cot_mine, cot_pair, own, head):
    summed = chip_sum[...] + recv[...].astype(f32) + bias[...]
    head[...] = (summed * jax.nn.sigmoid(summed)).astype(bf16)
    cot = jnp.where(row_ref[0] == half, cot_mine[...], cot_pair[...])
    own[...] = (cot.astype(f32) * silu_slope(summed)).astype(bf16)


def gradient_kernel(
    core_ref, keep_ref, own_a, own_b, other_a, other_b, slope, proj, features_t, hidden_t,
    grads_out, d_pre_out, grads, d_pre, window, d_out, sems,
):
    d_pre[0:COL] = jnp.zeros((COL, F), bf16)
    d_pre[COL + ROWS : 2 * COL + ROWS] = jnp.zeros((COL, F), bf16)
    for q in range(4):
        start = q * QUART
        own, other = ((own_a, other_a), (own_b, other_b))[q // 2]
        rows = jnp.where(core_ref[0] == q % 2, own[...], other[...])
        d_out[start : start + QUART] = rows
        d_hidden = matmul_rt(rows, proj[...])
        d_pre[COL + start : COL + start + QUART] = (d_hidden * slope[start : start + QUART]).astype(bf16)
    copies = [pltpu.make_async_copy(d_pre, d_pre_out, sems.at[4])]
    copies[0].start()
    for i in range(3):
        window[:, i * F : (i + 1) * F] = d_pre[(2 - i) * COL : (2 - i) * COL + ROWS]
    grads[TAPS:] = matmul(hidden_t[...], d_out[...]).astype(bf16)
    spans = [(TAPS, F)] + [(t * 9 * C, 9 * C) for t in range(3)]

    def send_span(k):
        first, count = spans[k]
        copy = pltpu.make_async_copy(
            grads.at[first : first + count], grads_out.at[first : first + count], sems.at[k]
        )
        copy.start()
        copies.append(copy)

    send_span(0)
    off_centre = keep_ref[0]
    for t in range(3):
        block = matmul(features_t[t * 3 * C : (t + 1) * 3 * C], window[...])
        for i in range(3):
            for j in range(3):
                tap = (t * 9 + i * 3 + j) * C
                piece = block[j * C : (j + 1) * C, i * F : (i + 1) * F]
                if (t, i, j) != (1, 1, 1):
                    piece = piece * off_centre
                grads[tap : tap + C] = piece.astype(bf16)
        send_span(t + 1)
    for copy in copies:
        copy.wait()


def feature_kernel(d_pre, weights, low, mid, high):
    for q in range(4):
        start = q * QUART
        window = jnp.concatenate(
            [d_pre[start + (2 - i) * COL : start + (2 - i) * COL + QUART] for i in range(3)], axis=1
        )
        parts = matmul_rt(window, weights[...])
        total = parts[:, 3 * C : 6 * C] + from_above(parts[:, : 3 * C]) + from_below(parts[:, 6 * C :])
        cells = slice(start, start + QUART)
        low[cells] = total[:, :C].astype(bf16)
        mid[cells] = total[:, C : 2 * C]
        high[cells] = total[:, 2 * C :].astype(bf16)


def sum_of(parts):
    acc = parts[0].astype(f32)
    for k in range(1, parts.shape[0]):
        acc = acc + parts[k].astype(f32)
    return acc.astype(bf16)


def sum_kernel(parts, copies, total, sems):
    total[...] = sum_of(parts)
    peers = copies.shape[0]
    moves = [pltpu.make_async_copy(total, copies.at[k], sems.at[k]) for k in range(peers)]
    for move in moves:
        move.start()
    for move in moves:
        move.wait()


def widen_kernel(total, taps_out, proj_out, wide, sems):
    moves = []
    for k in range(4):
        first = k * TAPS // 4
        last = first + TAPS // 4
        wide[first:last] = total[first:last].astype(f32)
        moves.append(pltpu.make_async_copy(wide.at[first:last], taps_out.at[first:last], sems.at[k]))
        moves[-1].start()
    wide[TAPS:] = total[TAPS:].astype(f32)
    moves.append(pltpu.make_async_copy(wide.at[TAPS:], proj_out, sems.at[4]))
    moves[-1].start()
    for move in moves:
        move.wait()


def call(kernel, outs, specs, scratch, flops, *args, place=VMEM):
    return pl.pallas_call(
        kernel,
        out_shape=[jax.ShapeDtypeStruct(*o) for o in outs],
        in_specs=specs,
        out_specs=[place] * len(outs),
        scratch_shapes=scratch,
        compiler_params=pltpu.CompilerParams(vmem_limit_bytes=12 * 1024 * 1024),
        cost_estimate=pl.CostEstimate(flops=flops, bytes_accessed=8_000_000, transcendentals=0),
    )(*args)


def depth_pairs(mesh_gz, sign):
    strides = (0, 1, 2, 4)
    pairs = []
    for g in range(mesh_gz):
        for b in range(1, 4):
            target = g + sign * strides[b]
            if 0 <= target < mesh_gz:
                pairs.append((g * 4 + b, target * 4 + b))
    return pairs


def shards(slabs, features, tap_weights, branch_bias, proj_weights, out_bias, cotangent):
    branch = lax.axis_index(BR)
    core = lax.axis_index("c")
    row = lax.axis_index("yl")
    core_arg = core.astype(jnp.int32)[None]
    row_arg = row.astype(jnp.int32)[None]
    up = depth_pairs(slabs, 1)
    down = depth_pairs(slabs, -1)
    everywhere = GZ + BR
    proj = proj_weights[0]

    centre = lax.all_gather(features.reshape(QUART, C), BR, axis=0, tiled=True)
    tap = jnp.arange(27).reshape(3, 3, 3)
    off_centre = jnp.where(branch > 0, 1.0, 0.0).astype(f32)
    mask = jnp.where(tap == 13, 1.0, off_centre).astype(bf16)
    cot_mine = cotangent.reshape(QUART, F)
    centre, cot_mine = lax.optimization_barrier((centre, cot_mine))
    below = lax.ppermute(centre, everywhere, up)
    above = lax.ppermute(centre, everywhere, down)
    cot_pair = lax.ppermute(cot_mine, "yl", SWAP)
    masked = tap_weights[0] * mask[:, :, :, None, None]
    by_window = masked.transpose(0, 1, 3, 2, 4).reshape(3, 3 * C, 3 * F)
    weights_mid = by_window[1]
    weights_out = jnp.concatenate([by_window[0], by_window[2]], axis=0)
    weights_bwd = masked.transpose(2, 0, 3, 1, 4).reshape(9 * C, 3 * F)
    (base,) = call(
        centre_kernel,
        [((ROWS, F), f32)],
        [VMEM] * 3,
        [pltpu.VMEM((ROWS + 2 * COL, C), bf16)],
        2 * ROWS * 9 * C * F,
        centre, weights_mid, branch_bias,
    )
    below, above, cot_pair, base, weights_out, weights_bwd = lax.optimization_barrier(
        (below, above, cot_pair, base, weights_out, weights_bwd)
    )

    def forward_half(half):
        return call(
            functools.partial(forward_kernel, half),
            [((HALF, F), f32), ((HALF, F), bf16), ((QUART, F), f32), ((QUART, F), bf16)],
            [SMEM] + [VMEM] * 5,
            [pltpu.VMEM((HALF + 2 * COL, C), bf16)] * 2,
            ROWS * 18 * C * F,
            core_arg, below, above, weights_out, base, proj,
        )

    preact_a, hidden_a, keep_a, send_a = forward_half(0)
    chip_a = keep_a + lax.ppermute(send_a, "c", SWAP).astype(f32)
    preact_b, hidden_b, keep_b, send_b = forward_half(1)
    chip_send_a, send_b = lax.optimization_barrier((chip_a.astype(bf16), send_b))
    recv_a = lax.ppermute(chip_send_a, "yl", SWAP)
    chip_b = keep_b + lax.ppermute(send_b, "c", SWAP).astype(f32)
    chip_send_b, preact_b = lax.optimization_barrier((chip_b.astype(bf16), preact_b))
    recv_b = lax.ppermute(chip_send_b, "yl", SWAP)
    slope, hidden_t, features_t = call(
        prepare_kernel,
        [((ROWS, F), f32), ((F, ROWS), bf16), ((9 * C, ROWS), bf16)],
        [VMEM] * 7,
        [],
        2 * ROWS * 9 * C * F,
        below, centre, above, preact_a, preact_b, hidden_a, hidden_b,
    )
    recv_a, slope, hidden_t, features_t = lax.optimization_barrier((recv_a, slope, hidden_t, features_t))

    def output_half(half, chip_sum, recv):
        return call(
            functools.partial(output_kernel, half),
            [((QUART, F), bf16), ((QUART, F), bf16)],
            [SMEM] + [VMEM] * 5,
            [],
            1_000_000,
            row_arg, chip_sum, recv, out_bias[None], cot_mine, cot_pair,
        )

    own_a, head_a = output_half(0, chip_a, recv_a)
    own_a, recv_b = lax.optimization_barrier((own_a, recv_b))
    other_a = lax.ppermute(own_a, "c", SWAP)
    own_b, head_b = output_half(1, chip_b, recv_b)
    other_b = lax.ppermute(own_b, "c", SWAP)

    grads, d_pre = call(
        gradient_kernel,
        [((GRAD_ROWS, F), bf16), ((ROWS + 2 * COL, F), bf16)],
        [SMEM, SMEM] + [VMEM] * 8,
        [
            pltpu.VMEM((GRAD_ROWS, F), bf16),
            pltpu.VMEM((ROWS + 2 * COL, F), bf16),
            pltpu.VMEM((ROWS, 3 * F), bf16),
            pltpu.VMEM((ROWS, F), bf16),
            pltpu.SemaphoreType.DMA((5,)),
        ],
        2 * ROWS * 27 * C * F,
        core_arg, off_centre[None], own_a, own_b, other_a, other_b, slope, proj, features_t, hidden_t,
        place=HBM,
    )
    near = lax.axis_size("zl") * lax.axis_size("x") * lax.axis_size("yh")
    far = lax.axis_size("zh")
    share = GRAD_ROWS // near
    part = lax.all_to_all(grads.reshape(near, share, F), NEAR, 0, 0, tiled=True)
    low, mid, high = call(
        feature_kernel,
        [((ROWS, C), bf16), ((ROWS, C), f32), ((ROWS, C), bf16)],
        [VMEM] * 2,
        [],
        2 * ROWS * 27 * C * F,
        d_pre, weights_bwd,
    )

    def sum_for(peers, parts):
        return call(
            sum_kernel,
            [((peers, share, F), bf16)],
            [VMEM],
            [pltpu.VMEM((share, F), bf16), pltpu.SemaphoreType.DMA((peers,))],
            1_000_000,
            parts,
            place=HBM,
        )[0]

    part = sum_for(far, part)
    part, low, high = lax.optimization_barrier((part, low, high))
    part = lax.all_to_all(part, "zh", 0, 0, tiled=True)
    from_low = lax.ppermute(low, everywhere, down)
    from_high = lax.ppermute(high, everywhere, up)
    part = sum_for(near, part)
    part, mid, from_low, from_high = lax.optimization_barrier((part, mid, from_low, from_high))
    total = lax.all_to_all(part, NEAR, 0, 0, tiled=True).reshape(GRAD_ROWS, F)

    branch_grad = (mid + from_low.astype(f32) + from_high.astype(f32)).reshape(2, 2, QUART, C)
    sent = lax.dynamic_index_in_dim(branch_grad, 1 - core, 1, keepdims=False).astype(bf16)
    kept = lax.dynamic_index_in_dim(branch_grad, core, 1, keepdims=False)
    chip_grad = kept + lax.ppermute(sent, "c", SWAP).astype(f32)
    sent = lax.dynamic_index_in_dim(chip_grad, 1 - row, 0, keepdims=False).astype(bf16)
    kept = lax.dynamic_index_in_dim(chip_grad, row, 0, keepdims=False)
    feature_grad = (kept + lax.ppermute(sent, "yl", SWAP).astype(f32)).astype(bf16)
    head_out = jnp.where(row == 0, head_a, head_b)

    taps, proj_total = call(
        widen_kernel,
        [((TAPS, F), f32), ((F, F), f32)],
        [VMEM],
        [pltpu.VMEM((GRAD_ROWS, F), f32), pltpu.SemaphoreType.DMA((5,))],
        1_000_000,
        total,
        place=HBM,
    )
    return (
        head_out.reshape(cotangent.shape),
        feature_grad.reshape(features.shape),
        taps.reshape(1, 3, 3, 3, C, F),
        proj_total.reshape(1, F, F),
    )


def solution(mesh):
    slabs = mesh.shape["gz"]
    split = (4, 2, 4, 2) if slabs == 64 else (slabs, 1, 1, 1)
    fine = Mesh(mesh.devices.reshape(split + (2, 2)), GZ + BR)
    in_specs = (
        P(BR, GZ, None, None),
        P(BR, None, None, None, None, None),
        P(BR, None),
        P(BR, None, None),
        P(),
        P(BR, GZ, None, None),
    )
    out_specs = (
        P(BR, GZ, None, None),
        P(BR, GZ, None, None),
        P(BR, None, None, None, None, None),
        P(BR, None, None),
    )
    return jax.shard_map(
        functools.partial(shards, slabs), mesh=fine, in_specs=in_specs, out_specs=out_specs, check_vma=False
    )
```

time: 182 us -> 183 us (level)
  the two profiles are of different devices: /device:TPU:8 before, /device:TPU:15 now
where the time goes in v3:
time: 183 us; the launch traced here: 182 us
  waiting for transfers between devices  87 us (48%)
  starting transfers between devices  40.6 us (22%)
  Pallas kernels  25.7 us (14%)
  local copies, waits for them, and re-layouts  13.7 us (7%)
  blocking collectives  7.5 us (4%)
  other arithmetic  6.83 us (4%)
    pallas_call x11, Pallas kernels, call(): pl.pallas_call(kernel, out_shape=[jax.ShapeDtypeStruct(*o) for o in outs]...  25.7 us
    all_to_all x1, waiting for transfers between devices, shards(): part = lax.all_to_all(grads.reshape(near, share, F), NEAR, 0, 0, tiled=True)  22.2 us
    all_to_all x1, waiting for transfers between devices, shards(): total = lax.all_to_all(part, NEAR, 0, 0, tiled=True).reshape(GRAD_ROWS, F)  14.7 us
    ppermute x1, waiting for transfers between devices, shards(): lax.ppermute(sent, 'yl', SWAP).astype(f32)  14 us
    all_to_all x1, starting transfers between devices, shards(): part = lax.all_to_all(part, 'zh', 0, 0, tiled=True)  10.5 us
    unnamed x28, local copies, waits for them, and re-layouts  9.4 us
    all_gather x1, blocking collectives, shards(): centre = lax.all_gather(features.reshape(QUART, C), BR, axis=0, tiled=True)  7.5 us
    ppermute x1, waiting for transfers between devices, shards(): from_high = lax.ppermute(high, everywhere, up)  7.4 us
  transfers between devices with their start and end apart: 16, of which 14 were waited for; matrix products, arithmetic and copies ran while one was open for 7% of the time, Pallas kernels for 7%

profile of v3, /device:TPU:15, one launch (start us, length us, event | category | flops | bytes accessed | tf_op | source)
XLA Modules:
  0.0 182.4 jit_solution(14936941816731432276)
XLA Ops:
  0.6 7.5 %all_gather.3.centre = bf16[2048,128]{1,0:T(8,128)(2,1)S(1)} all-gather(bf16[512,128]{1,0:T(8,128)(2,1)} %bitcast.65), channel_id=1, replica_groups=mesh['zh'=4,'zl'=2,'x'=4,'yh'=2,'yl'=2,'c'=2] {'yl','c'}, dimensions={0}, use_global_device_ids=true | all-gather | bytes 655360 | tf_op jit(solution)/shard_map/all_gather | solution.py:256
  8.1 4.4 %collective-permute-start = (bf16[2048,128]{1,0:T(8,128)(2,1)S(1)}, bf16[2048,128]{1,0:T(8,128)(2,1)S(1)}, u32[]{:S(2)}, u32[]{:S(2)}) collective-permute-start(bf16[2048,128]{1,0:T(8,128)(2,1)S(1)} %all_gather.3.centre), channel_id=1, source_target_pairs={{1,5},{2,10},{3,19},{5,9},{6,14},{7,23},{9,13},{10,18},{11,27},{13... | collective-permute-start | bytes 1572872 | tf_op jit(solution)/shard_map/ppermute | solution.py:262
  12.5 2.4 %collective-permute-start.1 = (bf16[2048,128]{1,0:T(8,128)(2,1)S(1)}, bf16[2048,128]{1,0:T(8,128)(2,1)S(1)}, u32[]{:S(2)}, u32[]{:S(2)}) collective-permute-start(bf16[2048,128]{1,0:T(8,128)(2,1)S(1)} %all_gather.3.centre), channel_id=1, source_target_pairs={{5,1},{9,5},{10,2},{13,9},{14,6},{17,13},{18,10},{19,3},{21,17},{2... | collective-permute-start | bytes 1572872 | tf_op jit(solution)/shard_map/ppermute | solution.py:263
  15.0 1.6 collective-permute-start.2
  16.6 1.8 fusion
  20.4 1.5 copy.17
  21.9 1.7 copy.21
  23.6 1.8 shard_map.93.base
  25.5 5.6 %collective-permute-done.2.cot_pair = bf16[512,256]{1,0:T(8,128)(2,1)S(1)} collective-permute-done((bf16[512,256]{1,0:T(8,128)(2,1)}, bf16[512,256]{1,0:T(8,128)(2,1)S(1)}, u32[]{:S(2)}, u32[]{:S(2)}) %collective-permute-start.2) | collective-permute-done | bytes 262176 | tf_op jit(solution)/shard_map/ppermute | solution.py:264
  32.0 2.3 %shard_map.94 = (f32[1024,256]{1,0:T(8,128)S(1)}, bf16[1024,256]{1,0:T(8,128)(2,1)S(1)}, f32[512,256]{1,0:T(8,128)S(1)}, bf16[512,256]{1,0:T(8,128)(2,1)S(1)}) custom-call(s32[1]{0:T(128)} %bitcast.1.core_ref, bf16[2048,128]{1,0:T(8,128)(2,1)S(1)} %collective-permute-done.below, bf16[2048,128]{1,0:T(8,128)(2,1)S(1)} %collective-permute-done.1.above, ...), custom_call_target="tpu_custom_call" | custom-call | flops 1207959552 | bytes 8000000 | tf_op jit(solution)/shard_map/pallas_call | solution.py:223
  34.7 2.3 %shard_map.95 = (f32[1024,256]{1,0:T(8,128)S(1)}, bf16[1024,256]{1,0:T(8,128)(2,1)S(1)}, f32[512,256]{1,0:T(8,128)S(1)}, bf16[512,256]{1,0:T(8,128)(2,1)S(1)}) custom-call(s32[1]{0:T(128)} %bitcast.1.core_ref, bf16[2048,128]{1,0:T(8,128)(2,1)S(1)} %collective-permute-done.below, bf16[2048,128]{1,0:T(8,128)(2,1)S(1)} %collective-permute-done.1.above, ...), custom_call_target="tpu_custom_call" | custom-call | flops 1207959552 | bytes 8000000 | tf_op jit(solution)/shard_map/pallas_call | solution.py:223
  39.1 2.3 %shard_map.96 = (f32[2048,256]{1,0:T(8,128)S(1)}, bf16[256,2048]{1,0:T(8,128)(2,1)S(1)}, bf16[1152,2048]{1,0:T(8,128)(2,1)S(1)}) custom-call(bf16[2048,128]{1,0:T(8,128)(2,1)S(1)} %collective-permute-done.below, bf16[2048,128]{1,0:T(8,128)(2,1)S(1)} %all_gather.3.centre, bf16[2048,128]{1,0:T(8,128)(2,1)S(1)} %collective-permute-done.1.above, ...), custom_call_target="tpu_custom_call" | custom-call | flops 1207959552 | bytes 8000000 | tf_op jit(solution)/shard_map/pallas_call | solution.py:223
  41.4 3.7 %collective-permute-done.4.recv = bf16[512,256]{1,0:T(8,128)(2,1)S(1)} collective-permute-done((bf16[512,256]{1,0:T(8,128)(2,1)S(1)}, bf16[512,256]{1,0:T(8,128)(2,1)S(1)}, u32[]{:S(2)}, u32[]{:S(2)}) %collective-permute-start.4) | collective-permute-done | bytes 262176 | tf_op jit(solution)/shard_map/ppermute | solution.py:296
  45.4 5.3 %collective-permute-done.6.recv = bf16[512,256]{1,0:T(8,128)(2,1)S(1)} collective-permute-done((bf16[512,256]{1,0:T(8,128)(2,1)S(1)}, bf16[512,256]{1,0:T(8,128)(2,1)S(1)}, u32[]{:S(2)}, u32[]{:S(2)}) %collective-permute-start.6) | collective-permute-done | bytes 262176 | tf_op jit(solution)/shard_map/ppermute | solution.py:299
  53.7 7.6 %shard_map.99 = (bf16[3712,256]{1,0:T(8,128)(2,1)S(1)}, bf16[2176,256]{1,0:T(8,128)(2,1)S(1)}) custom-call(s32[1]{0:T(128)} %bitcast.1.core_ref, f32[1]{0:T(128)} %bitcast.10.keep_ref, bf16[512,256]{1,0:T(8,128)(2,1)S(1)} %get-tuple-element.78.own_a, bf16[512,256]{1,0:T(8,128)(2,1)S(1)} %get-tuple-element.79.own_b, ...), custom_call_target="tpu_custom_call" | custom-call | flops 3623878656 | bytes 8000000 | tf_op jit(solution)/shard_map/pallas_call | solution.py:223
  63.6 7.4 %all-to-all-start = ((bf16[16,232,256]{2,1,0:T(8,128)(2,1)}), bf16[16,232,256]{2,1,0:T(8,128)(2,1)S(1)}, u32[]{:S(2)}, u32[]{:S(2)}) async-start(bf16[16,232,256]{2,1,0:T(8,128)(2,1)} %bitcast.47), calls=%async_computation | async-start | bytes 3801088 | tf_op jit(solution)/shard_map/all_to_all | solution.py:344
  71.0 1.5 copy-done.1
  73.7 4.3 %shard_map.101 = (bf16[2048,128]{1,0:T(8,128)(2,1)S(1)}, f32[2048,128]{1,0:T(8,128)S(1)}, bf16[2048,128]{1,0:T(8,128)(2,1)S(1)}) custom-call(bf16[2176,256]{1,0:T(8,128)(2,1)S(1)} %copy-done.9, bf16[1152,768]{1,0:T(8,128)(2,1)S(1)} %bitcast.48), custom_call_target="tpu_custom_call" | custom-call | flops 3623878656 | bytes 8000000 | tf_op jit(solution)/shard_map/pallas_call | solution.py:223
  79.6 22.2 %all-to-all-done.parts = bf16[16,232,256]{2,1,0:T(8,128)(2,1)S(1)} async-done(((bf16[16,232,256]{2,1,0:T(8,128)(2,1)}), bf16[16,232,256]{2,1,0:T(8,128)(2,1)S(1)}, u32[]{:S(2)}, u32[]{:S(2)}) %all-to-all-start) | async-done | bytes 1900576 | tf_op jit(solution)/shard_map/all_to_all | solution.py:344
  102.9 10.5 %all-to-all-start.1 = ((bf16[4,232,256]{2,1,0:T(8,128)(2,1)}), bf16[4,232,256]{2,1,0:T(8,128)(2,1)S(1)}, u32[]{:S(2)}, u32[]{:S(2)}) async-start(bf16[4,232,256]{2,1,0:T(8,128)(2,1)} %shard_map.100), calls=%async_computation.1 | async-start | bytes 950272 | tf_op jit(solution)/shard_map/all_to_all | solution.py:367
  113.4 1.9 %collective-permute-start.9 = (bf16[2048,128]{1,0:T(8,128)(2,1)}, bf16[2048,128]{1,0:T(8,128)(2,1)S(1)}, u32[]{:S(2)}, u32[]{:S(2)}) collective-permute-start(bf16[2048,128]{1,0:T(8,128)(2,1)} %copy-done.5), channel_id=1, source_target_pairs={{5,1},{9,5},{10,2},{13,9},{14,6},{17,13},{18,10},{19,3},{21,17},{2... | collective-permute-start | bytes 1572872 | tf_op jit(solution)/shard_map/ppermute | solution.py:368
  115.3 5.8 %collective-permute-start.10 = (bf16[2048,128]{1,0:T(8,128)(2,1)}, bf16[2048,128]{1,0:T(8,128)(2,1)S(1)}, u32[]{:S(2)}, u32[]{:S(2)}) collective-permute-start(bf16[2048,128]{1,0:T(8,128)(2,1)} %copy-done.4), channel_id=1, source_target_pairs={{1,5},{2,10},{3,19},{5,9},{6,14},{7,23},{9,13},{10,18},{11,27},{13... | collective-permute-start | bytes 1572872 | tf_op jit(solution)/shard_map/ppermute | solution.py:369
  121.1 5.5 %all-to-all-done.1.parts = bf16[4,232,256]{2,1,0:T(8,128)(2,1)S(1)} async-done(((bf16[4,232,256]{2,1,0:T(8,128)(2,1)}), bf16[4,232,256]{2,1,0:T(8,128)(2,1)S(1)}, u32[]{:S(2)}, u32[]{:S(2)}) %all-to-all-start.1) | async-done | bytes 475168 | tf_op jit(solution)/shard_map/all_to_all | solution.py:367
  126.5 1.4 shard_map.102
  128.0 3.4 %collective-permute-done.9 = bf16[2048,128]{1,0:T(8,128)(2,1)S(1)} collective-permute-done((bf16[2048,128]{1,0:T(8,128)(2,1)}, bf16[2048,128]{1,0:T(8,128)(2,1)S(1)}, u32[]{:S(2)}, u32[]{:S(2)}) %collective-permute-start.9) | collective-permute-done | bytes 524320 | tf_op jit(solution)/shard_map/ppermute | solution.py:368
  131.4 7.4 %collective-permute-done.10 = bf16[2048,128]{1,0:T(8,128)(2,1)S(1)} collective-permute-done((bf16[2048,128]{1,0:T(8,128)(2,1)}, bf16[2048,128]{1,0:T(8,128)(2,1)S(1)}, u32[]{:S(2)}, u32[]{:S(2)}) %collective-permute-start.10) | collective-permute-done | bytes 524320 | tf_op jit(solution)/shard_map/ppermute | solution.py:369
  139.6 4.3 %all-to-all-start.2 = ((bf16[16,232,256]{2,1,0:T(8,128)(2,1)}), bf16[16,232,256]{2,1,0:T(8,128)(2,1)S(1)}, u32[]{:S(2)}, u32[]{:S(2)}) async-start(bf16[16,232,256]{2,1,0:T(8,128)(2,1)} %shard_map.102), calls=%async_computation.2 | async-start | bytes 3801088 | tf_op jit(solution)/shard_map/all_to_all | solution.py:372
  144.0 2.3 %convert_add_fusion = f32[2048,128]{1,0:T(8,128)} fusion(bf16[2048,128]{1,0:T(8,128)(2,1)} %copy-done.11, f32[2048,128]{1,0:T(8,128)S(1)} %get-tuple-element.92, bf16[2048,128]{1,0:T(8,128)(2,1)} %copy-done.10), kind=kLoop, calls=%fused_computation.4 | loop fusion | flops 1048576 | bytes 3145728 | tf_op jit(solution)/shard_map/add | solution.py:374
  147.5 1.5 collective-permute-done.11
  150.9 14.0 %collective-permute-done.12 = bf16[512,128]{1,0:T(8,128)(2,1)S(1)} collective-permute-done((bf16[512,128]{1,0:T(8,128)(2,1)S(1)}, bf16[512,128]{1,0:T(8,128)(2,1)S(1)}, u32[]{:S(2)}, u32[]{:S(2)}) %collective-permute-start.12) | collective-permute-done | bytes 131104 | tf_op jit(solution)/shard_map/ppermute | solution.py:380
  165.6 14.7 %all-to-all-done.2 = bf16[16,232,256]{2,1,0:T(8,128)(2,1)S(1)} async-done(((bf16[16,232,256]{2,1,0:T(8,128)(2,1)}), bf16[16,232,256]{2,1,0:T(8,128)(2,1)S(1)}, u32[]{:S(2)}, u32[]{:S(2)}) %all-to-all-start.2) | async-done | bytes 1900576 | tf_op jit(solution)/shard_map/all_to_all | solution.py:372
  180.3 2.0 %shard_map.103 = (f32[3456,256]{1,0:T(8,128)}, f32[256,256]{1,0:T(8,128)}) custom-call(bf16[3712,256]{1,0:T(8,128)(2,1)S(1)} %bitcast.46), custom_call_target="tpu_custom_call" | custom-call | flops 1000000 | bytes 8000000 | tf_op jit(solution)/shard_map/pallas_call | solution.py:223
  (56 shorter events, 19.4 us)
Async XLA Ops:
  8.1 23.9 %collective-permute-start = (bf16[2048,128]{1,0:T(8,128)(2,1)S(1)}, bf16[2048,128]{1,0:T(8,128)(2,1)S(1)}, u32[]{:S(2)}, u32[]{:S(2)}) collective-permute-start(bf16[2048,128]{1,0:T(8,128)(2,1)S(1)} %all_gather.3.centre), channel_id=1, source_target_pairs={{1,5},{2,10},{3,19},{5,9},{6,14},{7,23},{9,13},{10,18},{11,27},{13... | collective-permute-start | bytes 1572872 | tf_op jit(solution)/shard_map/ppermute | solution.py:262
  12.5 19.5 %collective-permute-start.1 = (bf16[2048,128]{1,0:T(8,128)(2,1)S(1)}, bf16[2048,128]{1,0:T(8,128)(2,1)S(1)}, u32[]{:S(2)}, u32[]{:S(2)}) collective-permute-start(bf16[2048,128]{1,0:T(8,128)(2,1)S(1)} %all_gather.3.centre), channel_id=1, source_target_pairs={{5,1},{9,5},{10,2},{13,9},{14,6},{17,13},{18,10},{19,3},{21,17},{2... | collective-permute-start | bytes 1572872 | tf_op jit(solution)/shard_map/ppermute | solution.py:263
  15.0 16.1 %collective-permute-start.2 = (bf16[512,256]{1,0:T(8,128)(2,1)}, bf16[512,256]{1,0:T(8,128)(2,1)S(1)}, u32[]{:S(2)}, u32[]{:S(2)}) collective-permute-start(bf16[512,256]{1,0:T(8,128)(2,1)} %bitcast.49), channel_id=1, source_target_pairs={{0,2},{2,0},{1,3},{3,1},{4,6},{6,4},{5,7},{7,5},{8,10},{10,8},{9,1... | collective-permute-start | bytes 786440 | tf_op jit(solution)/shard_map/ppermute | solution.py:264
  21.9 1.7 copy-start.7
  25.4 6.6 %copy-start.6 = (bf16[1,256,256]{2,1,0:T(8,128)(2,1)S(1)}, bf16[1,256,256]{2,1,0:T(8,128)(2,1)}, u32[]{:S(2)}) copy-start(bf16[1,256,256]{2,1,0:T(8,128)(2,1)} %param.9) | copy-start | bytes 393220
  34.4 2.7 %collective-permute-start.3 = (bf16[512,256]{1,0:T(8,128)(2,1)S(1)}, bf16[512,256]{1,0:T(8,128)(2,1)S(1)}, u32[]{:S(2)}, u32[]{:S(2)}) collective-permute-start(bf16[512,256]{1,0:T(8,128)(2,1)S(1)} %get-tuple-element.58), channel_id=1, source_target_pairs={{0,1},{1,0},{2,3},{3,2},{4,5},{5,4},{6,7},{7,6},{8,9},{9,8},{10,11... | collective-permute-start | bytes 786440 | tf_op jit(solution)/shard_map/ppermute | solution.py:293
  37.1 1.6 collective-permute-start.5
  37.5 7.6 %collective-permute-start.4 = (bf16[512,256]{1,0:T(8,128)(2,1)S(1)}, bf16[512,256]{1,0:T(8,128)(2,1)S(1)}, u32[]{:S(2)}, u32[]{:S(2)}) collective-permute-start(bf16[512,256]{1,0:T(8,128)(2,1)S(1)} %get-tuple-element.60), channel_id=1, source_target_pairs={{0,2},{2,0},{1,3},{3,1},{4,6},{6,4},{5,7},{7,5},{8,10},{10,8},{9,1... | collective-permute-start | bytes 786440 | tf_op jit(solution)/shard_map/ppermute | solution.py:296
  38.8 11.9 %collective-permute-start.6 = (bf16[512,256]{1,0:T(8,128)(2,1)S(1)}, bf16[512,256]{1,0:T(8,128)(2,1)S(1)}, u32[]{:S(2)}, u32[]{:S(2)}) collective-permute-start(bf16[512,256]{1,0:T(8,128)(2,1)S(1)} %get-tuple-element.75), channel_id=1, source_target_pairs={{0,2},{2,0},{1,3},{3,1},{4,6},{6,4},{5,7},{7,5},{8,10},{10,8},{9,1... | collective-permute-start | bytes 786440 | tf_op jit(solution)/shard_map/ppermute | solution.py:299
  39.1 6.0 %copy-start.2 = (bf16[8,4,16,256]{3,2,1,0:T(8,128)(2,1)S(1)}, bf16[8,4,16,256]{3,2,1,0:T(8,128)(2,1)}, u32[]{:S(2)}) copy-start(bf16[8,4,16,256]{3,2,1,0:T(8,128)(2,1)} %param.11) | copy-start | bytes 786436
  39.1 6.0 %copy-start.3 = (f32[256]{0:T(256)S(1)}, f32[256]{0:T(256)}, u32[]{:S(2)}) copy-start(f32[256]{0:T(256)} %param.10) | copy-start | bytes 3076
  50.7 2.3 %collective-permute-start.7 = (bf16[512,256]{1,0:T(8,128)(2,1)S(1)}, bf16[512,256]{1,0:T(8,128)(2,1)S(1)}, u32[]{:S(2)}, u32[]{:S(2)}) collective-permute-start(bf16[512,256]{1,0:T(8,128)(2,1)S(1)} %get-tuple-element.78.own_a), channel_id=1, source_target_pairs={{0,1},{1,0},{2,3},{3,2},{4,5},{5,4},{6,7},{7,6},{8,9},{9,8},{10,11... | collective-permute-start | bytes 786440 | tf_op jit(solution)/shard_map/ppermute | solution.py:322
  52.1 1.6 collective-permute-start.8
  61.4 1.3 copy-start
  62.6 1.0 copy-start.8
  63.6 38.3 %all-to-all-start = ((bf16[16,232,256]{2,1,0:T(8,128)(2,1)}), bf16[16,232,256]{2,1,0:T(8,128)(2,1)S(1)}, u32[]{:S(2)}, u32[]{:S(2)}) async-start(bf16[16,232,256]{2,1,0:T(8,128)(2,1)} %bitcast.47), calls=%async_computation | async-start | bytes 3801088 | tf_op jit(solution)/shard_map/all_to_all | solution.py:344
  71.0 1.5 copy-start.1
  72.5 1.2 copy-start.9
  78.0 0.8 copy-start.4
  78.8 0.8 copy-start.5
  102.9 23.6 %all-to-all-start.1 = ((bf16[4,232,256]{2,1,0:T(8,128)(2,1)}), bf16[4,232,256]{2,1,0:T(8,128)(2,1)S(1)}, u32[]{:S(2)}, u32[]{:S(2)}) async-start(bf16[4,232,256]{2,1,0:T(8,128)(2,1)} %shard_map.100), calls=%async_computation.1 | async-start | bytes 950272 | tf_op jit(solution)/shard_map/all_to_all | solution.py:367
  113.4 18.0 %collective-permute-start.9 = (bf16[2048,128]{1,0:T(8,128)(2,1)}, bf16[2048,128]{1,0:T(8,128)(2,1)S(1)}, u32[]{:S(2)}, u32[]{:S(2)}) collective-permute-start(bf16[2048,128]{1,0:T(8,128)(2,1)} %copy-done.5), channel_id=1, source_target_pairs={{5,1},{9,5},{10,2},{13,9},{14,6},{17,13},{18,10},{19,3},{21,17},{2... | collective-permute-start | bytes 1572872 | tf_op jit(solution)/shard_map/ppermute | solution.py:368
  115.3 23.5 %collective-permute-start.10 = (bf16[2048,128]{1,0:T(8,128)(2,1)}, bf16[2048,128]{1,0:T(8,128)(2,1)S(1)}, u32[]{:S(2)}, u32[]{:S(2)}) collective-permute-start(bf16[2048,128]{1,0:T(8,128)(2,1)} %copy-done.4), channel_id=1, source_target_pairs={{1,5},{2,10},{3,19},{5,9},{6,14},{7,23},{9,13},{10,18},{11,27},{13... | collective-permute-start | bytes 1572872 | tf_op jit(solution)/shard_map/ppermute | solution.py:369
  131.4 7.4 %copy-start.10 = (bf16[2048,128]{1,0:T(8,128)(2,1)}, bf16[2048,128]{1,0:T(8,128)(2,1)S(1)}, u32[]{:S(2)}) copy-start(bf16[2048,128]{1,0:T(8,128)(2,1)S(1)} %collective-permute-done.9) | copy-start | bytes 1572868
  138.8 0.8 copy-start.11
  139.6 40.7 %all-to-all-start.2 = ((bf16[16,232,256]{2,1,0:T(8,128)(2,1)}), bf16[16,232,256]{2,1,0:T(8,128)(2,1)S(1)}, u32[]{:S(2)}, u32[]{:S(2)}) async-start(bf16[16,232,256]{2,1,0:T(8,128)(2,1)} %shard_map.102), calls=%async_computation.2 | async-start | bytes 3801088 | tf_op jit(solution)/shard_map/all_to_all | solution.py:372
  147.4 1.6 collective-permute-start.11
  150.1 14.8 %collective-permute-start.12 = (bf16[512,128]{1,0:T(8,128)(2,1)S(1)}, bf16[512,128]{1,0:T(8,128)(2,1)S(1)}, u32[]{:S(2)}, u32[]{:S(2)}) collective-permute-start(bf16[512,128]{1,0:T(8,128)(2,1)S(1)} %fusion.4), channel_id=1, source_target_pairs={{0,2},{2,0},{1,3},{3,1},{4,6},{6,4},{5,7},{7,5},{8,10},{10,8},{9,1... | collective-permute-start | bytes 393224 | tf_op jit(solution)/shard_map/ppermute | solution.py:380

commit v4 on v3

--- a/solution.py
+++ b/solution.py
@@ -1,4 +1,5 @@
 import functools
+import math
 
 import jax
 import jax.numpy as jnp
@@ -13,6 +14,7 @@
 COL = 64
 ROWS = 2048
 HALF = 1024
+EARLY = 14 * COL
 QUART = 512
 TAPS = 27 * C
 GRAD_ROWS = TAPS + F
@@ -20,6 +22,7 @@
 f32 = jnp.float32
 GZ = ("zh", "zl", "x", "yh")
 NEAR = ("zl", "x", "yh")
+FAR = "zh"
 BR = ("yl", "c")
 SWAP = [(0, 1), (1, 0)]
 VMEM = pl.BlockSpec(memory_space=pltpu.VMEM)
@@ -129,38 +132,73 @@
     own[...] = (cot.astype(f32) * silu_slope(summed)).astype(bf16)
 
 
-def gradient_kernel(
-    core_ref, keep_ref, own_a, own_b, other_a, other_b, slope, proj, features_t, hidden_t,
-    grads_out, d_pre_out, grads, d_pre, window, d_out, sems,
+def height_sum(parts):
+    return parts[:, 3 * C : 6 * C] + from_above(parts[:, : 3 * C]) + from_below(parts[:, 6 * C :])
+
+
+def back_rows(core_ref, own, other, slope, proj, d_pre, at, d_out):
+    for side in range(2):
+        cells = slice(side * QUART, (side + 1) * QUART)
+        rows = jnp.where(core_ref[0] == side, own[...], other[...])
+        d_out[cells] = rows
+        d_hidden = matmul_rt(rows, proj[...])
+        d_pre[at + side * QUART : at + (side + 1) * QUART] = (d_hidden * slope[cells]).astype(bf16)
+
+
+def back_features(d_pre, weights, start, count):
+    window = jnp.concatenate(
+        [d_pre[start + (2 - i) * COL : start + (2 - i) * COL + count] for i in range(3)], axis=1
+    )
+    return height_sum(matmul_rt(window, weights[...]))
+
+
+def back_first_kernel(
+    core_ref, own, other_0, other_1, slope, proj, weights, features_t, hidden_t,
+    d_pre, low, mid, high, taps, projs, window, d_out, other,
 ):
     d_pre[0:COL] = jnp.zeros((COL, F), bf16)
-    d_pre[COL + ROWS : 2 * COL + ROWS] = jnp.zeros((COL, F), bf16)
-    for q in range(4):
-        start = q * QUART
-        own, other = ((own_a, other_a), (own_b, other_b))[q // 2]
-        rows = jnp.where(core_ref[0] == q % 2, own[...], other[...])
-        d_out[start : start + QUART] = rows
-        d_hidden = matmul_rt(rows, proj[...])
-        d_pre[COL + start : COL + start + QUART] = (d_hidden * slope[start : start + QUART]).astype(bf16)
-    copies = [pltpu.make_async_copy(d_pre, d_pre_out, sems.at[4])]
-    copies[0].start()
+    other[: QUART // 2] = other_0[...]
+    other[QUART // 2 :] = other_1[...]
+    back_rows(core_ref, own, other, slope, proj, d_pre, COL, d_out)
+    for k in range(2):
+        step = EARLY // 2
+        total = back_features(d_pre, weights, k * step, step)
+        cells = slice(k * step, (k + 1) * step)
+        low[cells] = total[:, :C].astype(bf16)
+        mid[cells] = total[:, C : 2 * C]
+        high[cells] = total[:, 2 * C :].astype(bf16)
     for i in range(3):
-        window[:, i * F : (i + 1) * F] = d_pre[(2 - i) * COL : (2 - i) * COL + ROWS]
-    grads[TAPS:] = matmul(hidden_t[...], d_out[...]).astype(bf16)
-    spans = [(TAPS, F)] + [(t * 9 * C, 9 * C) for t in range(3)]
-
-    def send_span(k):
-        first, count = spans[k]
-        copy = pltpu.make_async_copy(
-            grads.at[first : first + count], grads_out.at[first : first + count], sems.at[k]
-        )
-        copy.start()
-        copies.append(copy)
-
-    send_span(0)
+        window[:, i * F : (i + 1) * F] = d_pre[(2 - i) * COL : (2 - i) * COL + EARLY]
+    for t in range(3):
+        rows = slice(t * 3 * C, (t + 1) * 3 * C)
+        taps[rows] = matmul(features_t[rows, :EARLY], window[...])
+    projs[...] = matmul(hidden_t[:, :HALF], d_out[...])
+
+
+def back_second_kernel(
+    core_ref, keep_ref, own, other, slope, proj, weights, features_t, hidden_t,
+    d_pre_a, low_a, mid_a, high_a, taps, projs, low, mid, high, grads, d_pre, window, d_out,
+):
+    d_pre[0 : 3 * COL] = d_pre_a[HALF - 2 * COL :]
+    d_pre[3 * COL + HALF :] = jnp.zeros((COL, F), bf16)
+    back_rows(core_ref, own, other, slope.at[HALF:], proj, d_pre, 3 * COL, d_out)
+    low[:EARLY] = low_a[...]
+    mid[:EARLY] = mid_a[...]
+    high[:EARLY] = high_a[...]
+    late = ROWS - EARLY
+    for k in range(3):
+        step = late // 3
+        total = back_features(d_pre, weights, k * step, step)
+        cells = slice(EARLY + k * step, EARLY + (k + 1) * step)
+        low[cells] = total[:, :C].astype(bf16)
+        mid[cells] = total[:, C : 2 * C]
+        high[cells] = total[:, 2 * C :].astype(bf16)
+    for i in range(3):
+        window[:, i * F : (i + 1) * F] = d_pre[(2 - i) * COL : (2 - i) * COL + late]
     off_centre = keep_ref[0]
     for t in range(3):
-        block = matmul(features_t[t * 3 * C : (t + 1) * 3 * C], window[...])
+        rows = slice(t * 3 * C, (t + 1) * 3 * C)
+        block = taps[rows] + matmul(features_t[rows, EARLY:], window[...])
         for i in range(3):
             for j in range(3):
                 tap = (t * 9 + i * 3 + j) * C
@@ -168,23 +206,28 @@
                 if (t, i, j) != (1, 1, 1):
                     piece = piece * off_centre
                 grads[tap : tap + C] = piece.astype(bf16)
-        send_span(t + 1)
-    for copy in copies:
-        copy.wait()
-
-
-def feature_kernel(d_pre, weights, low, mid, high):
+    grads[TAPS:] = (projs[...] + matmul(hidden_t[:, HALF:], d_out[...])).astype(bf16)
+
+
+def core_split_kernel(core_ref, low, mid, high, kept, sent):
+    core = core_ref[0]
     for q in range(4):
-        start = q * QUART
-        window = jnp.concatenate(
-            [d_pre[start + (2 - i) * COL : start + (2 - i) * COL + QUART] for i in range(3)], axis=1
-        )
-        parts = matmul_rt(window, weights[...])
-        total = parts[:, 3 * C : 6 * C] + from_above(parts[:, : 3 * C]) + from_below(parts[:, 6 * C :])
-        cells = slice(start, start + QUART)
-        low[cells] = total[:, :C].astype(bf16)
-        mid[cells] = total[:, C : 2 * C]
-        high[cells] = total[:, 2 * C :].astype(bf16)
+        cells = slice(q * QUART, (q + 1) * QUART)
+        total = mid[cells] + low[cells].astype(f32) + high[cells].astype(f32)
+
+        @pl.when(core == q % 2)
+        def _():
+            kept[q // 2] = total
+
+        @pl.when(core != q % 2)
+        def _():
+            sent[q // 2] = total.astype(bf16)
+
+
+def chip_split_kernel(row_ref, kept, recv, mine, sent):
+    row = row_ref[0]
+    mine[...] = kept[row] + recv[row].astype(f32)
+    sent[...] = (kept[1 - row] + recv[1 - row].astype(f32)).astype(bf16)
 
 
 def sum_of(parts):
@@ -227,7 +270,7 @@
         out_specs=[place] * len(outs),
         scratch_shapes=scratch,
         compiler_params=pltpu.CompilerParams(vmem_limit_bytes=12 * 1024 * 1024),
-        cost_estimate=pl.CostEstimate(flops=flops, bytes_accessed=8_000_000, transcendentals=0),
+        cost_estimate=pl.CostEstimate(flops=flops, bytes_accessed=flops // 1000, transcendentals=0),
     )(*args)
 
 
@@ -302,7 +345,7 @@
         [((ROWS, F), f32), ((F, ROWS), bf16), ((9 * C, ROWS), bf16)],
         [VMEM] * 7,
         [],
-        2 * ROWS * 9 * C * F,
+        1000,
         below, centre, above, preact_a, preact_b, hidden_a, hidden_b,
     )
     recv_a, slope, hidden_t, features_t = lax.optimization_barrier((recv_a, slope, hidden_t, features_t))
@@ -313,43 +356,50 @@
             [((QUART, F), bf16), ((QUART, F), bf16)],
             [SMEM] + [VMEM] * 5,
             [],
-            1_000_000,
+            1000,
             row_arg, chip_sum, recv, out_bias[None], cot_mine, cot_pair,
         )
 
     own_a, head_a = output_half(0, chip_a, recv_a)
-    own_a, recv_b = lax.optimization_barrier((own_a, recv_b))
-    other_a = lax.ppermute(own_a, "c", SWAP)
+    other_a = [lax.ppermute(own_a[k : k + QUART // 2], "c", SWAP) for k in (0, QUART // 2)]
+    d_pre_a, low_a, mid_a, high_a, taps_a, projs_a = call(
+        back_first_kernel,
+        [
+            ((HALF + COL, F), bf16),
+            ((EARLY, C), bf16),
+            ((EARLY, C), f32),
+            ((EARLY, C), bf16),
+            ((9 * C, 3 * F), f32),
+            ((F, F), f32),
+        ],
+        [SMEM] + [VMEM] * 8,
+        [pltpu.VMEM((EARLY, 3 * F), bf16), pltpu.VMEM((HALF, F), bf16), pltpu.VMEM((QUART, F), bf16)],
+        1000,
+        core_arg, own_a, *other_a, slope, proj, weights_bwd, features_t, hidden_t,
+    )
+    recv_b, taps_a, d_pre_a = lax.optimization_barrier((recv_b, taps_a, d_pre_a))
     own_b, head_b = output_half(1, chip_b, recv_b)
     other_b = lax.ppermute(own_b, "c", SWAP)
-
-    grads, d_pre = call(
-        gradient_kernel,
-        [((GRAD_ROWS, F), bf16), ((ROWS + 2 * COL, F), bf16)],
-        [SMEM, SMEM] + [VMEM] * 8,
+    low, mid, high, grads = call(
+        back_second_kernel,
+        [((ROWS, C), bf16), ((ROWS, C), f32), ((ROWS, C), bf16), ((GRAD_ROWS, F), bf16)],
+        [SMEM, SMEM] + [VMEM] * 13,
         [
-            pltpu.VMEM((GRAD_ROWS, F), bf16),
-            pltpu.VMEM((ROWS + 2 * COL, F), bf16),
-            pltpu.VMEM((ROWS, 3 * F), bf16),
-            pltpu.VMEM((ROWS, F), bf16),
-            pltpu.SemaphoreType.DMA((5,)),
+            pltpu.VMEM((HALF + 4 * COL, F), bf16),
+            pltpu.VMEM((ROWS - EARLY, 3 * F), bf16),
+            pltpu.VMEM((HALF, F), bf16),
         ],
         2 * ROWS * 27 * C * F,
-        core_arg, off_centre[None], own_a, own_b, other_a, other_b, slope, proj, features_t, hidden_t,
-        place=HBM,
-    )
-    near = lax.axis_size("zl") * lax.axis_size("x") * lax.axis_size("yh")
-    far = lax.axis_size("zh")
+        core_arg, off_centre[None], own_b, other_b, slope, proj, weights_bwd, features_t, hidden_t,
+        d_pre_a, low_a, mid_a, high_a, taps_a, projs_a,
+    )
+    head_out = jnp.where(row == 0, head_a, head_b)
+    near = math.prod(lax.axis_size(a) for a in NEAR)
+    far = lax.axis_size(FAR)
     share = GRAD_ROWS // near
+    grads, low, mid, high = lax.optimization_barrier((grads, low, mid, high))
     part = lax.all_to_all(grads.reshape(near, share, F), NEAR, 0, 0, tiled=True)
-    low, mid, high = call(
-        feature_kernel,
-        [((ROWS, C), bf16), ((ROWS, C), f32), ((ROWS, C), bf16)],
-        [VMEM] * 2,
-        [],
-        2 * ROWS * 27 * C * F,
-        d_pre, weights_bwd,
-    )
+    part, low, mid, high = lax.optimization_barrier((part, low, mid, high))
 
     def sum_for(peers, parts):
         return call(
@@ -364,21 +414,30 @@
 
     part = sum_for(far, part)
     part, low, high = lax.optimization_barrier((part, low, high))
-    part = lax.all_to_all(part, "zh", 0, 0, tiled=True)
     from_low = lax.ppermute(low, everywhere, down)
     from_high = lax.ppermute(high, everywhere, up)
+    part = lax.all_to_all(part, FAR, 0, 0, tiled=True)
     part = sum_for(near, part)
-    part, mid, from_low, from_high = lax.optimization_barrier((part, mid, from_low, from_high))
+
+    kept, sent = call(
+        core_split_kernel,
+        [((2, QUART, C), f32), ((2, QUART, C), bf16)],
+        [SMEM] + [VMEM] * 3,
+        [],
+        1_000_000,
+        core_arg, from_low, mid, from_high,
+    )
+    mine, sent = call(
+        chip_split_kernel,
+        [((QUART, C), f32), ((QUART, C), bf16)],
+        [SMEM] + [VMEM] * 2,
+        [],
+        1_000_000,
+        row_arg, kept, lax.ppermute(sent, "c", SWAP),
+    )
+    feature_grad = (mine + lax.ppermute(sent, "yl", SWAP).astype(f32)).astype(bf16)
+    part, feature_grad, head_out = lax.optimization_barrier((part, feature_grad, head_out))
     total = lax.all_to_all(part, NEAR, 0, 0, tiled=True).reshape(GRAD_ROWS, F)
-
-    branch_grad = (mid + from_low.astype(f32) + from_high.astype(f32)).reshape(2, 2, QUART, C)
-    sent = lax.dynamic_index_in_dim(branch_grad, 1 - core, 1, keepdims=False).astype(bf16)
-    kept = lax.dynamic_index_in_dim(branch_grad, core, 1, keepdims=False)
-    chip_grad = kept + lax.ppermute(sent, "c", SWAP).astype(f32)
-    sent = lax.dynamic_index_in_dim(chip_grad, 1 - row, 0, keepdims=False).astype(bf16)
-    kept = lax.dynamic_index_in_dim(chip_grad, row, 0, keepdims=False)
-    feature_grad = (kept + lax.ppermute(sent, "yl", SWAP).astype(f32)).astype(bf16)
-    head_out = jnp.where(row == 0, head_a, head_b)
 
     taps, proj_total = call(
         widen_kernel,

time: 183 us -> 166 us (0.907)
  the two profiles are of different devices: /device:TPU:15 before, /device:TPU:64 now
where the time goes in v4:
time: 166 us
  blocking collectives  77 us (46%)
  starting transfers between devices  44.1 us (27%)
  Pallas kernels  26.3 us (16%)
  waiting for transfers between devices  9.75 us (6%)
  local copies, waits for them, and re-layouts  3.99 us (2%)
  other arithmetic  3.42 us (2%)
    all_to_all x1, blocking collectives, shards(): part = lax.all_to_all(grads.reshape(near, share, F), NEAR, 0, 0, tiled=True)  36.1 us
    all_to_all x1, blocking collectives, shards(): total = lax.all_to_all(part, NEAR, 0, 0, tiled=True).reshape(GRAD_ROWS, F)  33.5 us
    pallas_call x13, Pallas kernels, call(): pl.pallas_call(kernel, out_shape=[jax.ShapeDtypeStruct(*o) for o in outs]...  26.3 us
    ppermute x1, starting transfers between devices, shards(): lax.ppermute(sent, 'c', SWAP)  11.1 us
    all_gather x1, blocking collectives, shards(): centre = lax.all_gather(features.reshape(QUART, C), BR, axis=0, tiled=True)  7.47 us
    ppermute x1, starting transfers between devices, shards(): lax.ppermute(sent, 'yl', SWAP).astype(f32)  6.87 us
    all_to_all x1, starting transfers between devices, shards(): part = lax.all_to_all(part, FAR, 0, 0, tiled=True)  6.57 us
    ppermute x1, starting transfers between devices, shards(): cot_pair = lax.ppermute(cot_mine, 'yl', SWAP)  5.93 us
  transfers between devices with their start and end apart: 15, of which 7 were waited for; matrix products, arithmetic and copies ran while one was open for 4% of the time, Pallas kernels for 9%

profile of v4, /device:TPU:64, one launch (start us, length us, event | category | flops | bytes accessed | tf_op | source)
XLA Modules:
  0.0 165.6 jit_solution(2099302195898202590)
XLA Ops:
  0.6 7.5 %all_gather.3.centre = bf16[2048,128]{1,0:T(8,128)(2,1)S(1)} all-gather(bf16[512,128]{1,0:T(8,128)(2,1)} %bitcast.56), channel_id=1, replica_groups=mesh['zh'=4,'zl'=2,'x'=4,'yh'=2,'yl'=2,'c'=2] {'yl','c'}, dimensions={0}, use_global_device_ids=true | all-gather | bytes 655360 | tf_op jit(solution)/shard_map/all_gather | solution.py:299
  8.8 0.7 collective-permute-start
  9.5 5.9 %collective-permute-start.2 = (bf16[512,256]{1,0:T(8,128)(2,1)}, bf16[512,256]{1,0:T(8,128)(2,1)S(1)}, u32[]{:S(2)}, u32[]{:S(2)}) collective-permute-start(bf16[512,256]{1,0:T(8,128)(2,1)} %bitcast.39), channel_id=1, source_target_pairs={{0,2},{2,0},{1,3},{3,1},{4,6},{6,4},{5,7},{7,5},{8,10},{10,8},{9,1... | collective-permute-start | bytes 786440 | tf_op jit(solution)/shard_map/ppermute | solution.py:307
  15.4 1.8 %fusion = (bf16[3,3,128,3,256]{4,2,0,3,1:T(8,128)(2,1)S(1)}, bf16[3,3,128,3,256]{4,2,3,1,0:T(8,128)(2,1)S(1)}) fusion(bf16[1,3,3,3,128,256]{5,4,3,2,1,0:T(8,128)(2,1)} %param.7, bf16[3,3,3]{2,1,0:T(4,128)(2,1)S(1)} %select_convert_fusion), kind=kLoop, calls=%fused_computation.1 | loop fusion | flops 884736 | bytes 5308470 | tf_op jit(solution)/shard_map/transpose | solution.py:312
  17.3 1.5 copy.17
  21.2 1.8 %shard_map.93.base = f32[2048,256]{1,0:T(8,128)S(1)} custom-call(bf16[2048,128]{1,0:T(8,128)(2,1)S(1)} %all_gather.3.centre, bf16[384,768]{1,0:T(8,128)(2,1)S(1)} %bitcast.42, f32[1,256]{1,0:T(1,128)S(1)} %copy-done.4), custom_call_target="tpu_custom_call" | custom-call | flops 1207959552 | bytes 1207959 | tf_op jit(solution)/shard_map/pallas_call | solution.py:266
  23.2 2.4 %collective-permute-done.2.cot_pair = bf16[512,256]{1,0:T(8,128)(2,1)S(1)} collective-permute-done((bf16[512,256]{1,0:T(8,128)(2,1)}, bf16[512,256]{1,0:T(8,128)(2,1)S(1)}, u32[]{:S(2)}, u32[]{:S(2)}) %collective-permute-start.2) | collective-permute-done | bytes 262176 | tf_op jit(solution)/shard_map/ppermute | solution.py:307
  25.6 2.4 %shard_map.95 = (f32[1024,256]{1,0:T(8,128)S(1)}, bf16[1024,256]{1,0:T(8,128)(2,1)S(1)}, f32[512,256]{1,0:T(8,128)S(1)}, bf16[512,256]{1,0:T(8,128)(2,1)S(1)}) custom-call(s32[1]{0:T(128)} %bitcast.core_ref, bf16[2048,128]{1,0:T(8,128)(2,1)S(1)} %collective-permute-done.below, bf16[2048,128]{1,0:T(8,128)(2,1)S(1)} %collective-permute-done.1.above, ...), custom_call_target="tpu_custom_call" | custom-call | flops 1207959552 | bytes 1207959 | tf_op jit(solution)/shard_map/pallas_call | solution.py:266
  27.9 5.8 %collective-permute-start.3 = (bf16[512,256]{1,0:T(8,128)(2,1)S(1)}, bf16[512,256]{1,0:T(8,128)(2,1)S(1)}, u32[]{:S(2)}, u32[]{:S(2)}) collective-permute-start(bf16[512,256]{1,0:T(8,128)(2,1)S(1)} %get-tuple-element.76), channel_id=1, source_target_pairs={{0,1},{1,0},{2,3},{3,2},{4,5},{5,4},{6,7},{7,6},{8,9},{9,8},{10,11... | collective-permute-start | bytes 786440 | tf_op jit(solution)/shard_map/ppermute | solution.py:336
  33.8 2.3 %shard_map.94 = (f32[1024,256]{1,0:T(8,128)S(1)}, bf16[1024,256]{1,0:T(8,128)(2,1)S(1)}, f32[512,256]{1,0:T(8,128)S(1)}, bf16[512,256]{1,0:T(8,128)(2,1)S(1)}) custom-call(s32[1]{0:T(128)} %bitcast.core_ref, bf16[2048,128]{1,0:T(8,128)(2,1)S(1)} %collective-permute-done.below, bf16[2048,128]{1,0:T(8,128)(2,1)S(1)} %collective-permute-done.1.above, ...), custom_call_target="tpu_custom_call" | custom-call | flops 1207959552 | bytes 1207959 | tf_op jit(solution)/shard_map/pallas_call | solution.py:266
  36.3 2.3 %collective-permute-start.6 = (bf16[512,256]{1,0:T(8,128)(2,1)S(1)}, bf16[512,256]{1,0:T(8,128)(2,1)S(1)}, u32[]{:S(2)}, u32[]{:S(2)}) collective-permute-start(bf16[512,256]{1,0:T(8,128)(2,1)S(1)} %get-tuple-element.81), channel_id=1, source_target_pairs={{0,2},{2,0},{1,3},{3,1},{4,6},{6,4},{5,7},{7,5},{8,10},{10,8},{9,1... | collective-permute-start | bytes 786440 | tf_op jit(solution)/shard_map/ppermute | solution.py:339
  38.7 1.3 collective-permute-start.5
  40.1 2.3 %shard_map.96 = (f32[2048,256]{1,0:T(8,128)S(1)}, bf16[256,2048]{1,0:T(8,128)(2,1)S(1)}, bf16[1152,2048]{1,0:T(8,128)(2,1)S(1)}) custom-call(bf16[2048,128]{1,0:T(8,128)(2,1)S(1)} %collective-permute-done.below, bf16[2048,128]{1,0:T(8,128)(2,1)S(1)} %all_gather.3.centre, bf16[2048,128]{1,0:T(8,128)(2,1)S(1)} %collective-permute-done.1.above, ...), custom_call_target="tpu_custom_call" | custom-call | flops 1000 | bytes 1 | tf_op jit(solution)/shard_map/pallas_call | solution.py:266
  42.4 3.4 %collective-permute-done.6.recv = bf16[512,256]{1,0:T(8,128)(2,1)S(1)} collective-permute-done((bf16[512,256]{1,0:T(8,128)(2,1)S(1)}, bf16[512,256]{1,0:T(8,128)(2,1)S(1)}, u32[]{:S(2)}, u32[]{:S(2)}) %collective-permute-start.6) | collective-permute-done | bytes 262176 | tf_op jit(solution)/shard_map/ppermute | solution.py:339
  46.7 0.8 collective-permute-done.8.other_1
  47.7 4.3 %shard_map.98 = (bf16[1088,256]{1,0:T(8,128)(2,1)S(1)}, bf16[896,128]{1,0:T(8,128)(2,1)S(1)}, f32[896,128]{1,0:T(8,128)S(1)}, bf16[896,128]{1,0:T(8,128)(2,1)S(1...) custom-call(s32[1]{0:T(128)} %bitcast.core_ref, bf16[512,256]{1,0:T(8,128)(2,1)S(1)} %get-tuple-element.91.own, ...), custom_call_target="tpu_custom_call" | custom-call | flops 1000 | bytes 1 | tf_op jit(solution)/shard_map/pallas_call | solution.py:266
  52.9 1.2 collective-permute-done.9.other
  54.1 6.0 %shard_map.100 = (bf16[2048,128]{1,0:T(8,128)(2,1)}, f32[2048,128]{1,0:T(8,128)S(1)}, bf16[2048,128]{1,0:T(8,128)(2,1)S(1)}, bf16[3712,256]{1,0:T(8,128)(2,1)S(1)}) custom-call(s32[1]{0:T(128)} %bitcast.core_ref, f32[1]{0:T(128)} %bitcast.1.keep_ref, bf16[512,256]{1,0:T(8,128)(2,1)S(1)} %get-tuple-element.99.own, ...), custom_call_target="tpu_custom_call" | custom-call | flops 3623878656 | bytes 3623878 | tf_op jit(solution)/shard_map/pallas_call | solution.py:266
  60.1 36.1 %all_to_all.15.parts = bf16[16,232,256]{2,1,0:T(8,128)(2,1)S(1)} all-to-all(bf16[16,232,256]{2,1,0:T(8,128)(2,1)S(1)} %bitcast.38), channel_id=1, replica_groups=mesh['zh'=4,'zl'=2,'x'=4,'yh'=2,'yl'=2,'c'=2] {'zl','x','yh'}, dimensions={0} | all-to-all | bytes 3801088 | tf_op jit(solution)/shard_map/all_to_all | solution.py:401
  96.2 1.1 shard_map.101
  97.3 0.7 collective-permute-start.10
  98.0 0.7 collective-permute-start.11
  98.7 6.6 %all-to-all-start.1 = ((bf16[4,232,256]{2,1,0:T(8,128)(2,1)}), bf16[4,232,256]{2,1,0:T(8,128)(2,1)S(1)}, u32[]{:S(2)}, u32[]{:S(2)}) async-start(bf16[4,232,256]{2,1,0:T(8,128)(2,1)} %shard_map.101), calls=%async_computation.1 | async-start | bytes 950272 | tf_op jit(solution)/shard_map/all_to_all | solution.py:419
  105.2 0.9 shard_map.103
  106.2 11.1 %collective-permute-start.12 = (bf16[2,512,128]{2,1,0:T(8,128)(2,1)}, bf16[2,512,128]{2,1,0:T(8,128)(2,1)S(1)}, u32[]{:S(2)}, u32[]{:S(2)}) collective-permute-start(bf16[2,512,128]{2,1,0:T(8,128)(2,1)} %get-tuple-element.122), channel_id=1, source_target_pairs={{0,1},{1,0},{2,3},{3,2},{4,5},{5,4},{6,7},{7,6},{8,9},{9,8},{10,11... | collective-permute-start | bytes 786440 | tf_op jit(solution)/shard_map/ppermute | solution.py:436
  117.2 1.4 collective-permute-done.12.recv
  118.7 6.9 %collective-permute-start.13 = (bf16[512,128]{1,0:T(8,128)(2,1)S(1)}, bf16[512,128]{1,0:T(8,128)(2,1)S(1)}, u32[]{:S(2)}, u32[]{:S(2)}) collective-permute-start(bf16[512,128]{1,0:T(8,128)(2,1)S(1)} %get-tuple-element.124), channel_id=1, source_target_pairs={{0,2},{2,0},{1,3},{3,1},{4,6},{6,4},{5,7},{7,5},{8,10},{10,8},{9,1... | collective-permute-start | bytes 393224 | tf_op jit(solution)/shard_map/ppermute | solution.py:438
  125.5 0.7 broadcast_select_fusion
  126.3 2.7 %shard_map.102 = bf16[16,232,256]{2,1,0:T(8,128)(2,1)S(1)} custom-call(bf16[4,232,256]{2,1,0:T(8,128)(2,1)S(1)} %all-to-all-done.1.parts), custom_call_target="tpu_custom_call" | custom-call | flops 1000000 | bytes 1000 | tf_op jit(solution)/shard_map/pallas_call | solution.py:266
  129.3 0.7 add_convert_fusion
  130.0 33.5 %all_to_all.16 = bf16[16,232,256]{2,1,0:T(8,128)(2,1)S(1)} all-to-all(bf16[16,232,256]{2,1,0:T(8,128)(2,1)S(1)} %shard_map.102), channel_id=1, replica_groups=mesh['zh'=4,'zl'=2,'x'=4,'yh'=2,'yl'=2,'c'=2] {'zl','x','yh'}, dimensions={0} | all-to-all | bytes 3801088 | tf_op jit(solution)/shard_map/all_to_all | solution.py:440
  163.5 2.0 %shard_map.105 = (f32[3456,256]{1,0:T(8,128)}, f32[256,256]{1,0:T(8,128)}) custom-call(bf16[3712,256]{1,0:T(8,128)(2,1)S(1)} %bitcast.37), custom_call_target="tpu_custom_call" | custom-call | flops 1000000 | bytes 1000 | tf_op jit(solution)/shard_map/pallas_call | solution.py:266
  (41 shorter events, 5.9 us)
Async XLA Ops:
  8.1 17.5 %collective-permute-start.1 = (bf16[2048,128]{1,0:T(8,128)(2,1)S(1)}, bf16[2048,128]{1,0:T(8,128)(2,1)S(1)}, u32[]{:S(2)}, u32[]{:S(2)}) collective-permute-start(bf16[2048,128]{1,0:T(8,128)(2,1)S(1)} %all_gather.3.centre), channel_id=1, source_target_pairs={{5,1},{9,5},{10,2},{13,9},{14,6},{17,13},{18,10},{19,3},{21,17},{2... | collective-permute-start | bytes 1572872 | tf_op jit(solution)/shard_map/ppermute | solution.py:306
  8.8 16.8 %collective-permute-start = (bf16[2048,128]{1,0:T(8,128)(2,1)S(1)}, bf16[2048,128]{1,0:T(8,128)(2,1)S(1)}, u32[]{:S(2)}, u32[]{:S(2)}) collective-permute-start(bf16[2048,128]{1,0:T(8,128)(2,1)S(1)} %all_gather.3.centre), channel_id=1, source_target_pairs={{1,5},{2,10},{3,19},{5,9},{6,14},{7,23},{9,13},{10,18},{11,27},{13... | collective-permute-start | bytes 1572872 | tf_op jit(solution)/shard_map/ppermute | solution.py:305
  9.5 16.1 %collective-permute-start.2 = (bf16[512,256]{1,0:T(8,128)(2,1)}, bf16[512,256]{1,0:T(8,128)(2,1)S(1)}, u32[]{:S(2)}, u32[]{:S(2)}) collective-permute-start(bf16[512,256]{1,0:T(8,128)(2,1)} %bitcast.39), channel_id=1, source_target_pairs={{0,2},{2,0},{1,3},{3,1},{4,6},{6,4},{5,7},{7,5},{8,10},{10,8},{9,1... | collective-permute-start | bytes 786440 | tf_op jit(solution)/shard_map/ppermute | solution.py:307
  20.5 0.8 copy-start.4
  23.1 2.5 %copy-start.1 = (bf16[1,256,256]{2,1,0:T(8,128)(2,1)S(1)}, bf16[1,256,256]{2,1,0:T(8,128)(2,1)}, u32[]{:S(2)}) copy-start(bf16[1,256,256]{2,1,0:T(8,128)(2,1)} %param.9) | copy-start | bytes 393220
  27.9 8.2 %collective-permute-start.3 = (bf16[512,256]{1,0:T(8,128)(2,1)S(1)}, bf16[512,256]{1,0:T(8,128)(2,1)S(1)}, u32[]{:S(2)}, u32[]{:S(2)}) collective-permute-start(bf16[512,256]{1,0:T(8,128)(2,1)S(1)} %get-tuple-element.76), channel_id=1, source_target_pairs={{0,1},{1,0},{2,3},{3,2},{4,5},{5,4},{6,7},{7,6},{8,9},{9,8},{10,11... | collective-permute-start | bytes 786440 | tf_op jit(solution)/shard_map/ppermute | solution.py:336
  36.2 2.5 %collective-permute-start.4 = (bf16[512,256]{1,0:T(8,128)(2,1)S(1)}, bf16[512,256]{1,0:T(8,128)(2,1)S(1)}, u32[]{:S(2)}, u32[]{:S(2)}) collective-permute-start(bf16[512,256]{1,0:T(8,128)(2,1)S(1)} %get-tuple-element.78), channel_id=1, source_target_pairs={{0,1},{1,0},{2,3},{3,2},{4,5},{5,4},{6,7},{7,6},{8,9},{9,8},{10,11... | collective-permute-start | bytes 786440 | tf_op jit(solution)/shard_map/ppermute | solution.py:340
  36.3 9.4 %collective-permute-start.6 = (bf16[512,256]{1,0:T(8,128)(2,1)S(1)}, bf16[512,256]{1,0:T(8,128)(2,1)S(1)}, u32[]{:S(2)}, u32[]{:S(2)}) collective-permute-start(bf16[512,256]{1,0:T(8,128)(2,1)S(1)} %get-tuple-element.81), channel_id=1, source_target_pairs={{0,2},{2,0},{1,3},{3,1},{4,6},{6,4},{5,7},{7,5},{8,10},{10,8},{9,1... | collective-permute-start | bytes 786440 | tf_op jit(solution)/shard_map/ppermute | solution.py:339
  38.7 13.2 %collective-permute-start.5 = (bf16[512,256]{1,0:T(8,128)(2,1)S(1)}, bf16[512,256]{1,0:T(8,128)(2,1)S(1)}, u32[]{:S(2)}, u32[]{:S(2)}) collective-permute-start(bf16[512,256]{1,0:T(8,128)(2,1)S(1)} %get-tuple-element.80), channel_id=1, source_target_pairs={{0,2},{2,0},{1,3},{3,1},{4,6},{6,4},{5,7},{7,5},{8,10},{10,8},{9,1... | collective-permute-start | bytes 786440 | tf_op jit(solution)/shard_map/ppermute | solution.py:342
  40.1 5.7 %copy-start = (bf16[8,4,16,256]{3,2,1,0:T(8,128)(2,1)S(1)}, bf16[8,4,16,256]{3,2,1,0:T(8,128)(2,1)}, u32[]{:S(2)}) copy-start(bf16[8,4,16,256]{3,2,1,0:T(8,128)(2,1)} %param.11) | copy-start | bytes 786436
  40.1 5.7 %copy-start.3 = (f32[256]{0:T(256)S(1)}, f32[256]{0:T(256)}, u32[]{:S(2)}) copy-start(f32[256]{0:T(256)} %param.10) | copy-start | bytes 3076
  46.1 1.4 collective-permute-start.8
  46.2 1.5 collective-permute-start.7
  52.2 7.8 %copy-start.2 = (bf16[512,256]{1,0:T(8,128)(2,1)}, bf16[512,256]{1,0:T(8,128)(2,1)S(1)}, u32[]{:S(2)}) copy-start(bf16[512,256]{1,0:T(8,128)(2,1)S(1)} %get-tuple-element.126) | copy-start | bytes 786436
  52.3 1.8 %collective-permute-start.9 = (bf16[512,256]{1,0:T(8,128)(2,1)S(1)}, bf16[512,256]{1,0:T(8,128)(2,1)S(1)}, u32[]{:S(2)}, u32[]{:S(2)}) collective-permute-start(bf16[512,256]{1,0:T(8,128)(2,1)S(1)} %get-tuple-element.99.own), channel_id=1, source_target_pairs={{0,1},{1,0},{2,3},{3,2},{4,5},{5,4},{6,7},{7,6},{8,9},{9,8},{10,11... | collective-permute-start | bytes 786440 | tf_op jit(solution)/shard_map/ppermute | solution.py:382
  97.3 8.0 %collective-permute-start.10 = (bf16[2048,128]{1,0:T(8,128)(2,1)}, bf16[2048,128]{1,0:T(8,128)(2,1)S(1)}, u32[]{:S(2)}, u32[]{:S(2)}) collective-permute-start(bf16[2048,128]{1,0:T(8,128)(2,1)} %get-tuple-element.118), channel_id=1, source_target_pairs={{5,1},{9,5},{10,2},{13,9},{14,6},{17,13},{18,10},{19,3},{21,17},{2... | collective-permute-start | bytes 1572872 | tf_op jit(solution)/shard_map/ppermute | solution.py:417
  98.0 7.3 %collective-permute-start.11 = (bf16[2048,128]{1,0:T(8,128)(2,1)S(1)}, bf16[2048,128]{1,0:T(8,128)(2,1)S(1)}, u32[]{:S(2)}, u32[]{:S(2)}) collective-permute-start(bf16[2048,128]{1,0:T(8,128)(2,1)S(1)} %get-tuple-element.120), channel_id=1, source_target_pairs={{1,5},{2,10},{3,19},{5,9},{6,14},{7,23},{9,13},{10,18},{11,27},{13... | collective-permute-start | bytes 1572872 | tf_op jit(solution)/shard_map/ppermute | solution.py:418
  98.7 27.6 %all-to-all-start.1 = ((bf16[4,232,256]{2,1,0:T(8,128)(2,1)}), bf16[4,232,256]{2,1,0:T(8,128)(2,1)S(1)}, u32[]{:S(2)}, u32[]{:S(2)}) async-start(bf16[4,232,256]{2,1,0:T(8,128)(2,1)} %shard_map.101), calls=%async_computation.1 | async-start | bytes 950272 | tf_op jit(solution)/shard_map/all_to_all | solution.py:419
  106.2 12.4 %collective-permute-start.12 = (bf16[2,512,128]{2,1,0:T(8,128)(2,1)}, bf16[2,512,128]{2,1,0:T(8,128)(2,1)S(1)}, u32[]{:S(2)}, u32[]{:S(2)}) collective-permute-start(bf16[2,512,128]{2,1,0:T(8,128)(2,1)} %get-tuple-element.122), channel_id=1, source_target_pairs={{0,1},{1,0},{2,3},{3,2},{4,5},{5,4},{6,7},{7,6},{8,9},{9,8},{10,11... | collective-permute-start | bytes 786440 | tf_op jit(solution)/shard_map/ppermute | solution.py:436
  118.7 10.7 %collective-permute-start.13 = (bf16[512,128]{1,0:T(8,128)(2,1)S(1)}, bf16[512,128]{1,0:T(8,128)(2,1)S(1)}, u32[]{:S(2)}, u32[]{:S(2)}) collective-permute-start(bf16[512,128]{1,0:T(8,128)(2,1)S(1)} %get-tuple-element.124), channel_id=1, source_target_pairs={{0,2},{2,0},{1,3},{3,1},{4,6},{6,4},{5,7},{7,5},{8,10},{10,8},{9,1... | collective-permute-start | bytes 393224 | tf_op jit(solution)/shard_map/ppermute | solution.py:438

commit v5 on v4

--- a/solution.py
+++ b/solution.py
@@ -14,7 +14,7 @@
 COL = 64
 ROWS = 2048
 HALF = 1024
-EARLY = 14 * COL
+EARLY = 12 * COL
 QUART = 512
 TAPS = 27 * C
 GRAD_ROWS = TAPS + F
@@ -84,10 +84,11 @@
         base[start : start + QUART] = bias[...] + over_height(matmul(window, weights[...]))
 
 
-def forward_kernel(half, core_ref, below, above, weights, base, proj, preact, hidden, keep, send, low, high):
+def forward_kernel(
+    half, core_ref, below, above, weights, base, proj, preact, hidden, keep, send_0, send_1, low, high, sides
+):
     pad_half(low, below, half)
     pad_half(high, above, half)
-    core = core_ref[0]
     for side in range(2):
         start = side * QUART
         cells = slice(start, start + QUART)
@@ -98,15 +99,11 @@
         preact[cells] = value
         active = (value * jax.nn.sigmoid(value)).astype(bf16)
         hidden[cells] = active
-        projected = matmul(active, proj[...])
-
-        @pl.when(core == side)
-        def _():
-            keep[...] = projected
-
-        @pl.when(core != side)
-        def _():
-            send[...] = projected.astype(bf16)
+        sides[side] = matmul(active, proj[...])
+    core = core_ref[0]
+    keep[...] = sides[core]
+    send_0[...] = sides[1 - core, : QUART // 2].astype(bf16)
+    send_1[...] = sides[1 - core, QUART // 2 :].astype(bf16)
 
 
 def prepare_kernel(
@@ -125,11 +122,30 @@
                 features_t[block : block + C, cells] = moved.T.astype(bf16)
 
 
-def output_kernel(half, row_ref, chip_sum, recv, bias, cot_mine, cot_pair, own, head):
+def d_out_of(summed, cot):
+    return (cot.astype(f32) * silu_slope(summed)).astype(bf16)
+
+
+def head_of(summed):
+    return (summed * jax.nn.sigmoid(summed)).astype(bf16)
+
+
+def first_output_kernel(row_ref, chip_sum, recv, bias, cot_mine, cot_pair, own_0, own_1):
+    for k, own in enumerate((own_0, own_1)):
+        cells = slice(k * (QUART // 2), (k + 1) * (QUART // 2))
+        summed = chip_sum[cells] + recv[cells].astype(f32) + bias[...]
+        own[...] = d_out_of(summed, jnp.where(row_ref[0] == 0, cot_mine[cells], cot_pair[cells]))
+
+
+def second_output_kernel(row_ref, chip_sum, recv, bias, cot_mine, cot_pair, own):
     summed = chip_sum[...] + recv[...].astype(f32) + bias[...]
-    head[...] = (summed * jax.nn.sigmoid(summed)).astype(bf16)
-    cot = jnp.where(row_ref[0] == half, cot_mine[...], cot_pair[...])
-    own[...] = (cot.astype(f32) * silu_slope(summed)).astype(bf16)
+    own[...] = d_out_of(summed, jnp.where(row_ref[0] == 1, cot_mine[...], cot_pair[...]))
+
+
+def head_kernel(row_ref, chip_a, recv_a, chip_b, recv_b, bias, head):
+    first = row_ref[0] == 0
+    partial = jnp.where(first, chip_a[...], chip_b[...])
+    head[...] = head_of(partial + jnp.where(first, recv_a[...], recv_b[...]).astype(f32) + bias[...])
 
 
 def height_sum(parts):
@@ -138,11 +154,14 @@
 
 def back_rows(core_ref, own, other, slope, proj, d_pre, at, d_out):
     for side in range(2):
-        cells = slice(side * QUART, (side + 1) * QUART)
-        rows = jnp.where(core_ref[0] == side, own[...], other[...])
-        d_out[cells] = rows
-        d_hidden = matmul_rt(rows, proj[...])
-        d_pre[at + side * QUART : at + (side + 1) * QUART] = (d_hidden * slope[cells]).astype(bf16)
+        start = side * QUART
+        for mine, theirs in zip(own, other):
+            count = mine.shape[0]
+            rows = jnp.where(core_ref[0] == side, mine[...], theirs[...])
+            d_out[start : start + count] = rows
+            d_hidden = matmul_rt(rows, proj[...])
+            d_pre[at + start : at + start + count] = (d_hidden * slope[start : start + count]).astype(bf16)
+            start += count
 
 
 def back_features(d_pre, weights, start, count):
@@ -153,13 +172,11 @@
 
 
 def back_first_kernel(
-    core_ref, own, other_0, other_1, slope, proj, weights, features_t, hidden_t,
-    d_pre, low, mid, high, taps, projs, window, d_out, other,
+    core_ref, own_0, own_1, other_0, other_1, slope, proj, weights, features_t, hidden_t,
+    d_pre, low, mid, high, taps, projs, window, d_out,
 ):
     d_pre[0:COL] = jnp.zeros((COL, F), bf16)
-    other[: QUART // 2] = other_0[...]
-    other[QUART // 2 :] = other_1[...]
-    back_rows(core_ref, own, other, slope, proj, d_pre, COL, d_out)
+    back_rows(core_ref, (own_0, own_1), (other_0, other_1), slope, proj, d_pre, COL, d_out)
     for k in range(2):
         step = EARLY // 2
         total = back_features(d_pre, weights, k * step, step)
@@ -179,15 +196,15 @@
     core_ref, keep_ref, own, other, slope, proj, weights, features_t, hidden_t,
     d_pre_a, low_a, mid_a, high_a, taps, projs, low, mid, high, grads, d_pre, window, d_out,
 ):
-    d_pre[0 : 3 * COL] = d_pre_a[HALF - 2 * COL :]
-    d_pre[3 * COL + HALF :] = jnp.zeros((COL, F), bf16)
-    back_rows(core_ref, own, other, slope.at[HALF:], proj, d_pre, 3 * COL, d_out)
+    d_pre[0 : 5 * COL] = d_pre_a[HALF - 4 * COL :]
+    d_pre[5 * COL + HALF :] = jnp.zeros((COL, F), bf16)
+    back_rows(core_ref, (own,), (other,), slope.at[HALF:], proj, d_pre, 5 * COL, d_out)
     low[:EARLY] = low_a[...]
     mid[:EARLY] = mid_a[...]
     high[:EARLY] = high_a[...]
     late = ROWS - EARLY
-    for k in range(3):
-        step = late // 3
+    for k in range(2):
+        step = late // 2
         total = back_features(d_pre, weights, k * step, step)
         cells = slice(EARLY + k * step, EARLY + (k + 1) * step)
         low[cells] = total[:, :C].astype(bf16)
@@ -209,19 +226,14 @@
     grads[TAPS:] = (projs[...] + matmul(hidden_t[:, HALF:], d_out[...])).astype(bf16)
 
 
-def core_split_kernel(core_ref, low, mid, high, kept, sent):
-    core = core_ref[0]
+def core_split_kernel(core_ref, low, mid, high, kept, sent, total):
     for q in range(4):
         cells = slice(q * QUART, (q + 1) * QUART)
-        total = mid[cells] + low[cells].astype(f32) + high[cells].astype(f32)
-
-        @pl.when(core == q % 2)
-        def _():
-            kept[q // 2] = total
-
-        @pl.when(core != q % 2)
-        def _():
-            sent[q // 2] = total.astype(bf16)
+        total[q] = mid[cells] + low[cells].astype(f32) + high[cells].astype(f32)
+    core = core_ref[0]
+    for row in range(2):
+        kept[row] = total[2 * row + core]
+        sent[row] = total[2 * row + 1 - core].astype(bf16)
 
 
 def chip_split_kernel(row_ref, kept, recv, mine, sent):
@@ -237,14 +249,10 @@
     return acc.astype(bf16)
 
 
-def sum_kernel(parts, copies, total, sems):
-    total[...] = sum_of(parts)
-    peers = copies.shape[0]
-    moves = [pltpu.make_async_copy(total, copies.at[k], sems.at[k]) for k in range(peers)]
-    for move in moves:
-        move.start()
-    for move in moves:
-        move.wait()
+def sum_kernel(parts, copies):
+    total = sum_of(parts)
+    for k in range(copies.shape[0]):
+        copies[k] = total
 
 
 def widen_kernel(total, taps_out, proj_out, wide, sems):
@@ -283,6 +291,10 @@
             if 0 <= target < mesh_gz:
                 pairs.append((g * 4 + b, target * 4 + b))
     return pairs
+
+
+def exchanged(parts, axis):
+    return jnp.concatenate([lax.ppermute(part, axis, SWAP) for part in parts], axis=0).astype(f32)
 
 
 def shards(slabs, features, tap_weights, branch_bias, proj_weights, out_bias, cotangent):
@@ -322,22 +334,22 @@
         (below, above, cot_pair, base, weights_out, weights_bwd)
     )
 
-    def forward_half(half):
+    def forward_half(half, base):
         return call(
             functools.partial(forward_kernel, half),
-            [((HALF, F), f32), ((HALF, F), bf16), ((QUART, F), f32), ((QUART, F), bf16)],
+            [((HALF, F), f32), ((HALF, F), bf16), ((QUART, F), f32)] + [((QUART // 2, F), bf16)] * 2,
             [SMEM] + [VMEM] * 5,
-            [pltpu.VMEM((HALF + 2 * COL, C), bf16)] * 2,
-            ROWS * 18 * C * F,
+            [pltpu.VMEM((HALF + 2 * COL, C), bf16)] * 2 + [pltpu.VMEM((2, QUART, F), f32)],
+            1000,
             core_arg, below, above, weights_out, base, proj,
         )
 
-    preact_a, hidden_a, keep_a, send_a = forward_half(0)
-    chip_a = keep_a + lax.ppermute(send_a, "c", SWAP).astype(f32)
-    preact_b, hidden_b, keep_b, send_b = forward_half(1)
-    chip_send_a, send_b = lax.optimization_barrier((chip_a.astype(bf16), send_b))
+    preact_a, hidden_a, keep_a, *send_a = forward_half(0, base)
+    chip_a = keep_a + exchanged(send_a, "c")
+    preact_b, hidden_b, keep_b, *send_b = forward_half(1, base)
+    chip_send_a, *send_b = lax.optimization_barrier((chip_a.astype(bf16), *send_b))
     recv_a = lax.ppermute(chip_send_a, "yl", SWAP)
-    chip_b = keep_b + lax.ppermute(send_b, "c", SWAP).astype(f32)
+    chip_b = keep_b + exchanged(send_b, "c")
     chip_send_b, preact_b = lax.optimization_barrier((chip_b.astype(bf16), preact_b))
     recv_b = lax.ppermute(chip_send_b, "yl", SWAP)
     slope, hidden_t, features_t = call(
@@ -350,18 +362,15 @@
     )
     recv_a, slope, hidden_t, features_t = lax.optimization_barrier((recv_a, slope, hidden_t, features_t))
 
-    def output_half(half, chip_sum, recv):
-        return call(
-            functools.partial(output_kernel, half),
-            [((QUART, F), bf16), ((QUART, F), bf16)],
-            [SMEM] + [VMEM] * 5,
-            [],
-            1000,
-            row_arg, chip_sum, recv, out_bias[None], cot_mine, cot_pair,
-        )
-
-    own_a, head_a = output_half(0, chip_a, recv_a)
-    other_a = [lax.ppermute(own_a[k : k + QUART // 2], "c", SWAP) for k in (0, QUART // 2)]
+    own_a = call(
+        first_output_kernel,
+        [((QUART // 2, F), bf16), ((QUART // 2, F), bf16)],
+        [SMEM] + [VMEM] * 5,
+        [],
+        1000,
+        row_arg, chip_a, recv_a, out_bias[None], cot_mine, cot_pair,
+    )
+    other_a = [lax.ppermute(part, "c", SWAP) for part in own_a]
     d_pre_a, low_a, mid_a, high_a, taps_a, projs_a = call(
         back_first_kernel,
         [
@@ -372,20 +381,27 @@
             ((9 * C, 3 * F), f32),
             ((F, F), f32),
         ],
-        [SMEM] + [VMEM] * 8,
-        [pltpu.VMEM((EARLY, 3 * F), bf16), pltpu.VMEM((HALF, F), bf16), pltpu.VMEM((QUART, F), bf16)],
+        [SMEM] + [VMEM] * 9,
+        [pltpu.VMEM((EARLY, 3 * F), bf16), pltpu.VMEM((HALF, F), bf16)],
         1000,
-        core_arg, own_a, *other_a, slope, proj, weights_bwd, features_t, hidden_t,
+        core_arg, *own_a, *other_a, slope, proj, weights_bwd, features_t, hidden_t,
     )
     recv_b, taps_a, d_pre_a = lax.optimization_barrier((recv_b, taps_a, d_pre_a))
-    own_b, head_b = output_half(1, chip_b, recv_b)
+    (own_b,) = call(
+        second_output_kernel,
+        [((QUART, F), bf16)],
+        [SMEM] + [VMEM] * 5,
+        [],
+        1000,
+        row_arg, chip_b, recv_b, out_bias[None], cot_mine, cot_pair,
+    )
     other_b = lax.ppermute(own_b, "c", SWAP)
     low, mid, high, grads = call(
         back_second_kernel,
         [((ROWS, C), bf16), ((ROWS, C), f32), ((ROWS, C), bf16), ((GRAD_ROWS, F), bf16)],
         [SMEM, SMEM] + [VMEM] * 13,
         [
-            pltpu.VMEM((HALF + 4 * COL, F), bf16),
+            pltpu.VMEM((HALF + 6 * COL, F), bf16),
             pltpu.VMEM((ROWS - EARLY, 3 * F), bf16),
             pltpu.VMEM((HALF, F), bf16),
         ],
@@ -393,7 +409,6 @@
         core_arg, off_centre[None], own_b, other_b, slope, proj, weights_bwd, features_t, hidden_t,
         d_pre_a, low_a, mid_a, high_a, taps_a, projs_a,
     )
-    head_out = jnp.where(row == 0, head_a, head_b)
     near = math.prod(lax.axis_size(a) for a in NEAR)
     far = lax.axis_size(FAR)
     share = GRAD_ROWS // near
@@ -406,14 +421,21 @@
             sum_kernel,
             [((peers, share, F), bf16)],
             [VMEM],
-            [pltpu.VMEM((share, F), bf16), pltpu.SemaphoreType.DMA((peers,))],
+            [],
             1_000_000,
             parts,
-            place=HBM,
         )[0]
 
     part = sum_for(far, part)
-    part, low, high = lax.optimization_barrier((part, low, high))
+    part, low, high, chip_a = lax.optimization_barrier((part, low, high, chip_a))
+    (head_out,) = call(
+        head_kernel,
+        [((QUART, F), bf16)],
+        [SMEM] + [VMEM] * 5,
+        [],
+        1000,
+        row_arg, chip_a, recv_a, chip_b, recv_b, out_bias[None],
+    )
     from_low = lax.ppermute(low, everywhere, down)
     from_high = lax.ppermute(high, everywhere, up)
     part = lax.all_to_all(part, FAR, 0, 0, tiled=True)
@@ -423,7 +445,7 @@
         core_split_kernel,
         [((2, QUART, C), f32), ((2, QUART, C), bf16)],
         [SMEM] + [VMEM] * 3,
-        [],
+        [pltpu.VMEM((4, QUART, C), f32)],
         1_000_000,
         core_arg, from_low, mid, from_high,
     )
@@ -435,10 +457,10 @@
         1_000_000,
         row_arg, kept, lax.ppermute(sent, "c", SWAP),
     )
-    feature_grad = (mine + lax.ppermute(sent, "yl", SWAP).astype(f32)).astype(bf16)
+    recv = lax.ppermute(sent, "yl", SWAP)
+    feature_grad = (mine + recv.astype(f32)).astype(bf16)
     part, feature_grad, head_out = lax.optimization_barrier((part, feature_grad, head_out))
     total = lax.all_to_all(part, NEAR, 0, 0, tiled=True).reshape(GRAD_ROWS, F)
-
     taps, proj_total = call(
         widen_kernel,
         [((TAPS, F), f32), ((F, F), f32)],

time: 166 us -> 167 us (level)
  waiting for transfers between devices: 9.75 us -> 12.2 us
  Pallas kernels: 26.3 us -> 24.4 us
    ppermute x5 -> x7, waiting for transfers between devices: 1.41 us -> 3.85 us  [the longest x1 2.81 us: shards(): recv = lax.ppermute(sent, 'yl', SWAP)]
    pallas_call x13 -> x14, Pallas kernels: 26.3 us -> 24.4 us  [call(): pl.pallas_call(kernel, out_shape=[jax.ShapeDtypeStruct(*o) for o in outs]...]
    ppermute x5 -> x7, starting transfers between devices: 13.4 us -> 14.5 us  [the longest x1 7.17 us: shards(): recv = lax.ppermute(sent, 'yl', SWAP)]
  transfers between devices with their start and end apart: 15 -> 17, of which waited for: 7 -> 7; matrix products, arithmetic and copies ran while one was open for 4% -> 4% of each run, Pallas kernels for 9% -> 8%
where the time goes in v5:
time: 167 us; the launch traced here: 166 us
  blocking collectives  77.2 us (46%)
  starting transfers between devices  44.8 us (27%)
  Pallas kernels  24.4 us (15%)
  waiting for transfers between devices  12.2 us (7%)
  local copies, waits for them, and re-layouts  3.97 us (2%)
  other arithmetic  2.69 us (2%)
    all_to_all x1, blocking collectives, shards(): part = lax.all_to_all(grads.reshape(near, share, F), NEAR, 0, 0, tiled=True)  36.1 us
    all_to_all x1, blocking collectives, shards(): total = lax.all_to_all(part, NEAR, 0, 0, tiled=True).reshape(GRAD_ROWS, F)  33.6 us
    pallas_call x14, Pallas kernels, call(): pl.pallas_call(kernel, out_shape=[jax.ShapeDtypeStruct(*o) for o in outs]...  24.4 us
    ppermute x1, starting transfers between devices, shards(): lax.ppermute(sent, 'c', SWAP)  9.52 us
    all_gather x1, blocking collectives, shards(): centre = lax.all_gather(features.reshape(QUART, C), BR, axis=0, tiled=True)  7.47 us
    ppermute x1, starting transfers between devices, shards(): recv = lax.ppermute(sent, 'yl', SWAP)  7.17 us
    ppermute x4, starting transfers between devices, exchanged(): lax.ppermute(part, axis, SWAP)  6.73 us
    all_to_all x1, starting transfers between devices, shards(): part = lax.all_to_all(part, FAR, 0, 0, tiled=True)  6.56 us
  transfers between devices with their start and end apart: 17, of which 7 were waited for; matrix products, arithmetic and copies ran while one was open for 4% of the time, Pallas kernels for 8%

profile of v5, /device:TPU:64, one launch (start us, length us, event | category | flops | bytes accessed | tf_op | source)
XLA Modules:
  0.0 166.2 jit_solution(9242655843240431872)
XLA Ops:
  0.6 7.5 %all_gather.3.centre = bf16[2048,128]{1,0:T(8,128)(2,1)S(1)} all-gather(bf16[512,128]{1,0:T(8,128)(2,1)} %bitcast.57), channel_id=1, replica_groups=mesh['zh'=4,'zl'=2,'x'=4,'yh'=2,'yl'=2,'c'=2] {'yl','c'}, dimensions={0}, use_global_device_ids=true | all-gather | bytes 655360 | tf_op jit(solution)/shard_map/all_gather | solution.py:311
  8.8 0.7 collective-permute-start
  9.5 5.9 %collective-permute-start.2 = (bf16[512,256]{1,0:T(8,128)(2,1)}, bf16[512,256]{1,0:T(8,128)(2,1)S(1)}, u32[]{:S(2)}, u32[]{:S(2)}) collective-permute-start(bf16[512,256]{1,0:T(8,128)(2,1)} %bitcast.43), channel_id=1, source_target_pairs={{0,2},{2,0},{1,3},{3,1},{4,6},{6,4},{5,7},{7,5},{8,10},{10,8},{9,1... | collective-permute-start | bytes 786440 | tf_op jit(solution)/shard_map/ppermute | solution.py:319
  15.4 1.8 %fusion = (bf16[3,3,128,3,256]{4,2,0,3,1:T(8,128)(2,1)S(1)}, bf16[3,3,128,3,256]{4,2,3,1,0:T(8,128)(2,1)S(1)}) fusion(bf16[1,3,3,3,128,256]{5,4,3,2,1,0:T(8,128)(2,1)} %param.7, bf16[3,3,3]{2,1,0:T(4,128)(2,1)S(1)} %select_convert_fusion), kind=kLoop, calls=%fused_computation.1 | loop fusion | flops 884736 | bytes 5308470 | tf_op jit(solution)/shard_map/transpose | solution.py:324
  17.3 1.5 copy.17
  21.2 1.8 %shard_map.93.base = f32[2048,256]{1,0:T(8,128)S(1)} custom-call(bf16[2048,128]{1,0:T(8,128)(2,1)S(1)} %all_gather.3.centre, bf16[384,768]{1,0:T(8,128)(2,1)S(1)} %bitcast.46, f32[1,256]{1,0:T(1,128)S(1)} %copy-done.5), custom_call_target="tpu_custom_call" | custom-call | flops 1207959552 | bytes 1207959 | tf_op jit(solution)/shard_map/pallas_call | solution.py:274
  23.1 2.4 %collective-permute-done.2.cot_pair = bf16[512,256]{1,0:T(8,128)(2,1)S(1)} collective-permute-done((bf16[512,256]{1,0:T(8,128)(2,1)}, bf16[512,256]{1,0:T(8,128)(2,1)S(1)}, u32[]{:S(2)}, u32[]{:S(2)}) %collective-permute-start.2) | collective-permute-done | bytes 262176 | tf_op jit(solution)/shard_map/ppermute | solution.py:319
  25.6 2.3 %shard_map.95 = (f32[1024,256]{1,0:T(8,128)S(1)}, bf16[1024,256]{1,0:T(8,128)(2,1)S(1)}, f32[512,256]{1,0:T(8,128)S(1)}, bf16[256,256]{1,0:T(8,128)(2,1)S(1)}, bf16[256,256]{1,0:T(8,128)(2,1)S(1)}) custom-call(s32[1]{0:T(128)} %bitcast.core_ref, bf16[2048,128]{1,0:T(8,128)(2,1)S(1)} %collective-permute-done.below, ...), custom_call_target="tpu_custom_call" | custom-call | flops 1000 | bytes 1 | tf_op jit(solution)/shard_map/pallas_call | solution.py:274
  27.8 5.8 %collective-permute-start.3 = (bf16[256,256]{1,0:T(8,128)(2,1)S(1)}, bf16[256,256]{1,0:T(8,128)(2,1)S(1)}, u32[]{:S(2)}, u32[]{:S(2)}) collective-permute-start(bf16[256,256]{1,0:T(8,128)(2,1)S(1)} %get-tuple-element.78), channel_id=1, source_target_pairs={{0,1},{1,0},{2,3},{3,2},{4,5},{5,4},{6,7},{7,6},{8,9},{9,8},{10,11... | collective-permute-start | bytes 393224 | tf_op jit(solution)/shard_map/ppermute | solution.py:297
  33.8 2.2 %shard_map.94 = (f32[1024,256]{1,0:T(8,128)S(1)}, bf16[1024,256]{1,0:T(8,128)(2,1)S(1)}, f32[512,256]{1,0:T(8,128)S(1)}, bf16[256,256]{1,0:T(8,128)(2,1)S(1)}, bf16[256,256]{1,0:T(8,128)(2,1)S(1)}) custom-call(s32[1]{0:T(128)} %bitcast.core_ref, bf16[2048,128]{1,0:T(8,128)(2,1)S(1)} %collective-permute-done.below, ...), custom_call_target="tpu_custom_call" | custom-call | flops 1000 | bytes 1 | tf_op jit(solution)/shard_map/pallas_call | solution.py:274
  36.9 2.1 %collective-permute-start.8 = (bf16[512,256]{1,0:T(8,128)(2,1)S(1)}, bf16[512,256]{1,0:T(8,128)(2,1)S(1)}, u32[]{:S(2)}, u32[]{:S(2)}) collective-permute-start(bf16[512,256]{1,0:T(8,128)(2,1)S(1)} %get-tuple-element.86), channel_id=1, source_target_pairs={{0,2},{2,0},{1,3},{3,1},{4,6},{6,4},{5,7},{7,5},{8,10},{10,8},{9,1... | collective-permute-start | bytes 786440 | tf_op jit(solution)/shard_map/ppermute | solution.py:351
  39.1 1.1 collective-permute-start.7
  40.2 2.3 %shard_map.96 = (f32[2048,256]{1,0:T(8,128)S(1)}, bf16[256,2048]{1,0:T(8,128)(2,1)S(1)}, bf16[1152,2048]{1,0:T(8,128)(2,1)S(1)}) custom-call(bf16[2048,128]{1,0:T(8,128)(2,1)S(1)} %collective-permute-done.below, bf16[2048,128]{1,0:T(8,128)(2,1)S(1)} %all_gather.3.centre, bf16[2048,128]{1,0:T(8,128)(2,1)S(1)} %collective-permute-done.1.above, ...), custom_call_target="tpu_custom_call" | custom-call | flops 1000 | bytes 1 | tf_op jit(solution)/shard_map/pallas_call | solution.py:274
  42.6 3.5 %collective-permute-done.8.recv.recv_a = bf16[512,256]{1,0:T(8,128)(2,1)S(1)} collective-permute-done((bf16[512,256]{1,0:T(8,128)(2,1)S(1)}, bf16[512,256]{1,0:T(8,128)(2,1)S(1)}, u32[]{:S(2)}, u32[]{:S(2)}) %collective-permute-start.8) | collective-permute-done | bytes 262176 | tf_op jit(solution)/shard_map/ppermute | solution.py:351
  46.9 0.8 collective-permute-done.9.other_0
  47.9 3.5 %shard_map.98 = (bf16[1088,256]{1,0:T(8,128)(2,1)S(1)}, bf16[768,128]{1,0:T(8,128)(2,1)S(1)}, f32[768,128]{1,0:T(8,128)S(1)}, bf16[768,128]{1,0:T(8,128)(2,1)S(1...) custom-call(s32[1]{0:T(128)} %bitcast.core_ref, bf16[256,256]{1,0:T(8,128)(2,1)S(1)} %get-tuple-element.96.own_0, ...), custom_call_target="tpu_custom_call" | custom-call | flops 1000 | bytes 1 | tf_op jit(solution)/shard_map/pallas_call | solution.py:274
  52.3 1.2 collective-permute-done.11.other
  53.5 6.4 %shard_map.100 = (bf16[2048,128]{1,0:T(8,128)(2,1)}, f32[2048,128]{1,0:T(8,128)S(1)}, bf16[2048,128]{1,0:T(8,128)(2,1)}, bf16[3712,256]{1,0:T(8,128)(2,1)S(1)}) custom-call(s32[1]{0:T(128)} %bitcast.core_ref, f32[1]{0:T(128)} %bitcast.1.keep_ref, bf16[512,256]{1,0:T(8,128)(2,1)S(1)} %shard_map.99.own, bf16[512,256]{1,0:T(8,128)(2,1)S(1)} %collective-permute-done.11.other, ...), custom_call_target="tpu_custom_call" | custom-call | flops 3623878656 | bytes 3623878 | tf_op jit(solution)/shard_map/pallas_call | solution.py:274
  59.9 36.1 %all_to_all.15.parts = bf16[16,232,256]{2,1,0:T(8,128)(2,1)S(1)} all-to-all(bf16[16,232,256]{2,1,0:T(8,128)(2,1)S(1)} %bitcast.42), channel_id=1, replica_groups=mesh['zh'=4,'zl'=2,'x'=4,'yh'=2,'yl'=2,'c'=2] {'zl','x','yh'}, dimensions={0} | all-to-all | bytes 3801088 | tf_op jit(solution)/shard_map/all_to_all | solution.py:416
  96.0 1.0 shard_map.101
  97.0 1.6 collective-permute-start.12
  98.6 1.4 collective-permute-start.13
  100.0 6.6 %all-to-all-start.1 = ((bf16[4,232,256]{2,1,0:T(8,128)(2,1)}), bf16[4,232,256]{2,1,0:T(8,128)(2,1)S(1)}, u32[]{:S(2)}, u32[]{:S(2)}) async-start(bf16[4,232,256]{2,1,0:T(8,128)(2,1)} %shard_map.101), calls=%async_computation.1 | async-start | bytes 950272 | tf_op jit(solution)/shard_map/all_to_all | solution.py:441
  106.6 1.4 shard_map.103
  108.0 9.5 %collective-permute-start.14 = (bf16[2,512,128]{2,1,0:T(8,128)(2,1)S(1)}, bf16[2,512,128]{2,1,0:T(8,128)(2,1)S(1)}, u32[]{:S(2)}, u32[]{:S(2)}) collective-permute-start(bf16[2,512,128]{2,1,0:T(8,128)(2,1)S(1)} %get-tuple-element.127), channel_id=1, source_target_pairs={{0,1},{1,0},{2,3},{3,2},{4,5},{5,4},{6,7},{7,6},{8,9},{9,8},{10,11... | collective-permute-start | bytes 786440 | tf_op jit(solution)/shard_map/ppermute | solution.py:458
  117.6 1.2 collective-permute-done.14.recv
  118.8 7.2 %collective-permute-start.15 = (bf16[512,128]{1,0:T(8,128)(2,1)S(1)}, bf16[512,128]{1,0:T(8,128)(2,1)S(1)}, u32[]{:S(2)}, u32[]{:S(2)}) collective-permute-start(bf16[512,128]{1,0:T(8,128)(2,1)S(1)} %get-tuple-element.129), channel_id=1, source_target_pairs={{0,2},{2,0},{1,3},{3,1},{4,6},{6,4},{5,7},{7,5},{8,10},{10,8},{9,1... | collective-permute-start | bytes 393224 | tf_op jit(solution)/shard_map/ppermute | solution.py:460
  125.9 0.8 shard_map.105
  126.9 2.8 %collective-permute-done.15 = bf16[512,128]{1,0:T(8,128)(2,1)S(1)} collective-permute-done((bf16[512,128]{1,0:T(8,128)(2,1)S(1)}, bf16[512,128]{1,0:T(8,128)(2,1)S(1)}, u32[]{:S(2)}, u32[]{:S(2)}) %collective-permute-start.15) | collective-permute-done | bytes 131104 | tf_op jit(solution)/shard_map/ppermute | solution.py:460
  129.7 0.7 add_convert_fusion
  130.4 33.6 %all_to_all.16 = bf16[16,232,256]{2,1,0:T(8,128)(2,1)S(1)} all-to-all(bf16[16,232,256]{2,1,0:T(8,128)(2,1)S(1)} %shard_map.102), channel_id=1, replica_groups=mesh['zh'=4,'zl'=2,'x'=4,'yh'=2,'yl'=2,'c'=2] {'zl','x','yh'}, dimensions={0} | all-to-all | bytes 3801088 | tf_op jit(solution)/shard_map/all_to_all | solution.py:463
  164.1 2.0 %shard_map.106 = (f32[3456,256]{1,0:T(8,128)}, f32[256,256]{1,0:T(8,128)}) custom-call(bf16[3712,256]{1,0:T(8,128)(2,1)S(1)} %bitcast.37), custom_call_target="tpu_custom_call" | custom-call | flops 1000000 | bytes 1000 | tf_op jit(solution)/shard_map/pallas_call | solution.py:274
  (46 shorter events, 6.3 us)
Async XLA Ops:
  8.1 17.5 %collective-permute-start.1 = (bf16[2048,128]{1,0:T(8,128)(2,1)S(1)}, bf16[2048,128]{1,0:T(8,128)(2,1)S(1)}, u32[]{:S(2)}, u32[]{:S(2)}) collective-permute-start(bf16[2048,128]{1,0:T(8,128)(2,1)S(1)} %all_gather.3.centre), channel_id=1, source_target_pairs={{5,1},{9,5},{10,2},{13,9},{14,6},{17,13},{18,10},{19,3},{21,17},{2... | collective-permute-start | bytes 1572872 | tf_op jit(solution)/shard_map/ppermute | solution.py:318
  8.8 16.8 %collective-permute-start = (bf16[2048,128]{1,0:T(8,128)(2,1)S(1)}, bf16[2048,128]{1,0:T(8,128)(2,1)S(1)}, u32[]{:S(2)}, u32[]{:S(2)}) collective-permute-start(bf16[2048,128]{1,0:T(8,128)(2,1)S(1)} %all_gather.3.centre), channel_id=1, source_target_pairs={{1,5},{2,10},{3,19},{5,9},{6,14},{7,23},{9,13},{10,18},{11,27},{13... | collective-permute-start | bytes 1572872 | tf_op jit(solution)/shard_map/ppermute | solution.py:317
  9.5 16.1 %collective-permute-start.2 = (bf16[512,256]{1,0:T(8,128)(2,1)}, bf16[512,256]{1,0:T(8,128)(2,1)S(1)}, u32[]{:S(2)}, u32[]{:S(2)}) collective-permute-start(bf16[512,256]{1,0:T(8,128)(2,1)} %bitcast.43), channel_id=1, source_target_pairs={{0,2},{2,0},{1,3},{3,1},{4,6},{6,4},{5,7},{7,5},{8,10},{10,8},{9,1... | collective-permute-start | bytes 786440 | tf_op jit(solution)/shard_map/ppermute | solution.py:319
  20.5 0.8 copy-start.5
  23.0 2.5 %copy-start = (bf16[1,256,256]{2,1,0:T(8,128)(2,1)S(1)}, bf16[1,256,256]{2,1,0:T(8,128)(2,1)}, u32[]{:S(2)}) copy-start(bf16[1,256,256]{2,1,0:T(8,128)(2,1)} %param.9) | copy-start | bytes 393220
  27.8 8.2 %collective-permute-start.3 = (bf16[256,256]{1,0:T(8,128)(2,1)S(1)}, bf16[256,256]{1,0:T(8,128)(2,1)S(1)}, u32[]{:S(2)}, u32[]{:S(2)}) collective-permute-start(bf16[256,256]{1,0:T(8,128)(2,1)S(1)} %get-tuple-element.78), channel_id=1, source_target_pairs={{0,1},{1,0},{2,3},{3,2},{4,5},{5,4},{6,7},{7,6},{8,9},{9,8},{10,11... | collective-permute-start | bytes 393224 | tf_op jit(solution)/shard_map/ppermute | solution.py:297
  33.7 2.4 %collective-permute-start.4 = (bf16[256,256]{1,0:T(8,128)(2,1)S(1)}, bf16[256,256]{1,0:T(8,128)(2,1)S(1)}, u32[]{:S(2)}, u32[]{:S(2)}) collective-permute-start(bf16[256,256]{1,0:T(8,128)(2,1)S(1)} %get-tuple-element.79), channel_id=1, source_target_pairs={{0,1},{1,0},{2,3},{3,2},{4,5},{5,4},{6,7},{7,6},{8,9},{9,8},{10,11... | collective-permute-start | bytes 393224 | tf_op jit(solution)/shard_map/ppermute | solution.py:297
  36.1 2.9 %collective-permute-start.5 = (bf16[256,256]{1,0:T(8,128)(2,1)S(1)}, bf16[256,256]{1,0:T(8,128)(2,1)S(1)}, u32[]{:S(2)}, u32[]{:S(2)}) collective-permute-start(bf16[256,256]{1,0:T(8,128)(2,1)S(1)} %get-tuple-element.82), channel_id=1, source_target_pairs={{0,1},{1,0},{2,3},{3,2},{4,5},{5,4},{6,7},{7,6},{8,9},{9,8},{10,11... | collective-permute-start | bytes 393224 | tf_op jit(solution)/shard_map/ppermute | solution.py:297
  36.6 2.4 %collective-permute-start.6 = (bf16[256,256]{1,0:T(8,128)(2,1)S(1)}, bf16[256,256]{1,0:T(8,128)(2,1)S(1)}, u32[]{:S(2)}, u32[]{:S(2)}) collective-permute-start(bf16[256,256]{1,0:T(8,128)(2,1)S(1)} %get-tuple-element.83), channel_id=1, source_target_pairs={{0,1},{1,0},{2,3},{3,2},{4,5},{5,4},{6,7},{7,6},{8,9},{9,8},{10,11... | collective-permute-start | bytes 393224 | tf_op jit(solution)/shard_map/ppermute | solution.py:297
  36.9 9.2 %collective-permute-start.8 = (bf16[512,256]{1,0:T(8,128)(2,1)S(1)}, bf16[512,256]{1,0:T(8,128)(2,1)S(1)}, u32[]{:S(2)}, u32[]{:S(2)}) collective-permute-start(bf16[512,256]{1,0:T(8,128)(2,1)S(1)} %get-tuple-element.86), channel_id=1, source_target_pairs={{0,2},{2,0},{1,3},{3,1},{4,6},{6,4},{5,7},{7,5},{8,10},{10,8},{9,1... | collective-permute-start | bytes 786440 | tf_op jit(solution)/shard_map/ppermute | solution.py:351
  39.1 12.3 %collective-permute-start.7 = (bf16[512,256]{1,0:T(8,128)(2,1)S(1)}, bf16[512,256]{1,0:T(8,128)(2,1)S(1)}, u32[]{:S(2)}, u32[]{:S(2)}) collective-permute-start(bf16[512,256]{1,0:T(8,128)(2,1)S(1)} %get-tuple-element.85), channel_id=1, source_target_pairs={{0,2},{2,0},{1,3},{3,1},{4,6},{6,4},{5,7},{7,5},{8,10},{10,8},{9,1... | collective-permute-start | bytes 786440 | tf_op jit(solution)/shard_map/ppermute | solution.py:354
  40.2 5.8 %copy-start.1 = (bf16[8,4,16,256]{3,2,1,0:T(8,128)(2,1)S(1)}, bf16[8,4,16,256]{3,2,1,0:T(8,128)(2,1)}, u32[]{:S(2)}) copy-start(bf16[8,4,16,256]{3,2,1,0:T(8,128)(2,1)} %param.11) | copy-start | bytes 786436
  40.2 5.8 %copy-start.4 = (f32[256]{0:T(256)S(1)}, f32[256]{0:T(256)}, u32[]{:S(2)}) copy-start(f32[256]{0:T(256)} %param.10) | copy-start | bytes 3076
  46.1 5.3 %copy-start.2 = (bf16[512,256]{1,0:T(8,128)(2,1)}, bf16[512,256]{1,0:T(8,128)(2,1)S(1)}, u32[]{:S(2)}) copy-start(bf16[512,256]{1,0:T(8,128)(2,1)S(1)} %collective-permute-done.8.recv.recv_a) | copy-start | bytes 786436
  46.3 1.4 collective-permute-start.9
  46.4 1.5 collective-permute-start.10
  51.6 1.8 %collective-permute-start.11 = (bf16[512,256]{1,0:T(8,128)(2,1)S(1)}, bf16[512,256]{1,0:T(8,128)(2,1)S(1)}, u32[]{:S(2)}, u32[]{:S(2)}) collective-permute-start(bf16[512,256]{1,0:T(8,128)(2,1)S(1)} %shard_map.99.own), channel_id=1, source_target_pairs={{0,1},{1,0},{2,3},{3,2},{4,5},{5,4},{6,7},{7,6},{8,9},{9,8},{10,11... | collective-permute-start | bytes 786440 | tf_op jit(solution)/shard_map/ppermute | solution.py:398
  97.0 28.9 %copy-start.3 = (bf16[512,256]{1,0:T(8,128)(2,1)S(1)}, bf16[512,256]{1,0:T(8,128)(2,1)}, u32[]{:S(2)}) copy-start(bf16[512,256]{1,0:T(8,128)(2,1)} %copy-done.2) | copy-start | bytes 786436
  97.0 9.6 %collective-permute-start.12 = (bf16[2048,128]{1,0:T(8,128)(2,1)}, bf16[2048,128]{1,0:T(8,128)(2,1)}, u32[]{:S(2)}, u32[]{:S(2)}) collective-permute-start(bf16[2048,128]{1,0:T(8,128)(2,1)} %get-tuple-element.123), channel_id=1, source_target_pairs={{5,1},{9,5},{10,2},{13,9},{14,6},{17,13},{18,10},{19,3},{21,17},{2... | collective-permute-start | bytes 1572872 | tf_op jit(solution)/shard_map/ppermute | solution.py:439
  98.6 8.0 %collective-permute-start.13 = (bf16[2048,128]{1,0:T(8,128)(2,1)}, bf16[2048,128]{1,0:T(8,128)(2,1)}, u32[]{:S(2)}, u32[]{:S(2)}) collective-permute-start(bf16[2048,128]{1,0:T(8,128)(2,1)} %get-tuple-element.125), channel_id=1, source_target_pairs={{1,5},{2,10},{3,19},{5,9},{6,14},{7,23},{9,13},{10,18},{11,27},{13... | collective-permute-start | bytes 1572872 | tf_op jit(solution)/shard_map/ppermute | solution.py:440
  100.0 26.8 %all-to-all-start.1 = ((bf16[4,232,256]{2,1,0:T(8,128)(2,1)}), bf16[4,232,256]{2,1,0:T(8,128)(2,1)S(1)}, u32[]{:S(2)}, u32[]{:S(2)}) async-start(bf16[4,232,256]{2,1,0:T(8,128)(2,1)} %shard_map.101), calls=%async_computation.1 | async-start | bytes 950272 | tf_op jit(solution)/shard_map/all_to_all | solution.py:441
  108.0 10.7 %collective-permute-start.14 = (bf16[2,512,128]{2,1,0:T(8,128)(2,1)S(1)}, bf16[2,512,128]{2,1,0:T(8,128)(2,1)S(1)}, u32[]{:S(2)}, u32[]{:S(2)}) collective-permute-start(bf16[2,512,128]{2,1,0:T(8,128)(2,1)S(1)} %get-tuple-element.127), channel_id=1, source_target_pairs={{0,1},{1,0},{2,3},{3,2},{4,5},{5,4},{6,7},{7,6},{8,9},{9,8},{10,11... | collective-permute-start | bytes 786440 | tf_op jit(solution)/shard_map/ppermute | solution.py:458
  118.8 11.0 %collective-permute-start.15 = (bf16[512,128]{1,0:T(8,128)(2,1)S(1)}, bf16[512,128]{1,0:T(8,128)(2,1)S(1)}, u32[]{:S(2)}, u32[]{:S(2)}) collective-permute-start(bf16[512,128]{1,0:T(8,128)(2,1)S(1)} %get-tuple-element.129), channel_id=1, source_target_pairs={{0,2},{2,0},{1,3},{3,1},{4,6},{6,4},{5,7},{7,5},{8,10},{10,8},{9,1... | collective-permute-start | bytes 393224 | tf_op jit(solution)/shard_map/ppermute | solution.py:460

commit v6 on v5

--- a/solution.py
+++ b/solution.py
@@ -130,22 +130,18 @@
     return (summed * jax.nn.sigmoid(summed)).astype(bf16)
 
 
-def first_output_kernel(row_ref, chip_sum, recv, bias, cot_mine, cot_pair, own_0, own_1):
+def first_output_kernel(row_ref, chip_sum, recv, bias, cot_mine, cot_pair, own_0, own_1, head):
     for k, own in enumerate((own_0, own_1)):
         cells = slice(k * (QUART // 2), (k + 1) * (QUART // 2))
         summed = chip_sum[cells] + recv[cells].astype(f32) + bias[...]
+        head[cells] = head_of(summed)
         own[...] = d_out_of(summed, jnp.where(row_ref[0] == 0, cot_mine[cells], cot_pair[cells]))
 
 
-def second_output_kernel(row_ref, chip_sum, recv, bias, cot_mine, cot_pair, own):
+def second_output_kernel(row_ref, chip_sum, recv, bias, cot_mine, cot_pair, head_a, own, head):
     summed = chip_sum[...] + recv[...].astype(f32) + bias[...]
     own[...] = d_out_of(summed, jnp.where(row_ref[0] == 1, cot_mine[...], cot_pair[...]))
-
-
-def head_kernel(row_ref, chip_a, recv_a, chip_b, recv_b, bias, head):
-    first = row_ref[0] == 0
-    partial = jnp.where(first, chip_a[...], chip_b[...])
-    head[...] = head_of(partial + jnp.where(first, recv_a[...], recv_b[...]).astype(f32) + bias[...])
+    head[...] = jnp.where(row_ref[0] == 0, head_a[...], head_of(summed))
 
 
 def height_sum(parts):
@@ -203,8 +199,8 @@
     mid[:EARLY] = mid_a[...]
     high[:EARLY] = high_a[...]
     late = ROWS - EARLY
-    for k in range(2):
-        step = late // 2
+    for k in range(4):
+        step = late // 4
         total = back_features(d_pre, weights, k * step, step)
         cells = slice(EARLY + k * step, EARLY + (k + 1) * step)
         low[cells] = total[:, :C].astype(bf16)
@@ -362,9 +358,9 @@
     )
     recv_a, slope, hidden_t, features_t = lax.optimization_barrier((recv_a, slope, hidden_t, features_t))
 
-    own_a = call(
+    *own_a, head_a = call(
         first_output_kernel,
-        [((QUART // 2, F), bf16), ((QUART // 2, F), bf16)],
+        [((QUART // 2, F), bf16), ((QUART // 2, F), bf16), ((QUART, F), bf16)],
         [SMEM] + [VMEM] * 5,
         [],
         1000,
@@ -387,13 +383,13 @@
         core_arg, *own_a, *other_a, slope, proj, weights_bwd, features_t, hidden_t,
     )
     recv_b, taps_a, d_pre_a = lax.optimization_barrier((recv_b, taps_a, d_pre_a))
-    (own_b,) = call(
+    own_b, head_out = call(
         second_output_kernel,
-        [((QUART, F), bf16)],
-        [SMEM] + [VMEM] * 5,
+        [((QUART, F), bf16), ((QUART, F), bf16)],
+        [SMEM] + [VMEM] * 6,
         [],
         1000,
-        row_arg, chip_b, recv_b, out_bias[None], cot_mine, cot_pair,
+        row_arg, chip_b, recv_b, out_bias[None], cot_mine, cot_pair, head_a,
     )
     other_b = lax.ppermute(own_b, "c", SWAP)
     low, mid, high, grads = call(
@@ -427,15 +423,7 @@
         )[0]
 
     part = sum_for(far, part)
-    part, low, high, chip_a = lax.optimization_barrier((part, low, high, chip_a))
-    (head_out,) = call(
-        head_kernel,
-        [((QUART, F), bf16)],
-        [SMEM] + [VMEM] * 5,
-        [],
-        1000,
-        row_arg, chip_a, recv_a, chip_b, recv_b, out_bias[None],
-    )
+    part, low, high = lax.optimization_barrier((part, low, high))
     from_low = lax.ppermute(low, everywhere, down)
     from_high = lax.ppermute(high, everywhere, up)
     part = lax.all_to_all(part, FAR, 0, 0, tiled=True)
@@ -459,7 +447,7 @@
     )
     recv = lax.ppermute(sent, "yl", SWAP)
     feature_grad = (mine + recv.astype(f32)).astype(bf16)
-    part, feature_grad, head_out = lax.optimization_barrier((part, feature_grad, head_out))
+    part, feature_grad = lax.optimization_barrier((part, feature_grad))
     total = lax.all_to_all(part, NEAR, 0, 0, tiled=True).reshape(GRAD_ROWS, F)
     taps, proj_total = call(
         widen_kernel,

time: 167 us -> 165 us (0.988)
    pallas_call x14 -> x13, Pallas kernels: 24.4 us -> 22.9 us  [call(): pl.pallas_call(kernel, out_shape=[jax.ShapeDtypeStruct(*o) for o in outs]...]
  transfers between devices with their start and end apart: 17 -> 17, of which waited for: 7 -> 7; matrix products, arithmetic and copies ran while one was open for 4% -> 4% of each run, Pallas kernels for 8% -> 6%
where the time goes in v6:
time: 165 us
  blocking collectives  77 us (47%)
  starting transfers between devices  44.2 us (27%)
  Pallas kernels  22.9 us (14%)
  waiting for transfers between devices  13 us (8%)
  local copies, waits for them, and re-layouts  3.96 us (2%)
  other arithmetic  2.68 us (2%)
    all_to_all x1, blocking collectives, shards(): part = lax.all_to_all(grads.reshape(near, share, F), NEAR, 0, 0, tiled=True)  36.1 us
    all_to_all x1, blocking collectives, shards(): total = lax.all_to_all(part, NEAR, 0, 0, tiled=True).reshape(GRAD_ROWS, F)  33.4 us
    pallas_call x13, Pallas kernels, call(): pl.pallas_call(kernel, out_shape=[jax.ShapeDtypeStruct(*o) for o in outs]...  22.9 us
    ppermute x1, starting transfers between devices, shards(): lax.ppermute(sent, 'c', SWAP)  11.1 us
    all_gather x1, blocking collectives, shards(): centre = lax.all_gather(features.reshape(QUART, C), BR, axis=0, tiled=True)  7.47 us
    ppermute x1, starting transfers between devices, shards(): recv = lax.ppermute(sent, 'yl', SWAP)  7 us
    ppermute x4, starting transfers between devices, exchanged(): lax.ppermute(part, axis, SWAP)  6.72 us
    all_to_all x1, starting transfers between devices, shards(): part = lax.all_to_all(part, FAR, 0, 0, tiled=True)  6.58 us
  transfers between devices with their start and end apart: 17, of which 7 were waited for; matrix products, arithmetic and copies ran while one was open for 4% of the time, Pallas kernels for 6%

profile of v6, /device:TPU:64, one launch (start us, length us, event | category | flops | bytes accessed | tf_op | source)
XLA Modules:
  0.0 164.9 jit_solution(3690999293270371257)
XLA Ops:
  0.6 7.5 %all_gather.3.centre = bf16[2048,128]{1,0:T(8,128)(2,1)S(1)} all-gather(bf16[512,128]{1,0:T(8,128)(2,1)} %bitcast.55), channel_id=1, replica_groups=mesh['zh'=4,'zl'=2,'x'=4,'yh'=2,'yl'=2,'c'=2] {'yl','c'}, dimensions={0}, use_global_device_ids=true | all-gather | bytes 655360 | tf_op jit(solution)/shard_map/all_gather | solution.py:307
  8.1 0.7 collective-permute-start.1
  8.8 0.7 collective-permute-start
  9.5 5.9 %collective-permute-start.2 = (bf16[512,256]{1,0:T(8,128)(2,1)}, bf16[512,256]{1,0:T(8,128)(2,1)S(1)}, u32[]{:S(2)}, u32[]{:S(2)}) collective-permute-start(bf16[512,256]{1,0:T(8,128)(2,1)} %bitcast.43), channel_id=1, source_target_pairs={{0,2},{2,0},{1,3},{3,1},{4,6},{6,4},{5,7},{7,5},{8,10},{10,8},{9,1... | collective-permute-start | bytes 786440 | tf_op jit(solution)/shard_map/ppermute | solution.py:315
  15.4 1.8 %fusion = (bf16[3,3,128,3,256]{4,2,0,3,1:T(8,128)(2,1)S(1)}, bf16[3,3,128,3,256]{4,2,3,1,0:T(8,128)(2,1)S(1)}) fusion(bf16[1,3,3,3,128,256]{5,4,3,2,1,0:T(8,128)(2,1)} %param.7, bf16[3,3,3]{2,1,0:T(4,128)(2,1)S(1)} %select_convert_fusion), kind=kLoop, calls=%fused_computation.1 | loop fusion | flops 884736 | bytes 5308470 | tf_op jit(solution)/shard_map/transpose | solution.py:320
  17.3 1.5 copy.17
  21.2 1.8 %shard_map.93.base = f32[2048,256]{1,0:T(8,128)S(1)} custom-call(bf16[2048,128]{1,0:T(8,128)(2,1)S(1)} %all_gather.3.centre, bf16[384,768]{1,0:T(8,128)(2,1)S(1)} %bitcast.46, f32[1,256]{1,0:T(1,128)S(1)} %copy-done.3), custom_call_target="tpu_custom_call" | custom-call | flops 1207959552 | bytes 1207959 | tf_op jit(solution)/shard_map/pallas_call | solution.py:270
  23.1 2.4 %collective-permute-done.2.cot_pair = bf16[512,256]{1,0:T(8,128)(2,1)S(1)} collective-permute-done((bf16[512,256]{1,0:T(8,128)(2,1)}, bf16[512,256]{1,0:T(8,128)(2,1)S(1)}, u32[]{:S(2)}, u32[]{:S(2)}) %collective-permute-start.2) | collective-permute-done | bytes 262176 | tf_op jit(solution)/shard_map/ppermute | solution.py:315
  25.6 2.3 %shard_map.95 = (f32[1024,256]{1,0:T(8,128)S(1)}, bf16[1024,256]{1,0:T(8,128)(2,1)S(1)}, f32[512,256]{1,0:T(8,128)S(1)}, bf16[256,256]{1,0:T(8,128)(2,1)S(1)}, bf16[256,256]{1,0:T(8,128)(2,1)S(1)}) custom-call(s32[1]{0:T(128)} %bitcast.1.core_ref, bf16[2048,128]{1,0:T(8,128)(2,1)S(1)} %collective-permute-done.below, ...), custom_call_target="tpu_custom_call" | custom-call | flops 1000 | bytes 1 | tf_op jit(solution)/shard_map/pallas_call | solution.py:270
  27.8 5.8 %collective-permute-start.3 = (bf16[256,256]{1,0:T(8,128)(2,1)S(1)}, bf16[256,256]{1,0:T(8,128)(2,1)S(1)}, u32[]{:S(2)}, u32[]{:S(2)}) collective-permute-start(bf16[256,256]{1,0:T(8,128)(2,1)S(1)} %get-tuple-element.79), channel_id=1, source_target_pairs={{0,1},{1,0},{2,3},{3,2},{4,5},{5,4},{6,7},{7,6},{8,9},{9,8},{10,11... | collective-permute-start | bytes 393224 | tf_op jit(solution)/shard_map/ppermute | solution.py:293
  33.8 2.3 %shard_map.94 = (f32[1024,256]{1,0:T(8,128)S(1)}, bf16[1024,256]{1,0:T(8,128)(2,1)S(1)}, f32[512,256]{1,0:T(8,128)S(1)}, bf16[256,256]{1,0:T(8,128)(2,1)S(1)}, bf16[256,256]{1,0:T(8,128)(2,1)S(1)}) custom-call(s32[1]{0:T(128)} %bitcast.1.core_ref, bf16[2048,128]{1,0:T(8,128)(2,1)S(1)} %collective-permute-done.below, ...), custom_call_target="tpu_custom_call" | custom-call | flops 1000 | bytes 1 | tf_op jit(solution)/shard_map/pallas_call | solution.py:270
  36.9 2.1 %collective-permute-start.8 = (bf16[512,256]{1,0:T(8,128)(2,1)S(1)}, bf16[512,256]{1,0:T(8,128)(2,1)S(1)}, u32[]{:S(2)}, u32[]{:S(2)}) collective-permute-start(bf16[512,256]{1,0:T(8,128)(2,1)S(1)} %get-tuple-element.87), channel_id=1, source_target_pairs={{0,2},{2,0},{1,3},{3,1},{4,6},{6,4},{5,7},{7,5},{8,10},{10,8},{9,1... | collective-permute-start | bytes 786440 | tf_op jit(solution)/shard_map/ppermute | solution.py:347
  39.1 1.1 collective-permute-start.7
  40.2 2.3 %shard_map.96 = (f32[2048,256]{1,0:T(8,128)S(1)}, bf16[256,2048]{1,0:T(8,128)(2,1)S(1)}, bf16[1152,2048]{1,0:T(8,128)(2,1)S(1)}) custom-call(bf16[2048,128]{1,0:T(8,128)(2,1)S(1)} %collective-permute-done.below, bf16[2048,128]{1,0:T(8,128)(2,1)S(1)} %all_gather.3.centre, bf16[2048,128]{1,0:T(8,128)(2,1)S(1)} %collective-permute-done.1.above, ...), custom_call_target="tpu_custom_call" | custom-call | flops 1000 | bytes 1 | tf_op jit(solution)/shard_map/pallas_call | solution.py:270
  42.6 3.5 %collective-permute-done.8.recv = bf16[512,256]{1,0:T(8,128)(2,1)S(1)} collective-permute-done((bf16[512,256]{1,0:T(8,128)(2,1)S(1)}, bf16[512,256]{1,0:T(8,128)(2,1)S(1)}, u32[]{:S(2)}, u32[]{:S(2)}) %collective-permute-start.8) | collective-permute-done | bytes 262176 | tf_op jit(solution)/shard_map/ppermute | solution.py:347
  47.0 0.8 collective-permute-done.9.other_0
  48.0 3.5 %shard_map.98 = (bf16[1088,256]{1,0:T(8,128)(2,1)S(1)}, bf16[768,128]{1,0:T(8,128)(2,1)S(1)}, f32[768,128]{1,0:T(8,128)S(1)}, bf16[768,128]{1,0:T(8,128)(2,1)S(1...) custom-call(s32[1]{0:T(128)} %bitcast.1.core_ref, bf16[256,256]{1,0:T(8,128)(2,1)S(1)} %get-tuple-element.97.own_0, ...), custom_call_target="tpu_custom_call" | custom-call | flops 1000 | bytes 1 | tf_op jit(solution)/shard_map/pallas_call | solution.py:270
  51.5 0.8 shard_map.99
  52.7 1.2 collective-permute-done.11.other
  53.9 6.3 %shard_map.100 = (bf16[2048,128]{1,0:T(8,128)(2,1)}, f32[2048,128]{1,0:T(8,128)S(1)}, bf16[2048,128]{1,0:T(8,128)(2,1)S(1)}, bf16[3712,256]{1,0:T(8,128)(2,1)S(1)}) custom-call(s32[1]{0:T(128)} %bitcast.1.core_ref, f32[1]{0:T(128)} %bitcast.10.keep_ref, bf16[512,256]{1,0:T(8,128)(2,1)S(1)} %get-tuple-element.108.own, ...), custom_call_target="tpu_custom_call" | custom-call | flops 3623878656 | bytes 3623878 | tf_op jit(solution)/shard_map/pallas_call | solution.py:270
  60.2 36.1 %all_to_all.15.parts = bf16[16,232,256]{2,1,0:T(8,128)(2,1)S(1)} all-to-all(bf16[16,232,256]{2,1,0:T(8,128)(2,1)S(1)} %bitcast.42), channel_id=1, replica_groups=mesh['zh'=4,'zl'=2,'x'=4,'yh'=2,'yl'=2,'c'=2] {'zl','x','yh'}, dimensions={0} | all-to-all | bytes 3801088 | tf_op jit(solution)/shard_map/all_to_all | solution.py:412
  96.3 1.0 shard_map.101
  97.3 0.7 collective-permute-start.12
  98.0 0.7 collective-permute-start.13
  98.7 6.6 %all-to-all-start.1 = ((bf16[4,232,256]{2,1,0:T(8,128)(2,1)}), bf16[4,232,256]{2,1,0:T(8,128)(2,1)S(1)}, u32[]{:S(2)}, u32[]{:S(2)}) async-start(bf16[4,232,256]{2,1,0:T(8,128)(2,1)} %shard_map.101), calls=%async_computation.1 | async-start | bytes 950272 | tf_op jit(solution)/shard_map/all_to_all | solution.py:429
  105.5 11.1 %collective-permute-start.14 = (bf16[2,512,128]{2,1,0:T(8,128)(2,1)S(1)}, bf16[2,512,128]{2,1,0:T(8,128)(2,1)S(1)}, u32[]{:S(2)}, u32[]{:S(2)}) collective-permute-start(bf16[2,512,128]{2,1,0:T(8,128)(2,1)S(1)} %get-tuple-element.131), channel_id=1, source_target_pairs={{0,1},{1,0},{2,3},{3,2},{4,5},{5,4},{6,7},{7,6},{8,9},{9,8},{10,11... | collective-permute-start | bytes 786440 | tf_op jit(solution)/shard_map/ppermute | solution.py:446
  116.6 1.2 collective-permute-done.14.recv
  117.8 7.0 %collective-permute-start.15 = (bf16[512,128]{1,0:T(8,128)(2,1)S(1)}, bf16[512,128]{1,0:T(8,128)(2,1)S(1)}, u32[]{:S(2)}, u32[]{:S(2)}) collective-permute-start(bf16[512,128]{1,0:T(8,128)(2,1)S(1)} %get-tuple-element.133), channel_id=1, source_target_pairs={{0,2},{2,0},{1,3},{3,1},{4,6},{6,4},{5,7},{7,5},{8,10},{10,8},{9,1... | collective-permute-start | bytes 393224 | tf_op jit(solution)/shard_map/ppermute | solution.py:448
  124.9 3.7 %collective-permute-done.15 = bf16[512,128]{1,0:T(8,128)(2,1)S(1)} collective-permute-done((bf16[512,128]{1,0:T(8,128)(2,1)S(1)}, bf16[512,128]{1,0:T(8,128)(2,1)S(1)}, u32[]{:S(2)}, u32[]{:S(2)}) %collective-permute-start.15) | collective-permute-done | bytes 131104 | tf_op jit(solution)/shard_map/ppermute | solution.py:448
  128.6 0.7 add_convert_fusion
  129.3 33.4 %all_to_all.16 = bf16[16,232,256]{2,1,0:T(8,128)(2,1)S(1)} all-to-all(bf16[16,232,256]{2,1,0:T(8,128)(2,1)S(1)} %shard_map.102), channel_id=1, replica_groups=mesh['zh'=4,'zl'=2,'x'=4,'yh'=2,'yl'=2,'c'=2] {'zl','x','yh'}, dimensions={0} | all-to-all | bytes 3801088 | tf_op jit(solution)/shard_map/all_to_all | solution.py:451
  162.7 2.0 %shard_map.105 = (f32[3456,256]{1,0:T(8,128)}, f32[256,256]{1,0:T(8,128)}) custom-call(bf16[3712,256]{1,0:T(8,128)(2,1)S(1)} %bitcast.37), custom_call_target="tpu_custom_call" | custom-call | flops 1000000 | bytes 1000 | tf_op jit(solution)/shard_map/pallas_call | solution.py:270
  (41 shorter events, 5.3 us)
Async XLA Ops:
  8.1 17.5 %collective-permute-start.1 = (bf16[2048,128]{1,0:T(8,128)(2,1)S(1)}, bf16[2048,128]{1,0:T(8,128)(2,1)S(1)}, u32[]{:S(2)}, u32[]{:S(2)}) collective-permute-start(bf16[2048,128]{1,0:T(8,128)(2,1)S(1)} %all_gather.3.centre), channel_id=1, source_target_pairs={{5,1},{9,5},{10,2},{13,9},{14,6},{17,13},{18,10},{19,3},{21,17},{2... | collective-permute-start | bytes 1572872 | tf_op jit(solution)/shard_map/ppermute | solution.py:314
  8.8 16.8 %collective-permute-start = (bf16[2048,128]{1,0:T(8,128)(2,1)S(1)}, bf16[2048,128]{1,0:T(8,128)(2,1)S(1)}, u32[]{:S(2)}, u32[]{:S(2)}) collective-permute-start(bf16[2048,128]{1,0:T(8,128)(2,1)S(1)} %all_gather.3.centre), channel_id=1, source_target_pairs={{1,5},{2,10},{3,19},{5,9},{6,14},{7,23},{9,13},{10,18},{11,27},{13... | collective-permute-start | bytes 1572872 | tf_op jit(solution)/shard_map/ppermute | solution.py:313
  9.5 16.1 %collective-permute-start.2 = (bf16[512,256]{1,0:T(8,128)(2,1)}, bf16[512,256]{1,0:T(8,128)(2,1)S(1)}, u32[]{:S(2)}, u32[]{:S(2)}) collective-permute-start(bf16[512,256]{1,0:T(8,128)(2,1)} %bitcast.43), channel_id=1, source_target_pairs={{0,2},{2,0},{1,3},{3,1},{4,6},{6,4},{5,7},{7,5},{8,10},{10,8},{9,1... | collective-permute-start | bytes 786440 | tf_op jit(solution)/shard_map/ppermute | solution.py:315
  20.5 0.8 copy-start.3
  23.0 2.5 %copy-start = (bf16[1,256,256]{2,1,0:T(8,128)(2,1)S(1)}, bf16[1,256,256]{2,1,0:T(8,128)(2,1)}, u32[]{:S(2)}) copy-start(bf16[1,256,256]{2,1,0:T(8,128)(2,1)} %param.9) | copy-start | bytes 393220
  27.8 8.2 %collective-permute-start.3 = (bf16[256,256]{1,0:T(8,128)(2,1)S(1)}, bf16[256,256]{1,0:T(8,128)(2,1)S(1)}, u32[]{:S(2)}, u32[]{:S(2)}) collective-permute-start(bf16[256,256]{1,0:T(8,128)(2,1)S(1)} %get-tuple-element.79), channel_id=1, source_target_pairs={{0,1},{1,0},{2,3},{3,2},{4,5},{5,4},{6,7},{7,6},{8,9},{9,8},{10,11... | collective-permute-start | bytes 393224 | tf_op jit(solution)/shard_map/ppermute | solution.py:293
  33.7 2.4 %collective-permute-start.4 = (bf16[256,256]{1,0:T(8,128)(2,1)S(1)}, bf16[256,256]{1,0:T(8,128)(2,1)S(1)}, u32[]{:S(2)}, u32[]{:S(2)}) collective-permute-start(bf16[256,256]{1,0:T(8,128)(2,1)S(1)} %get-tuple-element.80), channel_id=1, source_target_pairs={{0,1},{1,0},{2,3},{3,2},{4,5},{5,4},{6,7},{7,6},{8,9},{9,8},{10,11... | collective-permute-start | bytes 393224 | tf_op jit(solution)/shard_map/ppermute | solution.py:293
  36.1 2.9 %collective-permute-start.5 = (bf16[256,256]{1,0:T(8,128)(2,1)S(1)}, bf16[256,256]{1,0:T(8,128)(2,1)S(1)}, u32[]{:S(2)}, u32[]{:S(2)}) collective-permute-start(bf16[256,256]{1,0:T(8,128)(2,1)S(1)} %get-tuple-element.83), channel_id=1, source_target_pairs={{0,1},{1,0},{2,3},{3,2},{4,5},{5,4},{6,7},{7,6},{8,9},{9,8},{10,11... | collective-permute-start | bytes 393224 | tf_op jit(solution)/shard_map/ppermute | solution.py:293
  36.6 2.4 %collective-permute-start.6 = (bf16[256,256]{1,0:T(8,128)(2,1)S(1)}, bf16[256,256]{1,0:T(8,128)(2,1)S(1)}, u32[]{:S(2)}, u32[]{:S(2)}) collective-permute-start(bf16[256,256]{1,0:T(8,128)(2,1)S(1)} %get-tuple-element.84), channel_id=1, source_target_pairs={{0,1},{1,0},{2,3},{3,2},{4,5},{5,4},{6,7},{7,6},{8,9},{9,8},{10,11... | collective-permute-start | bytes 393224 | tf_op jit(solution)/shard_map/ppermute | solution.py:293
  36.9 9.2 %collective-permute-start.8 = (bf16[512,256]{1,0:T(8,128)(2,1)S(1)}, bf16[512,256]{1,0:T(8,128)(2,1)S(1)}, u32[]{:S(2)}, u32[]{:S(2)}) collective-permute-start(bf16[512,256]{1,0:T(8,128)(2,1)S(1)} %get-tuple-element.87), channel_id=1, source_target_pairs={{0,2},{2,0},{1,3},{3,1},{4,6},{6,4},{5,7},{7,5},{8,10},{10,8},{9,1... | collective-permute-start | bytes 786440 | tf_op jit(solution)/shard_map/ppermute | solution.py:347
  39.1 12.4 %collective-permute-start.7 = (bf16[512,256]{1,0:T(8,128)(2,1)S(1)}, bf16[512,256]{1,0:T(8,128)(2,1)S(1)}, u32[]{:S(2)}, u32[]{:S(2)}) collective-permute-start(bf16[512,256]{1,0:T(8,128)(2,1)S(1)} %get-tuple-element.86), channel_id=1, source_target_pairs={{0,2},{2,0},{1,3},{3,1},{4,6},{6,4},{5,7},{7,5},{8,10},{10,8},{9,1... | collective-permute-start | bytes 786440 | tf_op jit(solution)/shard_map/ppermute | solution.py:350
  40.2 5.8 %copy-start.1 = (bf16[8,4,16,256]{3,2,1,0:T(8,128)(2,1)S(1)}, bf16[8,4,16,256]{3,2,1,0:T(8,128)(2,1)}, u32[]{:S(2)}) copy-start(bf16[8,4,16,256]{3,2,1,0:T(8,128)(2,1)} %param.11) | copy-start | bytes 786436
  40.2 5.8 %copy-start.2 = (f32[256]{0:T(256)S(1)}, f32[256]{0:T(256)}, u32[]{:S(2)}) copy-start(f32[256]{0:T(256)} %param.10) | copy-start | bytes 3076
  46.4 1.4 collective-permute-start.9
  46.5 1.5 collective-permute-start.10
  52.3 1.5 collective-permute-start.11
  97.3 8.0 %collective-permute-start.12 = (bf16[2048,128]{1,0:T(8,128)(2,1)}, bf16[2048,128]{1,0:T(8,128)(2,1)S(1)}, u32[]{:S(2)}, u32[]{:S(2)}) collective-permute-start(bf16[2048,128]{1,0:T(8,128)(2,1)} %get-tuple-element.127), channel_id=1, source_target_pairs={{5,1},{9,5},{10,2},{13,9},{14,6},{17,13},{18,10},{19,3},{21,17},{2... | collective-permute-start | bytes 1572872 | tf_op jit(solution)/shard_map/ppermute | solution.py:427
  98.0 7.3 %collective-permute-start.13 = (bf16[2048,128]{1,0:T(8,128)(2,1)S(1)}, bf16[2048,128]{1,0:T(8,128)(2,1)S(1)}, u32[]{:S(2)}, u32[]{:S(2)}) collective-permute-start(bf16[2048,128]{1,0:T(8,128)(2,1)S(1)} %get-tuple-element.129), channel_id=1, source_target_pairs={{1,5},{2,10},{3,19},{5,9},{6,14},{7,23},{9,13},{10,18},{11,27},{13... | collective-permute-start | bytes 1572872 | tf_op jit(solution)/shard_map/ppermute | solution.py:428
  98.7 26.1 %all-to-all-start.1 = ((bf16[4,232,256]{2,1,0:T(8,128)(2,1)}), bf16[4,232,256]{2,1,0:T(8,128)(2,1)S(1)}, u32[]{:S(2)}, u32[]{:S(2)}) async-start(bf16[4,232,256]{2,1,0:T(8,128)(2,1)} %shard_map.101), calls=%async_computation.1 | async-start | bytes 950272 | tf_op jit(solution)/shard_map/all_to_all | solution.py:429
  105.5 12.2 %collective-permute-start.14 = (bf16[2,512,128]{2,1,0:T(8,128)(2,1)S(1)}, bf16[2,512,128]{2,1,0:T(8,128)(2,1)S(1)}, u32[]{:S(2)}, u32[]{:S(2)}) collective-permute-start(bf16[2,512,128]{2,1,0:T(8,128)(2,1)S(1)} %get-tuple-element.131), channel_id=1, source_target_pairs={{0,1},{1,0},{2,3},{3,2},{4,5},{5,4},{6,7},{7,6},{8,9},{9,8},{10,11... | collective-permute-start | bytes 786440 | tf_op jit(solution)/shard_map/ppermute | solution.py:446
  117.8 10.8 %collective-permute-start.15 = (bf16[512,128]{1,0:T(8,128)(2,1)S(1)}, bf16[512,128]{1,0:T(8,128)(2,1)S(1)}, u32[]{:S(2)}, u32[]{:S(2)}) collective-permute-start(bf16[512,128]{1,0:T(8,128)(2,1)S(1)} %get-tuple-element.133), channel_id=1, source_target_pairs={{0,2},{2,0},{1,3},{3,1},{4,6},{6,4},{5,7},{7,5},{8,10},{10,8},{9,1... | collective-permute-start | bytes 393224 | tf_op jit(solution)/shard_map/ppermute | solution.py:448

commit v7 on v6

--- a/solution.py
+++ b/solution.py
@@ -190,7 +190,7 @@
 
 def back_second_kernel(
     core_ref, keep_ref, own, other, slope, proj, weights, features_t, hidden_t,
-    d_pre_a, low_a, mid_a, high_a, taps, projs, low, mid, high, grads, d_pre, window, d_out,
+    d_pre_a, low_a, mid_a, high_a, taps, projs, low_out, mid, high, grads, d_pre, window, d_out, low, sem,
 ):
     d_pre[0 : 5 * COL] = d_pre_a[HALF - 4 * COL :]
     d_pre[5 * COL + HALF :] = jnp.zeros((COL, F), bf16)
@@ -206,6 +206,8 @@
         low[cells] = total[:, :C].astype(bf16)
         mid[cells] = total[:, C : 2 * C]
         high[cells] = total[:, 2 * C :].astype(bf16)
+    low_copy = pltpu.make_async_copy(low, low_out, sem)
+    low_copy.start()
     for i in range(3):
         window[:, i * F : (i + 1) * F] = d_pre[(2 - i) * COL : (2 - i) * COL + late]
     off_centre = keep_ref[0]
@@ -220,6 +222,7 @@
                     piece = piece * off_centre
                 grads[tap : tap + C] = piece.astype(bf16)
     grads[TAPS:] = (projs[...] + matmul(hidden_t[:, HALF:], d_out[...])).astype(bf16)
+    low_copy.wait()
 
 
 def core_split_kernel(core_ref, low, mid, high, kept, sent, total):
@@ -271,7 +274,7 @@
         kernel,
         out_shape=[jax.ShapeDtypeStruct(*o) for o in outs],
         in_specs=specs,
-        out_specs=[place] * len(outs),
+        out_specs=place if isinstance(place, list) else [place] * len(outs),
         scratch_shapes=scratch,
         compiler_params=pltpu.CompilerParams(vmem_limit_bytes=12 * 1024 * 1024),
         cost_estimate=pl.CostEstimate(flops=flops, bytes_accessed=flops // 1000, transcendentals=0),
@@ -400,10 +403,13 @@
             pltpu.VMEM((HALF + 6 * COL, F), bf16),
             pltpu.VMEM((ROWS - EARLY, 3 * F), bf16),
             pltpu.VMEM((HALF, F), bf16),
+            pltpu.VMEM((ROWS, C), bf16),
+            pltpu.SemaphoreType.DMA(()),
         ],
         2 * ROWS * 27 * C * F,
         core_arg, off_centre[None], own_b, other_b, slope, proj, weights_bwd, features_t, hidden_t,
         d_pre_a, low_a, mid_a, high_a, taps_a, projs_a,
+        place=[HBM, VMEM, VMEM, VMEM],
     )
     near = math.prod(lax.axis_size(a) for a in NEAR)
     far = lax.axis_size(FAR)
@@ -423,7 +429,6 @@
         )[0]
 
     part = sum_for(far, part)
-    part, low, high = lax.optimization_barrier((part, low, high))
     from_low = lax.ppermute(low, everywhere, down)
     from_high = lax.ppermute(high, everywhere, up)
     part = lax.all_to_all(part, FAR, 0, 0, tiled=True)

time: 165 us -> 164 us (level)
  transfers between devices with their start and end apart: 17 -> 17, of which waited for: 7 -> 7; matrix products, arithmetic and copies ran while one was open for 4% -> 4% of each run, Pallas kernels for 6% -> 7%
where the time goes in v7:
time: 164 us
  blocking collectives  76.7 us (47%)
  starting transfers between devices  43.2 us (26%)
  Pallas kernels  23 us (14%)
  waiting for transfers between devices  13 us (8%)
  local copies, waits for them, and re-layouts  3.96 us (2%)
  other arithmetic  2.68 us (2%)
    all_to_all x1, blocking collectives, shards(): part = lax.all_to_all(grads.reshape(near, share, F), NEAR, 0, 0, tiled=True)  36.1 us
    all_to_all x1, blocking collectives, shards(): total = lax.all_to_all(part, NEAR, 0, 0, tiled=True).reshape(GRAD_ROWS, F)  33.2 us
    pallas_call x13, Pallas kernels, call(): pl.pallas_call(kernel, out_shape=[jax.ShapeDtypeStruct(*o) for o in outs]...  23 us
    ppermute x1, starting transfers between devices, shards(): lax.ppermute(sent, 'c', SWAP)  9.68 us
    all_gather x1, blocking collectives, shards(): centre = lax.all_gather(features.reshape(QUART, C), BR, axis=0, tiled=True)  7.47 us
    ppermute x1, starting transfers between devices, shards(): recv = lax.ppermute(sent, 'yl', SWAP)  7.39 us
    ppermute x4, starting transfers between devices, exchanged(): lax.ppermute(part, axis, SWAP)  6.72 us
    all_to_all x1, starting transfers between devices, shards(): part = lax.all_to_all(part, FAR, 0, 0, tiled=True)  6.57 us
  transfers between devices with their start and end apart: 17, of which 7 were waited for; matrix products, arithmetic and copies ran while one was open for 4% of the time, Pallas kernels for 7%

profile of v7, /device:TPU:64, one launch (start us, length us, event | category | flops | bytes accessed | tf_op | source)
XLA Modules:
  0.0 163.6 jit_solution(8020414642743065278)
XLA Ops:
  0.6 7.5 %all_gather.3.centre = bf16[2048,128]{1,0:T(8,128)(2,1)S(1)} all-gather(bf16[512,128]{1,0:T(8,128)(2,1)} %bitcast.55), channel_id=1, replica_groups=mesh['zh'=4,'zl'=2,'x'=4,'yh'=2,'yl'=2,'c'=2] {'yl','c'}, dimensions={0}, use_global_device_ids=true | all-gather | bytes 655360 | tf_op jit(solution)/shard_map/all_gather | solution.py:310
  8.1 0.7 collective-permute-start.1
  8.8 0.7 collective-permute-start
  9.5 5.9 %collective-permute-start.2 = (bf16[512,256]{1,0:T(8,128)(2,1)}, bf16[512,256]{1,0:T(8,128)(2,1)S(1)}, u32[]{:S(2)}, u32[]{:S(2)}) collective-permute-start(bf16[512,256]{1,0:T(8,128)(2,1)} %bitcast.43), channel_id=1, source_target_pairs={{0,2},{2,0},{1,3},{3,1},{4,6},{6,4},{5,7},{7,5},{8,10},{10,8},{9,1... | collective-permute-start | bytes 786440 | tf_op jit(solution)/shard_map/ppermute | solution.py:318
  15.4 1.8 %fusion = (bf16[3,3,128,3,256]{4,2,0,3,1:T(8,128)(2,1)S(1)}, bf16[3,3,128,3,256]{4,2,3,1,0:T(8,128)(2,1)S(1)}) fusion(bf16[1,3,3,3,128,256]{5,4,3,2,1,0:T(8,128)(2,1)} %param.7, bf16[3,3,3]{2,1,0:T(4,128)(2,1)S(1)} %select_convert_fusion), kind=kLoop, calls=%fused_computation.1 | loop fusion | flops 884736 | bytes 5308470 | tf_op jit(solution)/shard_map/transpose | solution.py:323
  17.3 1.5 copy.17
  21.2 1.8 %shard_map.93.base = f32[2048,256]{1,0:T(8,128)S(1)} custom-call(bf16[2048,128]{1,0:T(8,128)(2,1)S(1)} %all_gather.3.centre, bf16[384,768]{1,0:T(8,128)(2,1)S(1)} %bitcast.46, f32[1,256]{1,0:T(1,128)S(1)} %copy-done.3), custom_call_target="tpu_custom_call" | custom-call | flops 1207959552 | bytes 1207959 | tf_op jit(solution)/shard_map/pallas_call | solution.py:273
  23.1 2.4 %collective-permute-done.2.cot_pair = bf16[512,256]{1,0:T(8,128)(2,1)S(1)} collective-permute-done((bf16[512,256]{1,0:T(8,128)(2,1)}, bf16[512,256]{1,0:T(8,128)(2,1)S(1)}, u32[]{:S(2)}, u32[]{:S(2)}) %collective-permute-start.2) | collective-permute-done | bytes 262176 | tf_op jit(solution)/shard_map/ppermute | solution.py:318
  25.6 2.3 %shard_map.95 = (f32[1024,256]{1,0:T(8,128)S(1)}, bf16[1024,256]{1,0:T(8,128)(2,1)S(1)}, f32[512,256]{1,0:T(8,128)S(1)}, bf16[256,256]{1,0:T(8,128)(2,1)S(1)}, bf16[256,256]{1,0:T(8,128)(2,1)S(1)}) custom-call(s32[1]{0:T(128)} %bitcast.1.core_ref, bf16[2048,128]{1,0:T(8,128)(2,1)S(1)} %collective-permute-done.below, ...), custom_call_target="tpu_custom_call" | custom-call | flops 1000 | bytes 1 | tf_op jit(solution)/shard_map/pallas_call | solution.py:273
  27.8 5.8 %collective-permute-start.3 = (bf16[256,256]{1,0:T(8,128)(2,1)S(1)}, bf16[256,256]{1,0:T(8,128)(2,1)S(1)}, u32[]{:S(2)}, u32[]{:S(2)}) collective-permute-start(bf16[256,256]{1,0:T(8,128)(2,1)S(1)} %get-tuple-element.76), channel_id=1, source_target_pairs={{0,1},{1,0},{2,3},{3,2},{4,5},{5,4},{6,7},{7,6},{8,9},{9,8},{10,11... | collective-permute-start | bytes 393224 | tf_op jit(solution)/shard_map/ppermute | solution.py:296
  33.8 2.3 %shard_map.94 = (f32[1024,256]{1,0:T(8,128)S(1)}, bf16[1024,256]{1,0:T(8,128)(2,1)S(1)}, f32[512,256]{1,0:T(8,128)S(1)}, bf16[256,256]{1,0:T(8,128)(2,1)S(1)}, bf16[256,256]{1,0:T(8,128)(2,1)S(1)}) custom-call(s32[1]{0:T(128)} %bitcast.1.core_ref, bf16[2048,128]{1,0:T(8,128)(2,1)S(1)} %collective-permute-done.below, ...), custom_call_target="tpu_custom_call" | custom-call | flops 1000 | bytes 1 | tf_op jit(solution)/shard_map/pallas_call | solution.py:273
  36.9 2.1 %collective-permute-start.8 = (bf16[512,256]{1,0:T(8,128)(2,1)S(1)}, bf16[512,256]{1,0:T(8,128)(2,1)S(1)}, u32[]{:S(2)}, u32[]{:S(2)}) collective-permute-start(bf16[512,256]{1,0:T(8,128)(2,1)S(1)} %get-tuple-element.84), channel_id=1, source_target_pairs={{0,2},{2,0},{1,3},{3,1},{4,6},{6,4},{5,7},{7,5},{8,10},{10,8},{9,1... | collective-permute-start | bytes 786440 | tf_op jit(solution)/shard_map/ppermute | solution.py:350
  39.1 1.1 collective-permute-start.7
  40.2 2.3 %shard_map.96 = (f32[2048,256]{1,0:T(8,128)S(1)}, bf16[256,2048]{1,0:T(8,128)(2,1)S(1)}, bf16[1152,2048]{1,0:T(8,128)(2,1)S(1)}) custom-call(bf16[2048,128]{1,0:T(8,128)(2,1)S(1)} %collective-permute-done.below, bf16[2048,128]{1,0:T(8,128)(2,1)S(1)} %all_gather.3.centre, bf16[2048,128]{1,0:T(8,128)(2,1)S(1)} %collective-permute-done.1.above, ...), custom_call_target="tpu_custom_call" | custom-call | flops 1000 | bytes 1 | tf_op jit(solution)/shard_map/pallas_call | solution.py:273
  42.6 3.5 %collective-permute-done.8.recv = bf16[512,256]{1,0:T(8,128)(2,1)S(1)} collective-permute-done((bf16[512,256]{1,0:T(8,128)(2,1)S(1)}, bf16[512,256]{1,0:T(8,128)(2,1)S(1)}, u32[]{:S(2)}, u32[]{:S(2)}) %collective-permute-start.8) | collective-permute-done | bytes 262176 | tf_op jit(solution)/shard_map/ppermute | solution.py:350
  47.0 0.8 collective-permute-done.9.other_0
  48.0 3.5 %shard_map.98 = (bf16[1088,256]{1,0:T(8,128)(2,1)S(1)}, bf16[768,128]{1,0:T(8,128)(2,1)S(1)}, f32[768,128]{1,0:T(8,128)S(1)}, bf16[768,128]{1,0:T(8,128)(2,1)S(1...) custom-call(s32[1]{0:T(128)} %bitcast.1.core_ref, bf16[256,256]{1,0:T(8,128)(2,1)S(1)} %get-tuple-element.94.own_0, ...), custom_call_target="tpu_custom_call" | custom-call | flops 1000 | bytes 1 | tf_op jit(solution)/shard_map/pallas_call | solution.py:273
  51.5 0.8 shard_map.99
  52.7 1.2 collective-permute-done.11.other
  53.9 6.3 %shard_map.100 = (bf16[2048,128]{1,0:T(8,128)(2,1)}, f32[2048,128]{1,0:T(8,128)S(1)}, bf16[2048,128]{1,0:T(8,128)(2,1)S(1)}, bf16[3712,256]{1,0:T(8,128)(2,1)S(1)}) custom-call(s32[1]{0:T(128)} %bitcast.1.core_ref, f32[1]{0:T(128)} %bitcast.10.keep_ref, bf16[512,256]{1,0:T(8,128)(2,1)S(1)} %get-tuple-element.105.own, ...), custom_call_target="tpu_custom_call" | custom-call | flops 3623878656 | bytes 3623878 | tf_op jit(solution)/shard_map/pallas_call | solution.py:273
  60.2 36.1 %all_to_all.15.parts = bf16[16,232,256]{2,1,0:T(8,128)(2,1)S(1)} all-to-all(bf16[16,232,256]{2,1,0:T(8,128)(2,1)S(1)} %bitcast.42), channel_id=1, replica_groups=mesh['zh'=4,'zl'=2,'x'=4,'yh'=2,'yl'=2,'c'=2] {'zl','x','yh'}, dimensions={0} | all-to-all | bytes 3801088 | tf_op jit(solution)/shard_map/all_to_all | solution.py:418
  96.3 0.7 collective-permute-start.12
  97.0 0.7 collective-permute-start.13
  97.7 1.0 shard_map.101
  98.7 6.6 %all-to-all-start.1 = ((bf16[4,232,256]{2,1,0:T(8,128)(2,1)}), bf16[4,232,256]{2,1,0:T(8,128)(2,1)S(1)}, u32[]{:S(2)}, u32[]{:S(2)}) async-start(bf16[4,232,256]{2,1,0:T(8,128)(2,1)} %shard_map.101), calls=%async_computation.1 | async-start | bytes 950272 | tf_op jit(solution)/shard_map/all_to_all | solution.py:434
  105.5 9.7 %collective-permute-start.14 = (bf16[2,512,128]{2,1,0:T(8,128)(2,1)S(1)}, bf16[2,512,128]{2,1,0:T(8,128)(2,1)S(1)}, u32[]{:S(2)}, u32[]{:S(2)}) collective-permute-start(bf16[2,512,128]{2,1,0:T(8,128)(2,1)S(1)} %get-tuple-element.125), channel_id=1, source_target_pairs={{0,1},{1,0},{2,3},{3,2},{4,5},{5,4},{6,7},{7,6},{8,9},{9,8},{10,11... | collective-permute-start | bytes 786440 | tf_op jit(solution)/shard_map/ppermute | solution.py:451
  115.2 1.2 collective-permute-done.14.recv
  116.4 7.4 %collective-permute-start.15 = (bf16[512,128]{1,0:T(8,128)(2,1)S(1)}, bf16[512,128]{1,0:T(8,128)(2,1)S(1)}, u32[]{:S(2)}, u32[]{:S(2)}) collective-permute-start(bf16[512,128]{1,0:T(8,128)(2,1)S(1)} %get-tuple-element.127), channel_id=1, source_target_pairs={{0,2},{2,0},{1,3},{3,1},{4,6},{6,4},{5,7},{7,5},{8,10},{10,8},{9,1... | collective-permute-start | bytes 393224 | tf_op jit(solution)/shard_map/ppermute | solution.py:453
  124.0 3.7 %collective-permute-done.15 = bf16[512,128]{1,0:T(8,128)(2,1)S(1)} collective-permute-done((bf16[512,128]{1,0:T(8,128)(2,1)S(1)}, bf16[512,128]{1,0:T(8,128)(2,1)S(1)}, u32[]{:S(2)}, u32[]{:S(2)}) %collective-permute-start.15) | collective-permute-done | bytes 131104 | tf_op jit(solution)/shard_map/ppermute | solution.py:453
  127.6 0.7 add_convert_fusion
  128.3 33.2 %all_to_all.16 = bf16[16,232,256]{2,1,0:T(8,128)(2,1)S(1)} all-to-all(bf16[16,232,256]{2,1,0:T(8,128)(2,1)S(1)} %shard_map.102), channel_id=1, replica_groups=mesh['zh'=4,'zl'=2,'x'=4,'yh'=2,'yl'=2,'c'=2] {'zl','x','yh'}, dimensions={0} | all-to-all | bytes 3801088 | tf_op jit(solution)/shard_map/all_to_all | solution.py:456
  161.5 2.0 %shard_map.105 = (f32[3456,256]{1,0:T(8,128)}, f32[256,256]{1,0:T(8,128)}) custom-call(bf16[3712,256]{1,0:T(8,128)(2,1)S(1)} %bitcast.37), custom_call_target="tpu_custom_call" | custom-call | flops 1000000 | bytes 1000 | tf_op jit(solution)/shard_map/pallas_call | solution.py:273
  (41 shorter events, 5.3 us)
Async XLA Ops:
  8.1 17.5 %collective-permute-start.1 = (bf16[2048,128]{1,0:T(8,128)(2,1)S(1)}, bf16[2048,128]{1,0:T(8,128)(2,1)S(1)}, u32[]{:S(2)}, u32[]{:S(2)}) collective-permute-start(bf16[2048,128]{1,0:T(8,128)(2,1)S(1)} %all_gather.3.centre), channel_id=1, source_target_pairs={{5,1},{9,5},{10,2},{13,9},{14,6},{17,13},{18,10},{19,3},{21,17},{2... | collective-permute-start | bytes 1572872 | tf_op jit(solution)/shard_map/ppermute | solution.py:317
  8.8 16.8 %collective-permute-start = (bf16[2048,128]{1,0:T(8,128)(2,1)S(1)}, bf16[2048,128]{1,0:T(8,128)(2,1)S(1)}, u32[]{:S(2)}, u32[]{:S(2)}) collective-permute-start(bf16[2048,128]{1,0:T(8,128)(2,1)S(1)} %all_gather.3.centre), channel_id=1, source_target_pairs={{1,5},{2,10},{3,19},{5,9},{6,14},{7,23},{9,13},{10,18},{11,27},{13... | collective-permute-start | bytes 1572872 | tf_op jit(solution)/shard_map/ppermute | solution.py:316
  9.5 16.1 %collective-permute-start.2 = (bf16[512,256]{1,0:T(8,128)(2,1)}, bf16[512,256]{1,0:T(8,128)(2,1)S(1)}, u32[]{:S(2)}, u32[]{:S(2)}) collective-permute-start(bf16[512,256]{1,0:T(8,128)(2,1)} %bitcast.43), channel_id=1, source_target_pairs={{0,2},{2,0},{1,3},{3,1},{4,6},{6,4},{5,7},{7,5},{8,10},{10,8},{9,1... | collective-permute-start | bytes 786440 | tf_op jit(solution)/shard_map/ppermute | solution.py:318
  20.5 0.8 copy-start.3
  23.0 2.5 %copy-start = (bf16[1,256,256]{2,1,0:T(8,128)(2,1)S(1)}, bf16[1,256,256]{2,1,0:T(8,128)(2,1)}, u32[]{:S(2)}) copy-start(bf16[1,256,256]{2,1,0:T(8,128)(2,1)} %param.9) | copy-start | bytes 393220
  27.8 8.2 %collective-permute-start.3 = (bf16[256,256]{1,0:T(8,128)(2,1)S(1)}, bf16[256,256]{1,0:T(8,128)(2,1)S(1)}, u32[]{:S(2)}, u32[]{:S(2)}) collective-permute-start(bf16[256,256]{1,0:T(8,128)(2,1)S(1)} %get-tuple-element.76), channel_id=1, source_target_pairs={{0,1},{1,0},{2,3},{3,2},{4,5},{5,4},{6,7},{7,6},{8,9},{9,8},{10,11... | collective-permute-start | bytes 393224 | tf_op jit(solution)/shard_map/ppermute | solution.py:296
  33.7 2.4 %collective-permute-start.4 = (bf16[256,256]{1,0:T(8,128)(2,1)S(1)}, bf16[256,256]{1,0:T(8,128)(2,1)S(1)}, u32[]{:S(2)}, u32[]{:S(2)}) collective-permute-start(bf16[256,256]{1,0:T(8,128)(2,1)S(1)} %get-tuple-element.77), channel_id=1, source_target_pairs={{0,1},{1,0},{2,3},{3,2},{4,5},{5,4},{6,7},{7,6},{8,9},{9,8},{10,11... | collective-permute-start | bytes 393224 | tf_op jit(solution)/shard_map/ppermute | solution.py:296
  36.1 2.9 %collective-permute-start.5 = (bf16[256,256]{1,0:T(8,128)(2,1)S(1)}, bf16[256,256]{1,0:T(8,128)(2,1)S(1)}, u32[]{:S(2)}, u32[]{:S(2)}) collective-permute-start(bf16[256,256]{1,0:T(8,128)(2,1)S(1)} %get-tuple-element.80), channel_id=1, source_target_pairs={{0,1},{1,0},{2,3},{3,2},{4,5},{5,4},{6,7},{7,6},{8,9},{9,8},{10,11... | collective-permute-start | bytes 393224 | tf_op jit(solution)/shard_map/ppermute | solution.py:296
  36.6 2.4 %collective-permute-start.6 = (bf16[256,256]{1,0:T(8,128)(2,1)S(1)}, bf16[256,256]{1,0:T(8,128)(2,1)S(1)}, u32[]{:S(2)}, u32[]{:S(2)}) collective-permute-start(bf16[256,256]{1,0:T(8,128)(2,1)S(1)} %get-tuple-element.81), channel_id=1, source_target_pairs={{0,1},{1,0},{2,3},{3,2},{4,5},{5,4},{6,7},{7,6},{8,9},{9,8},{10,11... | collective-permute-start | bytes 393224 | tf_op jit(solution)/shard_map/ppermute | solution.py:296
  36.9 9.2 %collective-permute-start.8 = (bf16[512,256]{1,0:T(8,128)(2,1)S(1)}, bf16[512,256]{1,0:T(8,128)(2,1)S(1)}, u32[]{:S(2)}, u32[]{:S(2)}) collective-permute-start(bf16[512,256]{1,0:T(8,128)(2,1)S(1)} %get-tuple-element.84), channel_id=1, source_target_pairs={{0,2},{2,0},{1,3},{3,1},{4,6},{6,4},{5,7},{7,5},{8,10},{10,8},{9,1... | collective-permute-start | bytes 786440 | tf_op jit(solution)/shard_map/ppermute | solution.py:350
  39.1 12.4 %collective-permute-start.7 = (bf16[512,256]{1,0:T(8,128)(2,1)S(1)}, bf16[512,256]{1,0:T(8,128)(2,1)S(1)}, u32[]{:S(2)}, u32[]{:S(2)}) collective-permute-start(bf16[512,256]{1,0:T(8,128)(2,1)S(1)} %get-tuple-element.83), channel_id=1, source_target_pairs={{0,2},{2,0},{1,3},{3,1},{4,6},{6,4},{5,7},{7,5},{8,10},{10,8},{9,1... | collective-permute-start | bytes 786440 | tf_op jit(solution)/shard_map/ppermute | solution.py:353
  40.2 5.8 %copy-start.1 = (bf16[8,4,16,256]{3,2,1,0:T(8,128)(2,1)S(1)}, bf16[8,4,16,256]{3,2,1,0:T(8,128)(2,1)}, u32[]{:S(2)}) copy-start(bf16[8,4,16,256]{3,2,1,0:T(8,128)(2,1)} %param.11) | copy-start | bytes 786436
  40.2 5.8 %copy-start.2 = (f32[256]{0:T(256)S(1)}, f32[256]{0:T(256)}, u32[]{:S(2)}) copy-start(f32[256]{0:T(256)} %param.10) | copy-start | bytes 3076
  46.4 1.4 collective-permute-start.9
  46.5 1.5 collective-permute-start.10
  52.3 1.5 collective-permute-start.11
  96.3 9.0 %collective-permute-start.12 = (bf16[2048,128]{1,0:T(8,128)(2,1)}, bf16[2048,128]{1,0:T(8,128)(2,1)S(1)}, u32[]{:S(2)}, u32[]{:S(2)}) collective-permute-start(bf16[2048,128]{1,0:T(8,128)(2,1)} %get-tuple-element.121), channel_id=1, source_target_pairs={{5,1},{9,5},{10,2},{13,9},{14,6},{17,13},{18,10},{19,3},{21,17},{2... | collective-permute-start | bytes 1572872 | tf_op jit(solution)/shard_map/ppermute | solution.py:432
  97.0 8.3 %collective-permute-start.13 = (bf16[2048,128]{1,0:T(8,128)(2,1)S(1)}, bf16[2048,128]{1,0:T(8,128)(2,1)S(1)}, u32[]{:S(2)}, u32[]{:S(2)}) collective-permute-start(bf16[2048,128]{1,0:T(8,128)(2,1)S(1)} %get-tuple-element.123), channel_id=1, source_target_pairs={{1,5},{2,10},{3,19},{5,9},{6,14},{7,23},{9,13},{10,18},{11,27},{13... | collective-permute-start | bytes 1572872 | tf_op jit(solution)/shard_map/ppermute | solution.py:433
  98.7 25.1 %all-to-all-start.1 = ((bf16[4,232,256]{2,1,0:T(8,128)(2,1)}), bf16[4,232,256]{2,1,0:T(8,128)(2,1)S(1)}, u32[]{:S(2)}, u32[]{:S(2)}) async-start(bf16[4,232,256]{2,1,0:T(8,128)(2,1)} %shard_map.101), calls=%async_computation.1 | async-start | bytes 950272 | tf_op jit(solution)/shard_map/all_to_all | solution.py:434
  105.5 10.8 %collective-permute-start.14 = (bf16[2,512,128]{2,1,0:T(8,128)(2,1)S(1)}, bf16[2,512,128]{2,1,0:T(8,128)(2,1)S(1)}, u32[]{:S(2)}, u32[]{:S(2)}) collective-permute-start(bf16[2,512,128]{2,1,0:T(8,128)(2,1)S(1)} %get-tuple-element.125), channel_id=1, source_target_pairs={{0,1},{1,0},{2,3},{3,2},{4,5},{5,4},{6,7},{7,6},{8,9},{9,8},{10,11... | collective-permute-start | bytes 786440 | tf_op jit(solution)/shard_map/ppermute | solution.py:451
  116.4 11.2 %collective-permute-start.15 = (bf16[512,128]{1,0:T(8,128)(2,1)S(1)}, bf16[512,128]{1,0:T(8,128)(2,1)S(1)}, u32[]{:S(2)}, u32[]{:S(2)}) collective-permute-start(bf16[512,128]{1,0:T(8,128)(2,1)S(1)} %get-tuple-element.127), channel_id=1, source_target_pairs={{0,2},{2,0},{1,3},{3,1},{4,6},{6,4},{5,7},{7,5},{8,10},{10,8},{9,1... | collective-permute-start | bytes 393224 | tf_op jit(solution)/shard_map/ppermute | solution.py:453

commit v8 on v7

--- a/solution.py
+++ b/solution.py
@@ -130,17 +130,24 @@
     return (summed * jax.nn.sigmoid(summed)).astype(bf16)
 
 
-def first_output_kernel(row_ref, chip_sum, recv, bias, cot_mine, cot_pair, own_0, own_1, head):
+def first_output_kernel(row_ref, chip_sum, recv, bias, cot_mine, cot_pair, own_0, own_1):
     for k, own in enumerate((own_0, own_1)):
         cells = slice(k * (QUART // 2), (k + 1) * (QUART // 2))
         summed = chip_sum[cells] + recv[cells].astype(f32) + bias[...]
-        head[cells] = head_of(summed)
         own[...] = d_out_of(summed, jnp.where(row_ref[0] == 0, cot_mine[cells], cot_pair[cells]))
 
 
-def second_output_kernel(row_ref, chip_sum, recv, bias, cot_mine, cot_pair, head_a, own, head):
+def second_output_kernel(row_ref, chip_sum, recv, bias, cot_mine, cot_pair, own):
     summed = chip_sum[...] + recv[...].astype(f32) + bias[...]
     own[...] = d_out_of(summed, jnp.where(row_ref[0] == 1, cot_mine[...], cot_pair[...]))
+
+
+def first_head_kernel(chip_sum, recv, bias, head):
+    head[...] = head_of(chip_sum[...] + recv[...].astype(f32) + bias[...])
+
+
+def second_head_kernel(row_ref, chip_sum, recv, bias, head_a, head):
+    summed = chip_sum[...] + recv[...].astype(f32) + bias[...]
     head[...] = jnp.where(row_ref[0] == 0, head_a[...], head_of(summed))
 
 
@@ -361,15 +368,19 @@
     )
     recv_a, slope, hidden_t, features_t = lax.optimization_barrier((recv_a, slope, hidden_t, features_t))
 
-    *own_a, head_a = call(
+    own_a = call(
         first_output_kernel,
-        [((QUART // 2, F), bf16), ((QUART // 2, F), bf16), ((QUART, F), bf16)],
+        [((QUART // 2, F), bf16), ((QUART // 2, F), bf16)],
         [SMEM] + [VMEM] * 5,
         [],
         1000,
         row_arg, chip_a, recv_a, out_bias[None], cot_mine, cot_pair,
     )
     other_a = [lax.ppermute(part, "c", SWAP) for part in own_a]
+    (head_a,) = call(
+        first_head_kernel, [((QUART, F), bf16)], [VMEM] * 3, [], 1000, chip_a, recv_a, out_bias[None]
+    )
+    head_a, *other_a = lax.optimization_barrier((head_a, *other_a))
     d_pre_a, low_a, mid_a, high_a, taps_a, projs_a = call(
         back_first_kernel,
         [
@@ -386,15 +397,24 @@
         core_arg, *own_a, *other_a, slope, proj, weights_bwd, features_t, hidden_t,
     )
     recv_b, taps_a, d_pre_a = lax.optimization_barrier((recv_b, taps_a, d_pre_a))
-    own_b, head_out = call(
+    (own_b,) = call(
         second_output_kernel,
-        [((QUART, F), bf16), ((QUART, F), bf16)],
-        [SMEM] + [VMEM] * 6,
+        [((QUART, F), bf16)],
+        [SMEM] + [VMEM] * 5,
         [],
         1000,
-        row_arg, chip_b, recv_b, out_bias[None], cot_mine, cot_pair, head_a,
+        row_arg, chip_b, recv_b, out_bias[None], cot_mine, cot_pair,
     )
     other_b = lax.ppermute(own_b, "c", SWAP)
+    (head_out,) = call(
+        second_head_kernel,
+        [((QUART, F), bf16)],
+        [SMEM] + [VMEM] * 4,
+        [],
+        1000,
+        row_arg, chip_b, recv_b, out_bias[None], head_a,
+    )
+    head_out, other_b = lax.optimization_barrier((head_out, other_b))
     low, mid, high, grads = call(
         back_second_kernel,
         [((ROWS, C), bf16), ((ROWS, C), f32), ((ROWS, C), bf16), ((GRAD_ROWS, F), bf16)],

time: 164 us -> 164 us (level)
  blocking collectives: 76.7 us -> 74.9 us
    ppermute x4, starting transfers between devices: 6.72 us -> 3.32 us  [exchanged(): lax.ppermute(part, axis, SWAP)]
    ppermute x1, starting transfers between devices: 2.08 us -> 4.61 us  [shards(): recv_a = lax.ppermute(chip_send_a, 'yl', SWAP)]
    all_to_all x1, blocking collectives: 36.1 us -> 34 us  [shards(): part = lax.all_to_all(grads.reshape(near, share, F), NEAR, 0, 0, tiled=True)]
    ppermute x1, starting transfers between devices: 5.93 us -> 7.75 us  [shards(): cot_pair = lax.ppermute(cot_mine, 'yl', SWAP)]
    pallas_call x13 -> x15, Pallas kernels: 23 us -> 23.3 us  [call(): pl.pallas_call(kernel, out_shape=[jax.ShapeDtypeStruct(*o) for o in outs]...]
  transfers between devices with their start and end apart: 17 -> 17, of which waited for: 7 -> 7; matrix products, arithmetic and copies ran while one was open for 4% -> 4% of each run, Pallas kernels for 7% -> 8%
where the time goes in v8:
time: 164 us
  blocking collectives  74.9 us (46%)
  starting transfers between devices  44.5 us (27%)
  Pallas kernels  23.3 us (14%)
  waiting for transfers between devices  13.4 us (8%)
  local copies, waits for them, and re-layouts  4.17 us (3%)
  other arithmetic  2.69 us (2%)
    all_to_all x1, blocking collectives, shards(): part = lax.all_to_all(grads.reshape(near, share, F), NEAR, 0, 0, tiled=True)  34 us
    all_to_all x1, blocking collectives, shards(): total = lax.all_to_all(part, NEAR, 0, 0, tiled=True).reshape(GRAD_ROWS, F)  33.4 us
    pallas_call x15, Pallas kernels, call(): pl.pallas_call(kernel, out_shape=[jax.ShapeDtypeStruct(*o) for o in outs]...  23.3 us
    ppermute x1, starting transfers between devices, shards(): lax.ppermute(sent, 'c', SWAP)  10.4 us
    ppermute x1, starting transfers between devices, shards(): cot_pair = lax.ppermute(cot_mine, 'yl', SWAP)  7.75 us
    all_gather x1, blocking collectives, shards(): centre = lax.all_gather(features.reshape(QUART, C), BR, axis=0, tiled=True)  7.47 us
    ppermute x1, starting transfers between devices, shards(): recv = lax.ppermute(sent, 'yl', SWAP)  7.23 us
    all_to_all x1, starting transfers between devices, shards(): part = lax.all_to_all(part, FAR, 0, 0, tiled=True)  6.01 us
  transfers between devices with their start and end apart: 17, of which 7 were waited for; matrix products, arithmetic and copies ran while one was open for 4% of the time, Pallas kernels for 8%

profile of v8, /device:TPU:64, one launch (start us, length us, event | category | flops | bytes accessed | tf_op | source)
XLA Modules:
  0.0 164.0 jit_solution(16533907706149122862)
XLA Ops:
  0.6 7.5 %all_gather.3.centre = bf16[2048,128]{1,0:T(8,128)(2,1)S(1)} all-gather(bf16[512,128]{1,0:T(8,128)(2,1)} %bitcast.58), channel_id=1, replica_groups=mesh['zh'=4,'zl'=2,'x'=4,'yh'=2,'yl'=2,'c'=2] {'yl','c'}, dimensions={0}, use_global_device_ids=true | all-gather | bytes 655360 | tf_op jit(solution)/shard_map/all_gather | solution.py:317
  8.1 0.7 collective-permute-start
  8.8 0.7 collective-permute-start.1
  9.5 7.7 %collective-permute-start.2 = (bf16[512,256]{1,0:T(8,128)(2,1)}, bf16[512,256]{1,0:T(8,128)(2,1)S(1)}, u32[]{:S(2)}, u32[]{:S(2)}) collective-permute-start(bf16[512,256]{1,0:T(8,128)(2,1)} %bitcast.43), channel_id=1, source_target_pairs={{0,2},{2,0},{1,3},{3,1},{4,6},{6,4},{5,7},{7,5},{8,10},{10,8},{9,1... | collective-permute-start | bytes 786440 | tf_op jit(solution)/shard_map/ppermute | solution.py:325
  17.3 1.8 %fusion = (bf16[3,3,128,3,256]{4,2,0,3,1:T(8,128)(2,1)S(1)}, bf16[3,3,128,3,256]{4,2,3,1,0:T(8,128)(2,1)S(1)}) fusion(bf16[1,3,3,3,128,256]{5,4,3,2,1,0:T(8,128)(2,1)} %param.7, bf16[3,3,3]{2,1,0:T(4,128)(2,1)S(1)} %select_convert_fusion), kind=kLoop, calls=%fused_computation.1 | loop fusion | flops 884736 | bytes 5308470 | tf_op jit(solution)/shard_map/transpose | solution.py:330
  21.0 1.5 copy.17
  23.3 1.8 %shard_map.93.base = f32[2048,256]{1,0:T(8,128)S(1)} custom-call(bf16[2048,128]{1,0:T(8,128)(2,1)S(1)} %all_gather.3.centre, bf16[384,768]{1,0:T(8,128)(2,1)S(1)} %bitcast.46, f32[1,256]{1,0:T(1,128)S(1)} %copy-done.3), custom_call_target="tpu_custom_call" | custom-call | flops 1207959552 | bytes 1207959 | tf_op jit(solution)/shard_map/pallas_call | solution.py:280
  25.2 3.8 %collective-permute-done.2.cot_pair = bf16[512,256]{1,0:T(8,128)(2,1)S(1)} collective-permute-done((bf16[512,256]{1,0:T(8,128)(2,1)}, bf16[512,256]{1,0:T(8,128)(2,1)S(1)}, u32[]{:S(2)}, u32[]{:S(2)}) %collective-permute-start.2) | collective-permute-done | bytes 262176 | tf_op jit(solution)/shard_map/ppermute | solution.py:325
  28.9 2.3 %shard_map.95 = (f32[1024,256]{1,0:T(8,128)S(1)}, bf16[1024,256]{1,0:T(8,128)(2,1)S(1)}, f32[512,256]{1,0:T(8,128)S(1)}, bf16[256,256]{1,0:T(8,128)(2,1)S(1)}, bf16[256,256]{1,0:T(8,128)(2,1)S(1)}) custom-call(s32[1]{0:T(128)} %bitcast.1.core_ref, bf16[2048,128]{1,0:T(8,128)(2,1)S(1)} %collective-permute-done.below, ...), custom_call_target="tpu_custom_call" | custom-call | flops 1000 | bytes 1 | tf_op jit(solution)/shard_map/pallas_call | solution.py:280
  31.2 2.4 %collective-permute-start.4 = (bf16[256,256]{1,0:T(8,128)(2,1)S(1)}, bf16[256,256]{1,0:T(8,128)(2,1)S(1)}, u32[]{:S(2)}, u32[]{:S(2)}) collective-permute-start(bf16[256,256]{1,0:T(8,128)(2,1)S(1)} %get-tuple-element.79), channel_id=1, source_target_pairs={{0,1},{1,0},{2,3},{3,2},{4,5},{5,4},{6,7},{7,6},{8,9},{9,8},{10,11... | collective-permute-start | bytes 393224 | tf_op jit(solution)/shard_map/ppermute | solution.py:303
  33.8 2.3 %shard_map.94 = (f32[1024,256]{1,0:T(8,128)S(1)}, bf16[1024,256]{1,0:T(8,128)(2,1)S(1)}, f32[512,256]{1,0:T(8,128)S(1)}, bf16[256,256]{1,0:T(8,128)(2,1)S(1)}, bf16[256,256]{1,0:T(8,128)(2,1)S(1)}) custom-call(s32[1]{0:T(128)} %bitcast.1.core_ref, bf16[2048,128]{1,0:T(8,128)(2,1)S(1)} %collective-permute-done.below, ...), custom_call_target="tpu_custom_call" | custom-call | flops 1000 | bytes 1 | tf_op jit(solution)/shard_map/pallas_call | solution.py:280
  36.9 4.6 %collective-permute-start.8 = (bf16[512,256]{1,0:T(8,128)(2,1)S(1)}, bf16[512,256]{1,0:T(8,128)(2,1)S(1)}, u32[]{:S(2)}, u32[]{:S(2)}) collective-permute-start(bf16[512,256]{1,0:T(8,128)(2,1)S(1)} %get-tuple-element.86), channel_id=1, source_target_pairs={{0,2},{2,0},{1,3},{3,1},{4,6},{6,4},{5,7},{7,5},{8,10},{10,8},{9,1... | collective-permute-start | bytes 786440 | tf_op jit(solution)/shard_map/ppermute | solution.py:357
  41.6 1.2 collective-permute-start.7
  42.8 2.3 %shard_map.96 = (f32[2048,256]{1,0:T(8,128)S(1)}, bf16[256,2048]{1,0:T(8,128)(2,1)S(1)}, bf16[1152,2048]{1,0:T(8,128)(2,1)S(1)}) custom-call(bf16[2048,128]{1,0:T(8,128)(2,1)S(1)} %collective-permute-done.below, bf16[2048,128]{1,0:T(8,128)(2,1)S(1)} %all_gather.3.centre, bf16[2048,128]{1,0:T(8,128)(2,1)S(1)} %collective-permute-done.1.above, ...), custom_call_target="tpu_custom_call" | custom-call | flops 1000 | bytes 1 | tf_op jit(solution)/shard_map/pallas_call | solution.py:280
  45.1 3.5 %collective-permute-done.8.recv = bf16[512,256]{1,0:T(8,128)(2,1)S(1)} collective-permute-done((bf16[512,256]{1,0:T(8,128)(2,1)S(1)}, bf16[512,256]{1,0:T(8,128)(2,1)S(1)}, u32[]{:S(2)}, u32[]{:S(2)}) %collective-permute-start.8) | collective-permute-done | bytes 262176 | tf_op jit(solution)/shard_map/ppermute | solution.py:357
  49.5 0.7 collective-permute-done.9.other_0
  50.4 3.5 %shard_map.99 = (bf16[1088,256]{1,0:T(8,128)(2,1)S(1)}, bf16[768,128]{1,0:T(8,128)(2,1)S(1)}, f32[768,128]{1,0:T(8,128)S(1)}, bf16[768,128]{1,0:T(8,128)(2,1)S(1...) custom-call(s32[1]{0:T(128)} %bitcast.1.core_ref, bf16[256,256]{1,0:T(8,128)(2,1)S(1)} %get-tuple-element.96.own_0, ...), custom_call_target="tpu_custom_call" | custom-call | flops 1000 | bytes 1 | tf_op jit(solution)/shard_map/pallas_call | solution.py:280
  54.2 0.6 collective-permute-start.11
  54.8 0.8 shard_map.100
  56.0 6.3 %shard_map.102 = (bf16[2048,128]{1,0:T(8,128)(2,1)}, f32[2048,128]{1,0:T(8,128)S(1)}, bf16[2048,128]{1,0:T(8,128)(2,1)S(1)}, bf16[3712,256]{1,0:T(8,128)(2,1)S(1)}) custom-call(s32[1]{0:T(128)} %bitcast.1.core_ref, f32[1]{0:T(128)} %bitcast.10.keep_ref, bf16[512,256]{1,0:T(8,128)(2,1)S(1)} %shard_map.101.own, ...), custom_call_target="tpu_custom_call" | custom-call | flops 3623878656 | bytes 3623878 | tf_op jit(solution)/shard_map/pallas_call | solution.py:280
  62.3 34.0 %all_to_all.15.parts = bf16[16,232,256]{2,1,0:T(8,128)(2,1)S(1)} all-to-all(bf16[16,232,256]{2,1,0:T(8,128)(2,1)S(1)} %bitcast.42), channel_id=1, replica_groups=mesh['zh'=4,'zl'=2,'x'=4,'yh'=2,'yl'=2,'c'=2] {'zl','x','yh'}, dimensions={0} | all-to-all | bytes 3801088 | tf_op jit(solution)/shard_map/all_to_all | solution.py:438
  96.4 0.7 collective-permute-start.12
  97.1 0.7 collective-permute-start.13
  97.8 1.0 shard_map.103
  98.8 6.0 %all-to-all-start.1 = ((bf16[4,232,256]{2,1,0:T(8,128)(2,1)}), bf16[4,232,256]{2,1,0:T(8,128)(2,1)S(1)}, u32[]{:S(2)}, u32[]{:S(2)}) async-start(bf16[4,232,256]{2,1,0:T(8,128)(2,1)} %shard_map.103), calls=%async_computation.1 | async-start | bytes 950272 | tf_op jit(solution)/shard_map/all_to_all | solution.py:454
  105.1 10.4 %collective-permute-start.14 = (bf16[2,512,128]{2,1,0:T(8,128)(2,1)S(1)}, bf16[2,512,128]{2,1,0:T(8,128)(2,1)S(1)}, u32[]{:S(2)}, u32[]{:S(2)}) collective-permute-start(bf16[2,512,128]{2,1,0:T(8,128)(2,1)S(1)} %get-tuple-element.129), channel_id=1, source_target_pairs={{0,1},{1,0},{2,3},{3,2},{4,5},{5,4},{6,7},{7,6},{8,9},{9,8},{10,11... | collective-permute-start | bytes 786440 | tf_op jit(solution)/shard_map/ppermute | solution.py:471
  115.5 1.2 collective-permute-done.14.recv
  116.7 7.2 %collective-permute-start.15 = (bf16[512,128]{1,0:T(8,128)(2,1)S(1)}, bf16[512,128]{1,0:T(8,128)(2,1)S(1)}, u32[]{:S(2)}, u32[]{:S(2)}) collective-permute-start(bf16[512,128]{1,0:T(8,128)(2,1)S(1)} %get-tuple-element.131), channel_id=1, source_target_pairs={{0,2},{2,0},{1,3},{3,1},{4,6},{6,4},{5,7},{7,5},{8,10},{10,8},{9,1... | collective-permute-start | bytes 393224 | tf_op jit(solution)/shard_map/ppermute | solution.py:473
  124.0 3.7 %collective-permute-done.15 = bf16[512,128]{1,0:T(8,128)(2,1)S(1)} collective-permute-done((bf16[512,128]{1,0:T(8,128)(2,1)S(1)}, bf16[512,128]{1,0:T(8,128)(2,1)S(1)}, u32[]{:S(2)}, u32[]{:S(2)}) %collective-permute-start.15) | collective-permute-done | bytes 131104 | tf_op jit(solution)/shard_map/ppermute | solution.py:473
  127.7 0.7 add_convert_fusion
  128.4 33.4 %all_to_all.16 = bf16[16,232,256]{2,1,0:T(8,128)(2,1)S(1)} all-to-all(bf16[16,232,256]{2,1,0:T(8,128)(2,1)S(1)} %shard_map.104), channel_id=1, replica_groups=mesh['zh'=4,'zl'=2,'x'=4,'yh'=2,'yl'=2,'c'=2] {'zl','x','yh'}, dimensions={0} | all-to-all | bytes 3801088 | tf_op jit(solution)/shard_map/all_to_all | solution.py:476
  161.8 2.0 %shard_map.107 = (f32[3456,256]{1,0:T(8,128)}, f32[256,256]{1,0:T(8,128)}) custom-call(bf16[3712,256]{1,0:T(8,128)(2,1)S(1)} %bitcast.37), custom_call_target="tpu_custom_call" | custom-call | flops 1000000 | bytes 1000 | tf_op jit(solution)/shard_map/pallas_call | solution.py:280
  (43 shorter events, 5.9 us)
Async XLA Ops:
  8.1 20.8 %collective-permute-start = (bf16[2048,128]{1,0:T(8,128)(2,1)S(1)}, bf16[2048,128]{1,0:T(8,128)(2,1)S(1)}, u32[]{:S(2)}, u32[]{:S(2)}) collective-permute-start(bf16[2048,128]{1,0:T(8,128)(2,1)S(1)} %all_gather.3.centre), channel_id=1, source_target_pairs={{1,5},{2,10},{3,19},{5,9},{6,14},{7,23},{9,13},{10,18},{11,27},{13... | collective-permute-start | bytes 1572872 | tf_op jit(solution)/shard_map/ppermute | solution.py:323
  8.8 20.2 %collective-permute-start.1 = (bf16[2048,128]{1,0:T(8,128)(2,1)S(1)}, bf16[2048,128]{1,0:T(8,128)(2,1)S(1)}, u32[]{:S(2)}, u32[]{:S(2)}) collective-permute-start(bf16[2048,128]{1,0:T(8,128)(2,1)S(1)} %all_gather.3.centre), channel_id=1, source_target_pairs={{5,1},{9,5},{10,2},{13,9},{14,6},{17,13},{18,10},{19,3},{21,17},{2... | collective-permute-start | bytes 1572872 | tf_op jit(solution)/shard_map/ppermute | solution.py:324
  9.5 19.4 %collective-permute-start.2 = (bf16[512,256]{1,0:T(8,128)(2,1)}, bf16[512,256]{1,0:T(8,128)(2,1)S(1)}, u32[]{:S(2)}, u32[]{:S(2)}) collective-permute-start(bf16[512,256]{1,0:T(8,128)(2,1)} %bitcast.43), channel_id=1, source_target_pairs={{0,2},{2,0},{1,3},{3,1},{4,6},{6,4},{5,7},{7,5},{8,10},{10,8},{9,1... | collective-permute-start | bytes 786440 | tf_op jit(solution)/shard_map/ppermute | solution.py:325
  22.6 0.7 copy-start.3
  25.1 3.9 %copy-start = (bf16[1,256,256]{2,1,0:T(8,128)(2,1)S(1)}, bf16[1,256,256]{2,1,0:T(8,128)(2,1)}, u32[]{:S(2)}) copy-start(bf16[1,256,256]{2,1,0:T(8,128)(2,1)} %param.9) | copy-start | bytes 393220
  31.2 4.8 %collective-permute-start.4 = (bf16[256,256]{1,0:T(8,128)(2,1)S(1)}, bf16[256,256]{1,0:T(8,128)(2,1)S(1)}, u32[]{:S(2)}, u32[]{:S(2)}) collective-permute-start(bf16[256,256]{1,0:T(8,128)(2,1)S(1)} %get-tuple-element.79), channel_id=1, source_target_pairs={{0,1},{1,0},{2,3},{3,2},{4,5},{5,4},{6,7},{7,6},{8,9},{9,8},{10,11... | collective-permute-start | bytes 393224 | tf_op jit(solution)/shard_map/ppermute | solution.py:303
  33.7 2.4 %collective-permute-start.3 = (bf16[256,256]{1,0:T(8,128)(2,1)S(1)}, bf16[256,256]{1,0:T(8,128)(2,1)S(1)}, u32[]{:S(2)}, u32[]{:S(2)}) collective-permute-start(bf16[256,256]{1,0:T(8,128)(2,1)S(1)} %get-tuple-element.78), channel_id=1, source_target_pairs={{0,1},{1,0},{2,3},{3,2},{4,5},{5,4},{6,7},{7,6},{8,9},{9,8},{10,11... | collective-permute-start | bytes 393224 | tf_op jit(solution)/shard_map/ppermute | solution.py:303
  36.1 5.4 %collective-permute-start.6 = (bf16[256,256]{1,0:T(8,128)(2,1)S(1)}, bf16[256,256]{1,0:T(8,128)(2,1)S(1)}, u32[]{:S(2)}, u32[]{:S(2)}) collective-permute-start(bf16[256,256]{1,0:T(8,128)(2,1)S(1)} %get-tuple-element.83), channel_id=1, source_target_pairs={{0,1},{1,0},{2,3},{3,2},{4,5},{5,4},{6,7},{7,6},{8,9},{9,8},{10,11... | collective-permute-start | bytes 393224 | tf_op jit(solution)/shard_map/ppermute | solution.py:303
  36.6 4.9 %collective-permute-start.5 = (bf16[256,256]{1,0:T(8,128)(2,1)S(1)}, bf16[256,256]{1,0:T(8,128)(2,1)S(1)}, u32[]{:S(2)}, u32[]{:S(2)}) collective-permute-start(bf16[256,256]{1,0:T(8,128)(2,1)S(1)} %get-tuple-element.82), channel_id=1, source_target_pairs={{0,1},{1,0},{2,3},{3,2},{4,5},{5,4},{6,7},{7,6},{8,9},{9,8},{10,11... | collective-permute-start | bytes 393224 | tf_op jit(solution)/shard_map/ppermute | solution.py:303
  36.9 11.7 %collective-permute-start.8 = (bf16[512,256]{1,0:T(8,128)(2,1)S(1)}, bf16[512,256]{1,0:T(8,128)(2,1)S(1)}, u32[]{:S(2)}, u32[]{:S(2)}) collective-permute-start(bf16[512,256]{1,0:T(8,128)(2,1)S(1)} %get-tuple-element.86), channel_id=1, source_target_pairs={{0,2},{2,0},{1,3},{3,1},{4,6},{6,4},{5,7},{7,5},{8,10},{10,8},{9,1... | collective-permute-start | bytes 786440 | tf_op jit(solution)/shard_map/ppermute | solution.py:357
  41.6 12.3 %collective-permute-start.7 = (bf16[512,256]{1,0:T(8,128)(2,1)S(1)}, bf16[512,256]{1,0:T(8,128)(2,1)S(1)}, u32[]{:S(2)}, u32[]{:S(2)}) collective-permute-start(bf16[512,256]{1,0:T(8,128)(2,1)S(1)} %get-tuple-element.85), channel_id=1, source_target_pairs={{0,2},{2,0},{1,3},{3,1},{4,6},{6,4},{5,7},{7,5},{8,10},{10,8},{9,1... | collective-permute-start | bytes 786440 | tf_op jit(solution)/shard_map/ppermute | solution.py:360
  42.8 5.8 %copy-start.1 = (bf16[8,4,16,256]{3,2,1,0:T(8,128)(2,1)S(1)}, bf16[8,4,16,256]{3,2,1,0:T(8,128)(2,1)}, u32[]{:S(2)}) copy-start(bf16[8,4,16,256]{3,2,1,0:T(8,128)(2,1)} %param.11) | copy-start | bytes 786436
  42.8 5.8 %copy-start.2 = (f32[256]{0:T(256)S(1)}, f32[256]{0:T(256)}, u32[]{:S(2)}) copy-start(f32[256]{0:T(256)} %param.10) | copy-start | bytes 3076
  48.8 1.4 collective-permute-start.9
  48.9 1.5 collective-permute-start.10
  54.2 1.8 %collective-permute-start.11 = (bf16[512,256]{1,0:T(8,128)(2,1)S(1)}, bf16[512,256]{1,0:T(8,128)(2,1)S(1)}, u32[]{:S(2)}, u32[]{:S(2)}) collective-permute-start(bf16[512,256]{1,0:T(8,128)(2,1)S(1)} %shard_map.101.own), channel_id=1, source_target_pairs={{0,1},{1,0},{2,3},{3,2},{4,5},{5,4},{6,7},{7,6},{8,9},{9,8},{10,11... | collective-permute-start | bytes 786440 | tf_op jit(solution)/shard_map/ppermute | solution.py:408
  96.4 8.4 %collective-permute-start.12 = (bf16[2048,128]{1,0:T(8,128)(2,1)}, bf16[2048,128]{1,0:T(8,128)(2,1)S(1)}, u32[]{:S(2)}, u32[]{:S(2)}) collective-permute-start(bf16[2048,128]{1,0:T(8,128)(2,1)} %get-tuple-element.125), channel_id=1, source_target_pairs={{5,1},{9,5},{10,2},{13,9},{14,6},{17,13},{18,10},{19,3},{21,17},{2... | collective-permute-start | bytes 1572872 | tf_op jit(solution)/shard_map/ppermute | solution.py:452
  97.1 7.8 %collective-permute-start.13 = (bf16[2048,128]{1,0:T(8,128)(2,1)S(1)}, bf16[2048,128]{1,0:T(8,128)(2,1)S(1)}, u32[]{:S(2)}, u32[]{:S(2)}) collective-permute-start(bf16[2048,128]{1,0:T(8,128)(2,1)S(1)} %get-tuple-element.127), channel_id=1, source_target_pairs={{1,5},{2,10},{3,19},{5,9},{6,14},{7,23},{9,13},{10,18},{11,27},{13... | collective-permute-start | bytes 1572872 | tf_op jit(solution)/shard_map/ppermute | solution.py:453
  98.8 25.1 %all-to-all-start.1 = ((bf16[4,232,256]{2,1,0:T(8,128)(2,1)}), bf16[4,232,256]{2,1,0:T(8,128)(2,1)S(1)}, u32[]{:S(2)}, u32[]{:S(2)}) async-start(bf16[4,232,256]{2,1,0:T(8,128)(2,1)} %shard_map.103), calls=%async_computation.1 | async-start | bytes 950272 | tf_op jit(solution)/shard_map/all_to_all | solution.py:454
  105.1 11.6 %collective-permute-start.14 = (bf16[2,512,128]{2,1,0:T(8,128)(2,1)S(1)}, bf16[2,512,128]{2,1,0:T(8,128)(2,1)S(1)}, u32[]{:S(2)}, u32[]{:S(2)}) collective-permute-start(bf16[2,512,128]{2,1,0:T(8,128)(2,1)S(1)} %get-tuple-element.129), channel_id=1, source_target_pairs={{0,1},{1,0},{2,3},{3,2},{4,5},{5,4},{6,7},{7,6},{8,9},{9,8},{10,11... | collective-permute-start | bytes 786440 | tf_op jit(solution)/shard_map/ppermute | solution.py:471
  116.7 11.0 %collective-permute-start.15 = (bf16[512,128]{1,0:T(8,128)(2,1)S(1)}, bf16[512,128]{1,0:T(8,128)(2,1)S(1)}, u32[]{:S(2)}, u32[]{:S(2)}) collective-permute-start(bf16[512,128]{1,0:T(8,128)(2,1)S(1)} %get-tuple-element.131), channel_id=1, source_target_pairs={{0,2},{2,0},{1,3},{3,1},{4,6},{6,4},{5,7},{7,5},{8,10},{10,8},{9,1... | collective-permute-start | bytes 393224 | tf_op jit(solution)/shard_map/ppermute | solution.py:473

commit v9 on v8

--- a/solution.py
+++ b/solution.py
@@ -263,14 +263,14 @@
 
 def widen_kernel(total, taps_out, proj_out, wide, sems):
     moves = []
-    for k in range(4):
-        first = k * TAPS // 4
-        last = first + TAPS // 4
+    for k in range(8):
+        first = k * TAPS // 8
+        last = first + TAPS // 8
         wide[first:last] = total[first:last].astype(f32)
         moves.append(pltpu.make_async_copy(wide.at[first:last], taps_out.at[first:last], sems.at[k]))
         moves[-1].start()
     wide[TAPS:] = total[TAPS:].astype(f32)
-    moves.append(pltpu.make_async_copy(wide.at[TAPS:], proj_out, sems.at[4]))
+    moves.append(pltpu.make_async_copy(wide.at[TAPS:], proj_out, sems.at[8]))
     moves[-1].start()
     for move in moves:
         move.wait()
@@ -478,7 +478,7 @@
         widen_kernel,
         [((TAPS, F), f32), ((F, F), f32)],
         [VMEM],
-        [pltpu.VMEM((GRAD_ROWS, F), f32), pltpu.SemaphoreType.DMA((5,))],
+        [pltpu.VMEM((GRAD_ROWS, F), f32), pltpu.SemaphoreType.DMA((9,))],
         1_000_000,
         total,
         place=HBM,

time: 164 us -> 164 us (level)
  no operation moved by 1% of the time
where the time goes in v9:
time: 164 us
  blocking collectives  74.9 us (46%)
  starting transfers between devices  44.5 us (27%)
  Pallas kernels  23.3 us (14%)
  waiting for transfers between devices  13.4 us (8%)
  local copies, waits for them, and re-layouts  4.17 us (3%)
  other arithmetic  2.69 us (2%)
    all_to_all x1, blocking collectives, shards(): part = lax.all_to_all(grads.reshape(near, share, F), NEAR, 0, 0, tiled=True)  34 us
    all_to_all x1, blocking collectives, shards(): total = lax.all_to_all(part, NEAR, 0, 0, tiled=True).reshape(GRAD_ROWS, F)  33.4 us
    pallas_call x15, Pallas kernels, call(): pl.pallas_call(kernel, out_shape=[jax.ShapeDtypeStruct(*o) for o in outs]...  23.3 us
    ppermute x1, starting transfers between devices, shards(): lax.ppermute(sent, 'c', SWAP)  10.4 us
    ppermute x1, starting transfers between devices, shards(): cot_pair = lax.ppermute(cot_mine, 'yl', SWAP)  7.75 us
    all_gather x1, blocking collectives, shards(): centre = lax.all_gather(features.reshape(QUART, C), BR, axis=0, tiled=True)  7.47 us
    ppermute x1, starting transfers between devices, shards(): recv = lax.ppermute(sent, 'yl', SWAP)  7.23 us
    all_to_all x1, starting transfers between devices, shards(): part = lax.all_to_all(part, FAR, 0, 0, tiled=True)  6.01 us
  transfers between devices with their start and end apart: 17, of which 7 were waited for; matrix products, arithmetic and copies ran while one was open for 4% of the time, Pallas kernels for 8%

profile of v9, /device:TPU:64, one launch (start us, length us, event | category | flops | bytes accessed | tf_op | source)
XLA Modules:
  0.0 164.0 jit_solution(16830748070545970367)
XLA Ops:
  0.6 7.5 %all_gather.3.centre = bf16[2048,128]{1,0:T(8,128)(2,1)S(1)} all-gather(bf16[512,128]{1,0:T(8,128)(2,1)} %bitcast.58), channel_id=1, replica_groups=mesh['zh'=4,'zl'=2,'x'=4,'yh'=2,'yl'=2,'c'=2] {'yl','c'}, dimensions={0}, use_global_device_ids=true | all-gather | bytes 655360 | tf_op jit(solution)/shard_map/all_gather | solution.py:317
  8.1 0.7 collective-permute-start
  8.8 0.7 collective-permute-start.1
  9.5 7.7 %collective-permute-start.2 = (bf16[512,256]{1,0:T(8,128)(2,1)}, bf16[512,256]{1,0:T(8,128)(2,1)S(1)}, u32[]{:S(2)}, u32[]{:S(2)}) collective-permute-start(bf16[512,256]{1,0:T(8,128)(2,1)} %bitcast.43), channel_id=1, source_target_pairs={{0,2},{2,0},{1,3},{3,1},{4,6},{6,4},{5,7},{7,5},{8,10},{10,8},{9,1... | collective-permute-start | bytes 786440 | tf_op jit(solution)/shard_map/ppermute | solution.py:325
  17.3 1.8 %fusion = (bf16[3,3,128,3,256]{4,2,0,3,1:T(8,128)(2,1)S(1)}, bf16[3,3,128,3,256]{4,2,3,1,0:T(8,128)(2,1)S(1)}) fusion(bf16[1,3,3,3,128,256]{5,4,3,2,1,0:T(8,128)(2,1)} %param.7, bf16[3,3,3]{2,1,0:T(4,128)(2,1)S(1)} %select_convert_fusion), kind=kLoop, calls=%fused_computation.1 | loop fusion | flops 884736 | bytes 5308470 | tf_op jit(solution)/shard_map/transpose | solution.py:330
  21.0 1.5 copy.17
  23.3 1.8 %shard_map.93.base = f32[2048,256]{1,0:T(8,128)S(1)} custom-call(bf16[2048,128]{1,0:T(8,128)(2,1)S(1)} %all_gather.3.centre, bf16[384,768]{1,0:T(8,128)(2,1)S(1)} %bitcast.46, f32[1,256]{1,0:T(1,128)S(1)} %copy-done.3), custom_call_target="tpu_custom_call" | custom-call | flops 1207959552 | bytes 1207959 | tf_op jit(solution)/shard_map/pallas_call | solution.py:280
  25.2 3.8 %collective-permute-done.2.cot_pair = bf16[512,256]{1,0:T(8,128)(2,1)S(1)} collective-permute-done((bf16[512,256]{1,0:T(8,128)(2,1)}, bf16[512,256]{1,0:T(8,128)(2,1)S(1)}, u32[]{:S(2)}, u32[]{:S(2)}) %collective-permute-start.2) | collective-permute-done | bytes 262176 | tf_op jit(solution)/shard_map/ppermute | solution.py:325
  28.9 2.3 %shard_map.95 = (f32[1024,256]{1,0:T(8,128)S(1)}, bf16[1024,256]{1,0:T(8,128)(2,1)S(1)}, f32[512,256]{1,0:T(8,128)S(1)}, bf16[256,256]{1,0:T(8,128)(2,1)S(1)}, bf16[256,256]{1,0:T(8,128)(2,1)S(1)}) custom-call(s32[1]{0:T(128)} %bitcast.1.core_ref, bf16[2048,128]{1,0:T(8,128)(2,1)S(1)} %collective-permute-done.below, ...), custom_call_target="tpu_custom_call" | custom-call | flops 1000 | bytes 1 | tf_op jit(solution)/shard_map/pallas_call | solution.py:280
  31.2 2.4 %collective-permute-start.4 = (bf16[256,256]{1,0:T(8,128)(2,1)S(1)}, bf16[256,256]{1,0:T(8,128)(2,1)S(1)}, u32[]{:S(2)}, u32[]{:S(2)}) collective-permute-start(bf16[256,256]{1,0:T(8,128)(2,1)S(1)} %get-tuple-element.79), channel_id=1, source_target_pairs={{0,1},{1,0},{2,3},{3,2},{4,5},{5,4},{6,7},{7,6},{8,9},{9,8},{10,11... | collective-permute-start | bytes 393224 | tf_op jit(solution)/shard_map/ppermute | solution.py:303
  33.8 2.3 %shard_map.94 = (f32[1024,256]{1,0:T(8,128)S(1)}, bf16[1024,256]{1,0:T(8,128)(2,1)S(1)}, f32[512,256]{1,0:T(8,128)S(1)}, bf16[256,256]{1,0:T(8,128)(2,1)S(1)}, bf16[256,256]{1,0:T(8,128)(2,1)S(1)}) custom-call(s32[1]{0:T(128)} %bitcast.1.core_ref, bf16[2048,128]{1,0:T(8,128)(2,1)S(1)} %collective-permute-done.below, ...), custom_call_target="tpu_custom_call" | custom-call | flops 1000 | bytes 1 | tf_op jit(solution)/shard_map/pallas_call | solution.py:280
  36.9 4.6 %collective-permute-start.8 = (bf16[512,256]{1,0:T(8,128)(2,1)S(1)}, bf16[512,256]{1,0:T(8,128)(2,1)S(1)}, u32[]{:S(2)}, u32[]{:S(2)}) collective-permute-start(bf16[512,256]{1,0:T(8,128)(2,1)S(1)} %get-tuple-element.86), channel_id=1, source_target_pairs={{0,2},{2,0},{1,3},{3,1},{4,6},{6,4},{5,7},{7,5},{8,10},{10,8},{9,1... | collective-permute-start | bytes 786440 | tf_op jit(solution)/shard_map/ppermute | solution.py:357
  41.6 1.2 collective-permute-start.7
  42.8 2.3 %shard_map.96 = (f32[2048,256]{1,0:T(8,128)S(1)}, bf16[256,2048]{1,0:T(8,128)(2,1)S(1)}, bf16[1152,2048]{1,0:T(8,128)(2,1)S(1)}) custom-call(bf16[2048,128]{1,0:T(8,128)(2,1)S(1)} %collective-permute-done.below, bf16[2048,128]{1,0:T(8,128)(2,1)S(1)} %all_gather.3.centre, bf16[2048,128]{1,0:T(8,128)(2,1)S(1)} %collective-permute-done.1.above, ...), custom_call_target="tpu_custom_call" | custom-call | flops 1000 | bytes 1 | tf_op jit(solution)/shard_map/pallas_call | solution.py:280
  45.1 3.5 %collective-permute-done.8.recv = bf16[512,256]{1,0:T(8,128)(2,1)S(1)} collective-permute-done((bf16[512,256]{1,0:T(8,128)(2,1)S(1)}, bf16[512,256]{1,0:T(8,128)(2,1)S(1)}, u32[]{:S(2)}, u32[]{:S(2)}) %collective-permute-start.8) | collective-permute-done | bytes 262176 | tf_op jit(solution)/shard_map/ppermute | solution.py:357
  49.5 0.7 collective-permute-done.9.other_0
  50.4 3.5 %shard_map.99 = (bf16[1088,256]{1,0:T(8,128)(2,1)S(1)}, bf16[768,128]{1,0:T(8,128)(2,1)S(1)}, f32[768,128]{1,0:T(8,128)S(1)}, bf16[768,128]{1,0:T(8,128)(2,1)S(1...) custom-call(s32[1]{0:T(128)} %bitcast.1.core_ref, bf16[256,256]{1,0:T(8,128)(2,1)S(1)} %get-tuple-element.96.own_0, ...), custom_call_target="tpu_custom_call" | custom-call | flops 1000 | bytes 1 | tf_op jit(solution)/shard_map/pallas_call | solution.py:280
  54.2 0.6 collective-permute-start.11
  54.8 0.8 shard_map.100
  56.0 6.3 %shard_map.102 = (bf16[2048,128]{1,0:T(8,128)(2,1)}, f32[2048,128]{1,0:T(8,128)S(1)}, bf16[2048,128]{1,0:T(8,128)(2,1)S(1)}, bf16[3712,256]{1,0:T(8,128)(2,1)S(1)}) custom-call(s32[1]{0:T(128)} %bitcast.1.core_ref, f32[1]{0:T(128)} %bitcast.10.keep_ref, bf16[512,256]{1,0:T(8,128)(2,1)S(1)} %shard_map.101.own, ...), custom_call_target="tpu_custom_call" | custom-call | flops 3623878656 | bytes 3623878 | tf_op jit(solution)/shard_map/pallas_call | solution.py:280
  62.3 34.0 %all_to_all.15.parts = bf16[16,232,256]{2,1,0:T(8,128)(2,1)S(1)} all-to-all(bf16[16,232,256]{2,1,0:T(8,128)(2,1)S(1)} %bitcast.42), channel_id=1, replica_groups=mesh['zh'=4,'zl'=2,'x'=4,'yh'=2,'yl'=2,'c'=2] {'zl','x','yh'}, dimensions={0} | all-to-all | bytes 3801088 | tf_op jit(solution)/shard_map/all_to_all | solution.py:438
  96.4 0.7 collective-permute-start.12
  97.1 0.7 collective-permute-start.13
  97.8 1.0 shard_map.103
  98.8 6.0 %all-to-all-start.1 = ((bf16[4,232,256]{2,1,0:T(8,128)(2,1)}), bf16[4,232,256]{2,1,0:T(8,128)(2,1)S(1)}, u32[]{:S(2)}, u32[]{:S(2)}) async-start(bf16[4,232,256]{2,1,0:T(8,128)(2,1)} %shard_map.103), calls=%async_computation.1 | async-start | bytes 950272 | tf_op jit(solution)/shard_map/all_to_all | solution.py:454
  105.1 10.4 %collective-permute-start.14 = (bf16[2,512,128]{2,1,0:T(8,128)(2,1)S(1)}, bf16[2,512,128]{2,1,0:T(8,128)(2,1)S(1)}, u32[]{:S(2)}, u32[]{:S(2)}) collective-permute-start(bf16[2,512,128]{2,1,0:T(8,128)(2,1)S(1)} %get-tuple-element.129), channel_id=1, source_target_pairs={{0,1},{1,0},{2,3},{3,2},{4,5},{5,4},{6,7},{7,6},{8,9},{9,8},{10,11... | collective-permute-start | bytes 786440 | tf_op jit(solution)/shard_map/ppermute | solution.py:471
  115.5 1.2 collective-permute-done.14.recv
  116.7 7.2 %collective-permute-start.15 = (bf16[512,128]{1,0:T(8,128)(2,1)S(1)}, bf16[512,128]{1,0:T(8,128)(2,1)S(1)}, u32[]{:S(2)}, u32[]{:S(2)}) collective-permute-start(bf16[512,128]{1,0:T(8,128)(2,1)S(1)} %get-tuple-element.131), channel_id=1, source_target_pairs={{0,2},{2,0},{1,3},{3,1},{4,6},{6,4},{5,7},{7,5},{8,10},{10,8},{9,1... | collective-permute-start | bytes 393224 | tf_op jit(solution)/shard_map/ppermute | solution.py:473
  124.0 3.7 %collective-permute-done.15 = bf16[512,128]{1,0:T(8,128)(2,1)S(1)} collective-permute-done((bf16[512,128]{1,0:T(8,128)(2,1)S(1)}, bf16[512,128]{1,0:T(8,128)(2,1)S(1)}, u32[]{:S(2)}, u32[]{:S(2)}) %collective-permute-start.15) | collective-permute-done | bytes 131104 | tf_op jit(solution)/shard_map/ppermute | solution.py:473
  127.7 0.7 add_convert_fusion
  128.4 33.4 %all_to_all.16 = bf16[16,232,256]{2,1,0:T(8,128)(2,1)S(1)} all-to-all(bf16[16,232,256]{2,1,0:T(8,128)(2,1)S(1)} %shard_map.104), channel_id=1, replica_groups=mesh['zh'=4,'zl'=2,'x'=4,'yh'=2,'yl'=2,'c'=2] {'zl','x','yh'}, dimensions={0} | all-to-all | bytes 3801088 | tf_op jit(solution)/shard_map/all_to_all | solution.py:476
  161.8 2.0 %shard_map.107 = (f32[3456,256]{1,0:T(8,128)}, f32[256,256]{1,0:T(8,128)}) custom-call(bf16[3712,256]{1,0:T(8,128)(2,1)S(1)} %bitcast.37), custom_call_target="tpu_custom_call" | custom-call | flops 1000000 | bytes 1000 | tf_op jit(solution)/shard_map/pallas_call | solution.py:280
  (43 shorter events, 5.9 us)
Async XLA Ops:
  8.1 20.8 %collective-permute-start = (bf16[2048,128]{1,0:T(8,128)(2,1)S(1)}, bf16[2048,128]{1,0:T(8,128)(2,1)S(1)}, u32[]{:S(2)}, u32[]{:S(2)}) collective-permute-start(bf16[2048,128]{1,0:T(8,128)(2,1)S(1)} %all_gather.3.centre), channel_id=1, source_target_pairs={{1,5},{2,10},{3,19},{5,9},{6,14},{7,23},{9,13},{10,18},{11,27},{13... | collective-permute-start | bytes 1572872 | tf_op jit(solution)/shard_map/ppermute | solution.py:323
  8.8 20.2 %collective-permute-start.1 = (bf16[2048,128]{1,0:T(8,128)(2,1)S(1)}, bf16[2048,128]{1,0:T(8,128)(2,1)S(1)}, u32[]{:S(2)}, u32[]{:S(2)}) collective-permute-start(bf16[2048,128]{1,0:T(8,128)(2,1)S(1)} %all_gather.3.centre), channel_id=1, source_target_pairs={{5,1},{9,5},{10,2},{13,9},{14,6},{17,13},{18,10},{19,3},{21,17},{2... | collective-permute-start | bytes 1572872 | tf_op jit(solution)/shard_map/ppermute | solution.py:324
  9.5 19.4 %collective-permute-start.2 = (bf16[512,256]{1,0:T(8,128)(2,1)}, bf16[512,256]{1,0:T(8,128)(2,1)S(1)}, u32[]{:S(2)}, u32[]{:S(2)}) collective-permute-start(bf16[512,256]{1,0:T(8,128)(2,1)} %bitcast.43), channel_id=1, source_target_pairs={{0,2},{2,0},{1,3},{3,1},{4,6},{6,4},{5,7},{7,5},{8,10},{10,8},{9,1... | collective-permute-start | bytes 786440 | tf_op jit(solution)/shard_map/ppermute | solution.py:325
  22.6 0.7 copy-start.3
  25.1 3.9 %copy-start = (bf16[1,256,256]{2,1,0:T(8,128)(2,1)S(1)}, bf16[1,256,256]{2,1,0:T(8,128)(2,1)}, u32[]{:S(2)}) copy-start(bf16[1,256,256]{2,1,0:T(8,128)(2,1)} %param.9) | copy-start | bytes 393220
  31.2 4.8 %collective-permute-start.4 = (bf16[256,256]{1,0:T(8,128)(2,1)S(1)}, bf16[256,256]{1,0:T(8,128)(2,1)S(1)}, u32[]{:S(2)}, u32[]{:S(2)}) collective-permute-start(bf16[256,256]{1,0:T(8,128)(2,1)S(1)} %get-tuple-element.79), channel_id=1, source_target_pairs={{0,1},{1,0},{2,3},{3,2},{4,5},{5,4},{6,7},{7,6},{8,9},{9,8},{10,11... | collective-permute-start | bytes 393224 | tf_op jit(solution)/shard_map/ppermute | solution.py:303
  33.7 2.4 %collective-permute-start.3 = (bf16[256,256]{1,0:T(8,128)(2,1)S(1)}, bf16[256,256]{1,0:T(8,128)(2,1)S(1)}, u32[]{:S(2)}, u32[]{:S(2)}) collective-permute-start(bf16[256,256]{1,0:T(8,128)(2,1)S(1)} %get-tuple-element.78), channel_id=1, source_target_pairs={{0,1},{1,0},{2,3},{3,2},{4,5},{5,4},{6,7},{7,6},{8,9},{9,8},{10,11... | collective-permute-start | bytes 393224 | tf_op jit(solution)/shard_map/ppermute | solution.py:303
  36.1 5.4 %collective-permute-start.6 = (bf16[256,256]{1,0:T(8,128)(2,1)S(1)}, bf16[256,256]{1,0:T(8,128)(2,1)S(1)}, u32[]{:S(2)}, u32[]{:S(2)}) collective-permute-start(bf16[256,256]{1,0:T(8,128)(2,1)S(1)} %get-tuple-element.83), channel_id=1, source_target_pairs={{0,1},{1,0},{2,3},{3,2},{4,5},{5,4},{6,7},{7,6},{8,9},{9,8},{10,11... | collective-permute-start | bytes 393224 | tf_op jit(solution)/shard_map/ppermute | solution.py:303
  36.6 4.9 %collective-permute-start.5 = (bf16[256,256]{1,0:T(8,128)(2,1)S(1)}, bf16[256,256]{1,0:T(8,128)(2,1)S(1)}, u32[]{:S(2)}, u32[]{:S(2)}) collective-permute-start(bf16[256,256]{1,0:T(8,128)(2,1)S(1)} %get-tuple-element.82), channel_id=1, source_target_pairs={{0,1},{1,0},{2,3},{3,2},{4,5},{5,4},{6,7},{7,6},{8,9},{9,8},{10,11... | collective-permute-start | bytes 393224 | tf_op jit(solution)/shard_map/ppermute | solution.py:303
  36.9 11.7 %collective-permute-start.8 = (bf16[512,256]{1,0:T(8,128)(2,1)S(1)}, bf16[512,256]{1,0:T(8,128)(2,1)S(1)}, u32[]{:S(2)}, u32[]{:S(2)}) collective-permute-start(bf16[512,256]{1,0:T(8,128)(2,1)S(1)} %get-tuple-element.86), channel_id=1, source_target_pairs={{0,2},{2,0},{1,3},{3,1},{4,6},{6,4},{5,7},{7,5},{8,10},{10,8},{9,1... | collective-permute-start | bytes 786440 | tf_op jit(solution)/shard_map/ppermute | solution.py:357
  41.6 12.3 %collective-permute-start.7 = (bf16[512,256]{1,0:T(8,128)(2,1)S(1)}, bf16[512,256]{1,0:T(8,128)(2,1)S(1)}, u32[]{:S(2)}, u32[]{:S(2)}) collective-permute-start(bf16[512,256]{1,0:T(8,128)(2,1)S(1)} %get-tuple-element.85), channel_id=1, source_target_pairs={{0,2},{2,0},{1,3},{3,1},{4,6},{6,4},{5,7},{7,5},{8,10},{10,8},{9,1... | collective-permute-start | bytes 786440 | tf_op jit(solution)/shard_map/ppermute | solution.py:360
  42.8 5.8 %copy-start.1 = (bf16[8,4,16,256]{3,2,1,0:T(8,128)(2,1)S(1)}, bf16[8,4,16,256]{3,2,1,0:T(8,128)(2,1)}, u32[]{:S(2)}) copy-start(bf16[8,4,16,256]{3,2,1,0:T(8,128)(2,1)} %param.11) | copy-start | bytes 786436
  42.8 5.8 %copy-start.2 = (f32[256]{0:T(256)S(1)}, f32[256]{0:T(256)}, u32[]{:S(2)}) copy-start(f32[256]{0:T(256)} %param.10) | copy-start | bytes 3076
  48.8 1.4 collective-permute-start.9
  48.9 1.5 collective-permute-start.10
  54.2 1.8 %collective-permute-start.11 = (bf16[512,256]{1,0:T(8,128)(2,1)S(1)}, bf16[512,256]{1,0:T(8,128)(2,1)S(1)}, u32[]{:S(2)}, u32[]{:S(2)}) collective-permute-start(bf16[512,256]{1,0:T(8,128)(2,1)S(1)} %shard_map.101.own), channel_id=1, source_target_pairs={{0,1},{1,0},{2,3},{3,2},{4,5},{5,4},{6,7},{7,6},{8,9},{9,8},{10,11... | collective-permute-start | bytes 786440 | tf_op jit(solution)/shard_map/ppermute | solution.py:408
  96.4 8.4 %collective-permute-start.12 = (bf16[2048,128]{1,0:T(8,128)(2,1)}, bf16[2048,128]{1,0:T(8,128)(2,1)S(1)}, u32[]{:S(2)}, u32[]{:S(2)}) collective-permute-start(bf16[2048,128]{1,0:T(8,128)(2,1)} %get-tuple-element.125), channel_id=1, source_target_pairs={{5,1},{9,5},{10,2},{13,9},{14,6},{17,13},{18,10},{19,3},{21,17},{2... | collective-permute-start | bytes 1572872 | tf_op jit(solution)/shard_map/ppermute | solution.py:452
  97.1 7.8 %collective-permute-start.13 = (bf16[2048,128]{1,0:T(8,128)(2,1)S(1)}, bf16[2048,128]{1,0:T(8,128)(2,1)S(1)}, u32[]{:S(2)}, u32[]{:S(2)}) collective-permute-start(bf16[2048,128]{1,0:T(8,128)(2,1)S(1)} %get-tuple-element.127), channel_id=1, source_target_pairs={{1,5},{2,10},{3,19},{5,9},{6,14},{7,23},{9,13},{10,18},{11,27},{13... | collective-permute-start | bytes 1572872 | tf_op jit(solution)/shard_map/ppermute | solution.py:453
  98.8 25.1 %all-to-all-start.1 = ((bf16[4,232,256]{2,1,0:T(8,128)(2,1)}), bf16[4,232,256]{2,1,0:T(8,128)(2,1)S(1)}, u32[]{:S(2)}, u32[]{:S(2)}) async-start(bf16[4,232,256]{2,1,0:T(8,128)(2,1)} %shard_map.103), calls=%async_computation.1 | async-start | bytes 950272 | tf_op jit(solution)/shard_map/all_to_all | solution.py:454
  105.1 11.6 %collective-permute-start.14 = (bf16[2,512,128]{2,1,0:T(8,128)(2,1)S(1)}, bf16[2,512,128]{2,1,0:T(8,128)(2,1)S(1)}, u32[]{:S(2)}, u32[]{:S(2)}) collective-permute-start(bf16[2,512,128]{2,1,0:T(8,128)(2,1)S(1)} %get-tuple-element.129), channel_id=1, source_target_pairs={{0,1},{1,0},{2,3},{3,2},{4,5},{5,4},{6,7},{7,6},{8,9},{9,8},{10,11... | collective-permute-start | bytes 786440 | tf_op jit(solution)/shard_map/ppermute | solution.py:471
  116.7 11.0 %collective-permute-start.15 = (bf16[512,128]{1,0:T(8,128)(2,1)S(1)}, bf16[512,128]{1,0:T(8,128)(2,1)S(1)}, u32[]{:S(2)}, u32[]{:S(2)}) collective-permute-start(bf16[512,128]{1,0:T(8,128)(2,1)S(1)} %get-tuple-element.131), channel_id=1, source_target_pairs={{0,2},{2,0},{1,3},{3,1},{4,6},{6,4},{5,7},{7,5},{8,10},{10,8},{9,1... | collective-permute-start | bytes 393224 | tf_op jit(solution)/shard_map/ppermute | solution.py:473
